TPU v7x, 256 devices: a whole 4x4x8 slice. The times are simulated.
256 devices in a mesh: row: 8 (over x, core), col: 32 (over z, y).
Axes of the slice: x: 4, y: 4, z: 8, core: 2. Of those that a mesh axis runs over, the one named last changes fastest.
Arguments:
- embeddings: bfloat16 [256, 131072], P(None, ('row', 'col')), may hold values from -10.1875 to 10.1875
- vectors: float32 [32, 131072], P(None, ('row', 'col')), may hold values from -17 to 17
- block_pairs: int32 [6144, 2], P(('row', 'col')), may hold values from 0 to 255, as said below
- counts: int32 [256], P(('row', 'col')), may hold values from 1 to 24, as said below
Outputs:
- embedding_basis: float32 [32, 131072], P(None, ('row', 'col'))
- gram_factor: float32 [32, 32], replicated
Inputs may be any that keep to these rules, and one draw needn't show every extreme that they name: `block_pairs`: device d = r * 32 + c of row+col lists in its first counts[d] rows only pairs (I, J) with I <= J, I // 32 == r and J % 32 == c; its first row is (d, d); each pair appears at most once among the listed rows of all devices. Its other rows hold block numbers and are ignored. `counts`: the most, 24, is reached in every draw.
All inputs are finite; a program needn't handle non-finite values.
Results may differ from a plain program's by a relative error of at most 0.004.
Values may be sent and summed in bfloat16 or wider, within the bound.
No kernel may reach another device: no remote copies, remote signals or barrier semaphores. Data moves between devices by JAX's collectives and lax.ppermute only.
A program may use at most 256 MiB of HBM per device.

v0:
```python
import math

import jax
import jax.numpy as jnp
from jax import lax
from jax.sharding import PartitionSpec as P


def on_device(embeddings, vectors, block_pairs, counts):
    block_len = embeddings.shape[1]
    row_devices = lax.axis_size("row")
    col_devices = lax.axis_size("col")
    vec_width = vectors.shape[0]
    score_scale = 1.0 / math.sqrt(embeddings.shape[0])
    vector_bf16 = vectors.astype(jnp.bfloat16)
    col_embed, col_vec = (
        lax.all_gather(embeddings, "row", axis=1, tiled=True),
        lax.all_gather(vector_bf16, "row", axis=1, tiled=True),
    )
    listed = counts[0]
    initial = (
        jnp.zeros((vec_width, col_devices * block_len), jnp.float32),
        jnp.zeros((1, col_devices * block_len), jnp.float32),
        jnp.zeros((vec_width, row_devices * block_len), jnp.float32),
        jnp.zeros((1, row_devices * block_len), jnp.float32),
    )
    row_embed, row_vec = (
        lax.all_gather(embeddings, "col", axis=1, tiled=True),
        lax.all_gather(vector_bf16, "col", axis=1, tiled=True),
    )
    begin_at = jnp.int32(0)
    piece_len = row_embed.shape[1]
    part_len = min(piece_len, block_len)

    def visit_slot(slot_number, running):
        row_block = block_pairs[slot_number, 0]
        col_block = block_pairs[slot_number, 1]
        first_row = row_block % col_devices * block_len
        far_start = col_block // col_devices * block_len
        inside = (first_row >= begin_at) & (first_row < begin_at + piece_len)
        is_live = inside & (slot_number < listed)

        def add_tile(current):
            row_image, row_degree, col_image, col_degree = current
            near_embed = lax.dynamic_slice_in_dim(row_embed, first_row, part_len, 1)
            near_vec = lax.dynamic_slice_in_dim(row_vec, first_row, part_len, 1)
            far_embed = lax.dynamic_slice_in_dim(col_embed, far_start, block_len, 1)
            far_vec = lax.dynamic_slice_in_dim(col_vec, far_start, block_len, 1)
            scores = lax.dot_general(
                near_embed, far_embed, (((0,), (0,)), ((), ())), preferred_element_type=jnp.float32
            )
            weights = jax.nn.sigmoid(scores * score_scale)
            tile_bf16 = weights.astype(jnp.bfloat16)
            mirror_mask = (row_block != col_block).astype(jnp.float32)
            near_terms = lax.dot_general(
                far_vec, tile_bf16, (((1,), (1,)), ((), ())), preferred_element_type=jnp.float32
            )
            far_terms = (
                jnp.dot(near_vec, tile_bf16, preferred_element_type=jnp.float32) * mirror_mask
            )
            row_mass = jnp.sum(weights, axis=1)[None, :]
            col_mass = jnp.sum(weights, axis=0)[None, :] * mirror_mask
            slab = lax.dynamic_slice_in_dim(row_image, first_row, part_len, 1)
            row_image = lax.dynamic_update_slice_in_dim(row_image, slab + near_terms, first_row, 1)
            slab = lax.dynamic_slice_in_dim(row_degree, first_row, part_len, 1)
            row_degree = lax.dynamic_update_slice_in_dim(row_degree, slab + row_mass, first_row, 1)
            slab = lax.dynamic_slice_in_dim(col_image, far_start, block_len, 1)
            col_image = lax.dynamic_update_slice_in_dim(col_image, slab + far_terms, far_start, 1)
            slab = lax.dynamic_slice_in_dim(col_degree, far_start, block_len, 1)
            col_degree = lax.dynamic_update_slice_in_dim(col_degree, slab + col_mass, far_start, 1)
            return (row_image, row_degree, col_image, col_degree)

        return lax.cond(is_live, add_tile, lambda current: current, running)

    totals = lax.fori_loop(0, block_pairs.shape[0], visit_slot, initial)
    row_image, row_degree, col_image, col_degree = totals
    col_sums, col_mass_sum = (
        lax.psum_scatter(col_image, "row", scatter_dimension=1, tiled=True),
        lax.psum_scatter(col_degree, "row", scatter_dimension=1, tiled=True),
    )
    row_sums, row_mass_sum = (
        lax.psum_scatter(row_image, "col", scatter_dimension=1, tiled=True),
        lax.psum_scatter(row_degree, "col", scatter_dimension=1, tiled=True),
    )
    image_sum = row_sums + col_sums
    degree = row_mass_sum + col_mass_sum
    walked = image_sum / degree
    points = block_len * row_devices * col_devices
    local_gram = jnp.dot(
        walked, walked.T, precision=lax.Precision.HIGHEST, preferred_element_type=jnp.float32
    )
    gram_matrix = lax.psum(local_gram, ("row", "col")) / points
    gram_factor = jnp.linalg.cholesky(gram_matrix)
    inverse = lax.linalg.triangular_solve(
        gram_factor, jnp.eye(vec_width, dtype=jnp.float32), left_side=True, lower=True
    )
    embedding_basis = jnp.dot(
        inverse, walked, precision=lax.Precision.HIGHEST, preferred_element_type=jnp.float32
    )
    return (embedding_basis, gram_factor)


def solution(mesh):
    in_specs = (
        P(None, ("row", "col")),
        P(None, ("row", "col")),
        P(("row", "col"), None),
        P(("row", "col")),
    )
    out_specs = (P(None, ("row", "col")), P())
    return jax.shard_map(
        on_device, mesh=mesh, in_specs=in_specs, out_specs=out_specs, check_vma=False
    )
```

profile of v0, /device:TPU:1, one launch (start us, length us, event | category | flops | bytes accessed | tf_op | source)
XLA Modules:
  0.0 1088.2 jit_solution(3778482447780300538)
XLA Ops:
  7.2 1.5 convert_element_type.26
  10.2 16.1 %all_gather.12 = bf16[32,4096]{1,0:T(8,128)(2,1)S(1)} all-gather(bf16[32,512]{1,0:T(8,128)(2,1)} %convert_element_type.26), channel_id=1, replica_groups=mesh['row'=8,'col'=32] {'row'}, dimensions={1}, use_global_device_ids=true | all-gather | bytes 294912 | tf_op jit(solution)/shard_map/all_gather | solution.py:18
  26.4 55.5 %all-gather.8.cloned.1.call-done = bf16[32,16384]{1,0:T(8,128)(2,1)} async-done(((bf16[32,512]{1,0:T(8,128)(2,1)}), bf16[32,16384]{1,0:T(8,128)(2,1)}) %all-gather.8.cloned.1.call-update) | async-done | bytes 1048592 | tf_op jit(solution)/shard_map/all_gather | solution.py:29
  81.9 32.9 %all-gather.6.cloned.1.call-done = bf16[256,4096]{1,0:T(8,128)(2,1)} async-done(((bf16[256,512]{1,0:T(8,128)(2,1)}), bf16[256,4096]{1,0:T(8,128)(2,1)}) %all-gather.6.cloned.1.call-update) | async-done | bytes 2097168 | tf_op jit(solution)/shard_map/all_gather | solution.py:17
  114.8 103.6 %all-gather.4.cloned.1.call-done = bf16[256,16384]{1,0:T(8,128)(2,1)} async-done(((bf16[256,512]{1,0:T(8,128)(2,1)}), bf16[256,16384]{1,0:T(8,128)(2,1)}) %all-gather.4.cloned.1.call-update) | async-done | bytes 8388624 | tf_op jit(solution)/shard_map/all_gather | solution.py:28
  218.7 234.2 %while.21 = (s32[]{:T(128)}, f32[32,16384]{1,0:T(8,128)S(1)}, f32[1,16384]{1,0:T(1,128)S(1)}, f32[32,4096]{1,0:T(8,128)S(1)}, f32[1,4096]{1,0:T(1,128)S(1)}, /*i...) while((s32[]{:T(128)}, f32[32,16384]{1,0:T(8,128)S(1)}, ...), condition=%wide.region_5.6_spmd, body=%wide.region_0.5_spmd.sunk | while | flops 169656864 | bytes 2581292 | solution.py:75
  221.7 7.7 conditional.2
  225.5 1.7 fusion.22
  227.2 1.0 fusion.5
  232.4 7.7 conditional.2
  236.3 1.7 fusion.22
  243.2 7.7 conditional.2
  247.0 1.7 fusion.22
  253.9 7.7 conditional.2
  257.7 1.7 fusion.22
  259.4 1.0 fusion.5
  264.6 7.7 conditional.2
  268.5 1.7 fusion.22
  275.4 7.7 conditional.2
  279.2 1.7 fusion.22
  286.1 7.7 conditional.2
  289.9 1.7 fusion.22
  296.8 7.7 conditional.2
  300.7 1.7 fusion.22
  307.6 7.7 conditional.2
  311.4 1.7 fusion.22
  318.3 7.7 conditional.2
  322.2 1.7 fusion.22
  329.1 7.7 conditional.2
  332.9 1.7 fusion.22
  339.8 7.7 conditional.2
  343.6 1.7 fusion.22
  350.5 7.7 conditional.2
  354.4 1.7 fusion.22
  361.3 7.7 conditional.2
  365.1 1.7 fusion.22
  372.0 7.7 conditional.2
  375.8 1.7 fusion.22
  382.7 7.7 conditional.2
  386.6 1.7 fusion.22
  393.5 7.7 conditional.2
  397.3 1.7 fusion.22
  404.2 7.7 conditional.2
  408.0 1.7 fusion.22
  414.9 7.7 conditional.2
  418.8 1.7 fusion.22
  425.7 7.7 conditional.2
  429.5 1.7 fusion.22
  436.4 7.5 conditional.2
  440.3 1.7 fusion.22
  452.9 2.1 copy.13
  455.1 4.9 copy.11
  461.4 46.9 %reduce-scatter.15.cloned.1.call-done = f32[512,1]{1,0:T(8,128)} async-done(((f32[4096,1]{1,0:T(8,128)}), f32[512,1]{1,0:T(8,128)}) %reduce-scatter.15.cloned.1.call-update) | async-done | bytes 2064
  508.2 1.1 copy.14
  509.3 229.5 %reduce-scatter.13.cloned.1.call-done = f32[512,1]{1,0:T(8,128)} async-done(((f32[16384,1]{1,0:T(8,128)}), f32[512,1]{1,0:T(8,128)}) %reduce-scatter.13.cloned.1.call-update) | async-done | bytes 2064
  738.8 1.1 copy.12
  739.9 35.1 %reduce-scatter.11.cloned.1.call-done = f32[32,512]{1,0:T(8,128)} async-done(((f32[32,4096]{1,0:T(8,128)}), f32[32,512]{1,0:T(8,128)}) %reduce-scatter.11.cloned.1.call-update) | async-done | bytes 65552 | tf_op jit(solution)/shard_map/reduce_scatter | solution.py:78
  775.0 216.2 %reduce-scatter.9.cloned.1.call-done = f32[32,512]{1,0:T(8,128)} async-done(((f32[32,16384]{1,0:T(8,128)}), f32[32,512]{1,0:T(8,128)}) %reduce-scatter.9.cloned.1.call-update) | async-done | bytes 65552 | tf_op jit(solution)/shard_map/reduce_scatter | solution.py:82
  991.2 1.1 fusion.21
  992.4 79.7 %psum.7 = f32[32,32]{0,1:T(8,128)S(1)} all-reduce(f32[32,32]{0,1:T(8,128)S(1)} %fusion.21), channel_id=1, replica_groups=mesh['row'=8,'col'=32] {'row','col'}, use_global_device_ids=true, to_apply=%region_10.11 | all-reduce | flops 1024 | bytes 8192 | tf_op jit(solution)/shard_map/psum | solution.py:92
  1072.1 2.9 cholesky.17
  1075.7 1.3 select_bitcast_fusion
  1077.0 2.4 custom-call.6
  1079.6 1.7 fusion.20
  (182 shorter events, 61.3 us)
Async XLA Ops:
  7.2 211.5 %copy-start.2 = (s32[24,2]{0,1:T(2,128)S(1)}, s32[24,2]{0,1:T(2,128)}, u32[]{:S(2)}) copy-start(s32[24,2]{0,1:T(2,128)} %param.10) | copy-start | bytes 580
  7.2 74.7 %all-gather.8.cloned.1.call-start = ((), (), s32[]{:S(2)}) async-start(), calls=%async_computation.6 | async-start | bytes 1081344 | tf_op jit(solution)/shard_map/all_gather | solution.py:29
  8.7 106.1 %all-gather.6.cloned.1.call-start = ((), (), s32[]{:S(2)}) async-start(), calls=%async_computation.5 | async-start | bytes 2359296 | tf_op jit(solution)/shard_map/all_gather | solution.py:17
  9.5 209.0 %all-gather.4.cloned.1.call-start = ((), (), s32[]{:S(2)}) async-start(), calls=%async_computation.4 | async-start | bytes 8650752 | tf_op jit(solution)/shard_map/all_gather | solution.py:28
  10.2 498.1 %reduce-scatter.15.cloned.1.call-start = ((), (), s32[]{:S(2)}) async-start(), calls=%async_computation.10 | async-start | bytes 2359296
  452.9 2.1 copy-start
  452.9 2.1 copy-start.1
  455.1 283.8 %reduce-scatter.13.cloned.1.call-start = ((), (), s32[]{:S(2)}) async-start(), calls=%async_computation.9 | async-start | bytes 8650752
  460.0 314.9 %reduce-scatter.11.cloned.1.call-start = ((), (), s32[]{:S(2)}) async-start(), calls=%async_computation.8 | async-start | bytes 589824 | tf_op jit(solution)/shard_map/reduce_scatter | solution.py:78
  460.6 530.6 %reduce-scatter.9.cloned.1.call-start = ((), (), s32[]{:S(2)}) async-start(), calls=%async_computation.7 | async-start | bytes 2162688 | tf_op jit(solution)/shard_map/reduce_scatter | solution.py:82
Sparse Core Ops, SparseCore 0:
  11.0 70.7 all-gather.7
  83.7 31.0 all-gather.5
  117.3 101.1 all-gather.3
  455.2 53.0 reduce-scatter.14
  512.1 226.6 reduce-scatter.12
  741.4 33.5 reduce-scatter.10
  778.8 212.3 reduce-scatter.8
where the time goes:
time: 1090 us
  waiting for transfers between devices  722 us (66%)
  loops' own time  139 us (13%)
  blocking collectives  95.8 us (9%)
  matrix products  65.6 us (6%)
  local copies, waits for them, and re-layouts  39.9 us (4%)
  between operations  14.2 us (1%)
    unnamed x9, waiting for transfers between devices  279 us
    reduce_scatter x1, waiting for transfers between devices, on_device(): lax.psum_scatter(row_image, 'col', scatter_dimension=1, tiled=True)  216 us
    all_gather x1, waiting for transfers between devices, on_device(): lax.all_gather(embeddings, 'col', axis=1, tiled=True)  104 us
    another operation x24, loops' own time, visit_slot(): return lax.cond(is_live, add_tile, lambda current: current, running)  81.5 us
    psum x1, blocking collectives, on_device(): gram_matrix = lax.psum(local_gram, ('row', 'col')) / points  79.7 us
    another operation x1, loops' own time, on_device(): totals = lax.fori_loop(0, block_pairs.shape[0], visit_slot, initial)  57.7 us
    all_gather x1, waiting for transfers between devices, on_device(): lax.all_gather(vector_bf16, 'col', axis=1, tiled=True)  55.5 us
    dot_general x21, matrix products, add_tile(): lax.dot_general(near_embed, far_embed, (((0,), (0,)), ((), ())), preferre...  35.8 us
  transfers between devices with their start and end apart: 7, of which 7 were waited for; matrix products, arithmetic and copies ran while one was open for 1% of the time, Pallas kernels for 0%

commit v1 on v0

v1 whole, which is shorter than its diff:
```python
import functools
import math

import jax
import jax.numpy as jnp
from jax import lax
from jax.experimental import pallas as pl
from jax.experimental.pallas import tpu as pltpu
from jax.sharding import Mesh
from jax.sharding import PartitionSpec as P

X, K, Z, Y = 4, 2, 8, 4
COLS = Z * Y
NEAR = ("k", "z")
FAR = ("x", "y")
EVERY = ("x", "k", "z", "y")
WAYS = 16
BS = 512
EMB = 256
VEC = 32
AUG = 48
MAXP = 24
LISTS = K * Y
SLOTS = 256


def select_kernel(place_ref, lists_ref, picked_ref):
    own_y = place_ref[0]
    own_k = place_ref[1]

    def each_list(which, found):
        def each_slot(slot, found):
            row_block = lists_ref[which, 2 * slot]
            col_block = lists_ref[which, 2 * slot + 1]
            near = ((row_block >> 5) & 1) * Z + ((row_block >> 2) & 7)
            far = ((col_block >> 6) & 3) * Y + (col_block & 3)
            same = (row_block == col_block).astype(jnp.int32)
            mine = ((row_block & 3) == own_y) & (((col_block >> 5) & 1) == own_k)
            picked_ref[found + 1] = same * 256 + near * 16 + far
            return found + mine.astype(jnp.int32)

        return lax.fori_loop(0, lists_ref[which, 2 * MAXP], each_slot, found)

    picked_ref[0] = lax.fori_loop(0, LISTS, each_list, jnp.int32(0))


def tile_kernel(picked_ref, near_ref, far_ref, near_out, far_out, near_sum, far_sum):
    near_sum[...] = jnp.zeros_like(near_sum)
    far_sum[...] = jnp.zeros_like(far_sum)
    ones = (lax.broadcasted_iota(jnp.int32, (AUG - VEC, BS), 0) == 0).astype(jnp.bfloat16)

    def each_tile(number, carry):
        code = picked_ref[number + 1]
        same = code >> 8
        near = (code >> 4) & 15
        far = code & 15
        mirror = jnp.where(same == 1, 0.0, 1.0).astype(jnp.float32)
        far_embed = far_ref[far, :EMB, :]
        near_vec = jnp.concatenate([near_ref[near, EMB:, :], ones], axis=0)
        far_vec = jnp.concatenate([far_ref[far, EMB:, :], ones], axis=0)
        far_terms = None
        for half in range(2):
            cut = slice(half * 256, half * 256 + 256)
            scores = jnp.dot(
                near_ref[near, :EMB, cut], far_embed, preferred_element_type=jnp.float32
            )
            tile = (0.5 * jnp.tanh(scores) + 0.5).astype(jnp.bfloat16)
            near_terms = lax.dot_general(
                far_vec, tile, (((1,), (1,)), ((), ())), preferred_element_type=jnp.float32
            )
            near_sum[near, :, cut] += near_terms
            part = jnp.dot(near_vec[:, cut], tile, preferred_element_type=jnp.float32)
            far_terms = part if far_terms is None else far_terms + part
        far_sum[far] += far_terms * mirror
        return carry

    lax.fori_loop(0, picked_ref[0], each_tile, 0)
    near_out[...] = near_sum[...].astype(jnp.bfloat16)
    far_out[...] = far_sum[...].astype(jnp.bfloat16)


def on_device(embeddings, vectors, block_pairs, counts):
    score_scale = 0.5 / math.sqrt(EMB)
    vector_bf16 = vectors.astype(jnp.bfloat16)
    turned = embeddings.T
    near_send = jnp.concatenate(
        [
            jnp.concatenate([turned[:256], turned[256:]], axis=1)
            * jnp.asarray(score_scale, jnp.bfloat16),
            vector_bf16,
        ],
        axis=0,
    )
    far_send = jnp.concatenate([embeddings, vector_bf16], axis=0)
    near_all = lax.all_gather(near_send, NEAR)
    far_all = lax.all_to_all(
        jnp.broadcast_to(far_send[None], (WAYS,) + far_send.shape), FAR, 0, 0
    )
    own_list = jnp.concatenate(
        [block_pairs.reshape(-1), counts, jnp.zeros((128 - 2 * MAXP - 1,), jnp.int32)]
    )
    lists = lax.all_gather(own_list, ("k", "y"))
    place = jnp.stack([lax.axis_index("y"), lax.axis_index("k")]).astype(jnp.int32)
    smem = pl.BlockSpec(memory_space=pltpu.SMEM)
    vmem = pl.BlockSpec(memory_space=pltpu.VMEM)
    picked = pl.pallas_call(
        select_kernel,
        out_shape=jax.ShapeDtypeStruct((SLOTS,), jnp.int32),
        in_specs=[smem, smem],
        out_specs=smem,
        name="select_pairs",
    )(place, lists)
    near_part, far_part = pl.pallas_call(
        tile_kernel,
        out_shape=[jax.ShapeDtypeStruct((WAYS, AUG, BS), jnp.bfloat16)] * 2,
        in_specs=[smem, vmem, vmem],
        out_specs=[vmem, vmem],
        scratch_shapes=[pltpu.VMEM((WAYS, AUG, BS), jnp.float32)] * 2,
        compiler_params=pltpu.CompilerParams(vmem_limit_bytes=48 * 1024 * 1024),
        name="tiles",
    )(picked, near_all, far_all)
    near_back = lax.all_to_all(near_part, NEAR, 0, 0)
    far_back = lax.all_to_all(far_part, FAR, 0, 0)
    total = jnp.sum(near_back.astype(jnp.float32), axis=0) + jnp.sum(
        far_back.astype(jnp.float32), axis=0
    )
    walked = total[:VEC] / total[VEC : VEC + 1]
    points = BS * X * K * Z * Y
    local_gram = jnp.dot(
        walked, walked.T, precision=lax.Precision.HIGHEST, preferred_element_type=jnp.float32
    )
    partial_gram = local_gram.reshape(1, 8, 128)
    for group in (FAR, NEAR):
        shares = lax.all_to_all(jnp.broadcast_to(partial_gram, (WAYS, 8, 128)), group, 0, 0)
        partial_gram = jnp.sum(shares, axis=0, keepdims=True)
    gram_matrix = partial_gram.reshape(VEC, VEC) / points
    gram_factor = jnp.linalg.cholesky(gram_matrix)
    inverse = lax.linalg.triangular_solve(
        gram_factor, jnp.eye(VEC, dtype=jnp.float32), left_side=True, lower=True
    )
    embedding_basis = jnp.dot(
        inverse, walked, precision=lax.Precision.HIGHEST, preferred_element_type=jnp.float32
    )
    return (embedding_basis, gram_factor)


def solution(mesh):
    fine = Mesh(mesh.devices.reshape(X, K, Z, Y), EVERY)
    in_specs = (P(None, EVERY), P(None, EVERY), P(EVERY, None), P(EVERY))
    out_specs = (P(None, EVERY), P())
    return jax.shard_map(
        on_device, mesh=fine, in_specs=in_specs, out_specs=out_specs, check_vma=False
    )
```

time: 1090 us -> 204 us (0.19)
  waiting for transfers between devices: 722 us -> 40.4 us
  loops' own time: 139 us -> 0 us
  matrix products: 65.6 us -> 1.26 us
  local copies, waits for them, and re-layouts: 39.9 us -> 4.9 us
  Pallas kernels: 0 us -> 20.6 us
  starting transfers between devices: 0.28 us -> 19.3 us
    unnamed x9 -> x1, waiting for transfers between devices: 279 us -> 0.02 us
    reduce_scatter x2 -> x0, waiting for transfers between devices: 251 us -> none  [the longest x1 216 us: on_device(): lax.psum_scatter(row_image, 'col', scatter_dimension=1, tiled=True)]
    all_gather x3 -> x1, waiting for transfers between devices: 192 us -> 0.01 us  [on_device(): near_all = lax.all_gather(near_send, NEAR)]
    another operation x25 -> x0, loops' own time: 139 us -> none  [the longest x24 81.5 us: visit_slot(): return lax.cond(is_live, add_tile, lambda current: current, running)]
    psum x1 -> x0, blocking collectives: 79.7 us -> none  [on_device(): gram_matrix = lax.psum(local_gram, ('row', 'col')) / points]
    dot_general x63 -> x0, matrix products: 62.5 us -> none  [the longest x21 35.8 us: add_tile(): lax.dot_general(near_embed, far_embed, (((0,), (0,)), ((), ())), preferre...]
    all_to_all x0 -> x3, blocking collectives: none -> 45.2 us  [the longest x2 22.7 us: on_device(): lax.all_to_all(jnp.broadcast_to(partial_gram, (WAYS, 8, 128)), group, 0, 0)]
    all_to_all x0 -> x2, waiting for transfers between devices: none -> 40.4 us  [the longest x1 21.1 us: on_device(): near_back = lax.all_to_all(near_part, NEAR, 0, 0)]
  transfers between devices with their start and end apart: 7 -> 3, of which waited for: 7 -> 2; matrix products, arithmetic and copies ran while one was open for 1% -> 2% of each run, Pallas kernels for 0% -> 2%
where the time goes in v1:
time: 204 us; the launch traced here: 205 us
  blocking collectives  92.6 us (45%)
  waiting for transfers between devices  40.4 us (20%)
  Pallas kernels  20.6 us (10%)
  starting transfers between devices  19.3 us (9%)
  between operations  14.8 us (7%)
  other arithmetic  10.9 us (5%)
  local copies, waits for them, and re-layouts  4.9 us (2%)
    all_gather x1, blocking collectives, on_device(): lists = lax.all_gather(own_list, ('k', 'y'))  47.4 us
    all_to_all x2, blocking collectives, on_device(): lax.all_to_all(jnp.broadcast_to(partial_gram, (WAYS, 8, 128)), group, 0, 0)  22.7 us
    all_to_all x1, blocking collectives, on_device(): far_back = lax.all_to_all(far_part, FAR, 0, 0)  22.5 us
    all_to_all x1, waiting for transfers between devices, on_device(): near_back = lax.all_to_all(near_part, NEAR, 0, 0)  21.1 us
    all_to_all x1, waiting for transfers between devices, on_device(): lax.all_to_all(jnp.broadcast_to(far_send[None], (WAYS,) + far_send.shape)...  19.3 us
    pallas_call x1, Pallas kernels, on_device(): pl.pallas_call(tile_kernel, out_shape=[jax.ShapeDtypeStruct((WAYS, AUG, B...  17 us
    all_to_all x1, starting transfers between devices, on_device(): near_back = lax.all_to_all(near_part, NEAR, 0, 0)  11.5 us
    all_to_all x1, starting transfers between devices, on_device(): lax.all_to_all(jnp.broadcast_to(far_send[None], (WAYS,) + far_send.shape)...  7.76 us
  transfers between devices with their start and end apart: 3, of which 2 were waited for; matrix products, arithmetic and copies ran while one was open for 2% of the time, Pallas kernels for 2%

profile of v1, /device:TPU:1, one launch (start us, length us, event | category | flops | bytes accessed | tf_op | source)
XLA Modules:
  0.0 204.7 jit_solution(16095244518675526587)
XLA Ops:
  7.2 0.0 all-gather.5.cloned.1.call-start
  7.2 1.1 copy.20
  8.3 0.8 convert_element_type.10
  9.2 1.7 pad_maximum_fusion
  10.9 0.0 all-gather.5.cloned.1.call-update
  11.0 2.7 %broadcast_in_dim.12 = bf16[16,288,512]{2,1,0:T(8,128)(2,1)} broadcast(bf16[288,512]{1,0:T(8,128)(2,1)S(1)} %get-tuple-element.10), dimensions={1,2} | broadcast | bytes 5013504 | tf_op jit(solution)/shard_map/broadcast_in_dim | solution.py:97
  13.6 0.0 copy-start.1
  13.6 7.8 %all-to-all-start = ((bf16[16,288,512]{2,1,0:T(8,128)(2,1)}), bf16[16,288,512]{2,1,0:T(8,128)(2,1)}, u32[]{:S(2)}, u32[]{:S(2)}) async-start(bf16[16,288,512]{2,1,0:T(8,128)(2,1)} %broadcast_in_dim.12), calls=%async_computation | async-start | bytes 9437184 | tf_op jit(solution)/shard_map/all_to_all | solution.py:96
  21.4 0.0 copy-done.1
  21.4 0.1 copy.19
  21.5 0.1 reshape.22
  22.3 0.1 add_bitcast_fusion
  22.4 47.4 %all-gather.2 = s32[8,1,128]{2,1,0:T(1,128)} all-gather(s32[1,1,128]{2,1,0:T(1,128)S(1)} %add_bitcast_fusion), channel_id=2, replica_groups=mesh['x'=4,'k'=2,'z'=8,'y'=4] {'k','y'}, dimensions={0}, use_global_device_ids=true | all-gather | bytes 4608 | tf_op jit(solution)/shard_map/all_gather | solution.py:102
  69.8 0.7 pad_add_fusion.place_ref
  70.4 3.5 %select_pairs.1.picked_ref = s32[256]{0:T(256)} custom-call(s32[2]{0:T(128)} %pad_add_fusion.place_ref, s32[8,128]{1,0:T(8,128)} %bitcast.20), custom_call_target="tpu_custom_call" | custom-call | tf_op jit(solution)/shard_map/select_pairs/pallas_call | solution.py:106
  73.9 19.3 %all-to-all-done.far_ref = bf16[16,288,512]{2,1,0:T(8,128)(2,1)} async-done(((bf16[16,288,512]{2,1,0:T(8,128)(2,1)}), bf16[16,288,512]{2,1,0:T(8,128)(2,1)}, u32[]{:S(2)}, u32[]{:S(2)}) %all-to-all-start) | async-done | bytes 4718624 | tf_op jit(solution)/shard_map/all_to_all | solution.py:96
  93.2 0.0 all-gather.5.cloned.1.call-done
  93.2 0.0 copy-start
  93.2 0.7 copy-done
  93.9 17.0 %tiles.1 = (bf16[16,48,512]{2,1,0:T(8,128)(2,1)}, bf16[16,48,512]{2,1,0:T(8,128)(2,1)S(1)}) custom-call(s32[256]{0:T(256)S(1)} %copy-done, bf16[16,288,512]{2,1,0:T(8,128)(2,1)} %bitcast.18, bf16[16,288,512]{2,1,0:T(8,128)(2,1)} %all-to-all-done.far_ref), custom_call_target="tpu_custom_call" | custom-call | tf_op jit(solution)/shard_map/tiles/pallas_call | solution.py:113
  110.9 22.5 %all_to_all.25 = bf16[16,48,512]{2,1,0:T(8,128)(2,1)S(1)} all-to-all(bf16[16,48,512]{2,1,0:T(8,128)(2,1)S(1)} %get-tuple-element.5), channel_id=1, replica_groups=mesh['x'=4,'k'=2,'z'=8,'y'=4] {'x','y'}, dimensions={0} | all-to-all | bytes 1572864 | tf_op jit(solution)/shard_map/all_to_all | solution.py:123
  133.5 11.5 %all-to-all-start.1 = ((bf16[16,48,512]{2,1,0:T(8,128)(2,1)}), bf16[16,48,512]{2,1,0:T(8,128)(2,1)S(1)}, u32[]{:S(2)}, u32[]{:S(2)}) async-start(bf16[16,48,512]{2,1,0:T(8,128)(2,1)} %get-tuple-element.4), calls=%async_computation.1 | async-start | bytes 1572864 | tf_op jit(solution)/shard_map/all_to_all | solution.py:122
  144.9 0.1 convert_reduce_fusion
  145.0 21.1 %all-to-all-done.1 = bf16[16,48,512]{2,1,0:T(8,128)(2,1)S(1)} async-done(((bf16[16,48,512]{2,1,0:T(8,128)(2,1)}), bf16[16,48,512]{2,1,0:T(8,128)(2,1)S(1)}, u32[]{:S(2)}, u32[]{:S(2)}) %all-to-all-start.1) | async-done | bytes 786464 | tf_op jit(solution)/shard_map/all_to_all | solution.py:122
  166.2 0.1 convert_reduce_fusion.1
  166.3 0.2 fusion.1
  166.5 0.1 broadcast_in_dim.26
  166.6 9.9 %all_to_all.26 = f32[16,8,128]{2,1,0:T(8,128)S(1)} all-to-all(f32[16,8,128]{2,1,0:T(8,128)S(1)} %broadcast_in_dim.27), channel_id=1, replica_groups=mesh['x'=4,'k'=2,'z'=8,'y'=4] {'x','y'}, dimensions={0} | all-to-all | bytes 131072 | tf_op jit(solution)/shard_map/all_to_all | solution.py:134
  176.6 12.8 %all_to_all.27 = f32[16,8,128]{2,1,0:T(8,128)S(1)} all-to-all(f32[16,8,128]{2,1,0:T(8,128)S(1)} %broadcast_in_dim.28), channel_id=1, replica_groups=mesh['x'=4,'k'=2,'z'=8,'y'=4] {'k','z'}, dimensions={0} | all-to-all | bytes 131072 | tf_op jit(solution)/shard_map/all_to_all | solution.py:134
  189.3 0.1 div.31
  189.4 0.1 copy.21
  189.5 2.9 %cholesky.17 = f32[32,32]{1,0:T(8,128)S(1)} custom-call(f32[32,32]{1,0:T(8,128)S(1)} %fusion.4), custom_call_target="Cholesky" | custom-call | tf_op jit(solution)/shard_map/jit(cholesky)/cholesky | solution.py:137
  192.5 0.6 compare_reduce_fusion
  193.1 1.3 select_bitcast_fusion
  194.4 2.4 %custom-call.6 = f32[1,32,32]{1,2,0:T(8,128)S(1)} custom-call(f32[1,32,32]{2,1,0:T(8,128)S(1)} %get-tuple-element.6), custom_call_target="InvertDiagBlocksLowerTriangular" | custom-call | tf_op jit(solution)/shard_map/triangular_solve | solution.py:138
  196.8 0.2 fusion.2
  197.0 0.8 fusion
  (12 shorter events, 0.2 us)
Async XLA Ops:
  7.2 86.0 %all-gather.5.cloned.1.call-start = ((), (), s32[]{:S(2)}) async-start(), calls=%async_computation.5 | async-start | bytes 5013504 | tf_op jit(solution)/shard_map/all_gather | solution.py:95
  13.6 7.8 %copy-start.1 = (s32[24,2]{0,1:T(2,128)S(1)}, s32[24,2]{0,1:T(2,128)}, u32[]{:S(2)}) copy-start(s32[24,2]{0,1:T(2,128)} %param.6) | copy-start | bytes 580
  13.6 79.6 %all-to-all-start = ((bf16[16,288,512]{2,1,0:T(8,128)(2,1)}), bf16[16,288,512]{2,1,0:T(8,128)(2,1)}, u32[]{:S(2)}, u32[]{:S(2)}) async-start(bf16[16,288,512]{2,1,0:T(8,128)(2,1)} %broadcast_in_dim.12), calls=%async_computation | async-start | bytes 9437184 | tf_op jit(solution)/shard_map/all_to_all | solution.py:96
  93.2 0.7 copy-start
  133.5 32.7 %all-to-all-start.1 = ((bf16[16,48,512]{2,1,0:T(8,128)(2,1)}), bf16[16,48,512]{2,1,0:T(8,128)(2,1)S(1)}, u32[]{:S(2)}, u32[]{:S(2)}) async-start(bf16[16,48,512]{2,1,0:T(8,128)(2,1)} %get-tuple-element.4), calls=%async_computation.1 | async-start | bytes 1572864 | tf_op jit(solution)/shard_map/all_to_all | solution.py:122
Sparse Core Ops, SparseCore 0:
  11.1 46.9 all-gather.4

commit v2 on v1

--- a/solution.py
+++ b/solution.py
@@ -44,7 +44,9 @@
     picked_ref[0] = lax.fori_loop(0, LISTS, each_list, jnp.int32(0))
 
 
-def tile_kernel(picked_ref, near_ref, far_ref, near_out, far_out, near_sum, far_sum):
+def tile_kernel(
+    place_ref, picked_ref, near_ref, far_ref, keep_out, give_out, far_out, near_sum, far_sum
+):
     near_sum[...] = jnp.zeros_like(near_sum)
     far_sum[...] = jnp.zeros_like(far_sum)
     ones = (lax.broadcasted_iota(jnp.int32, (AUG - VEC, BS), 0) == 0).astype(jnp.bfloat16)
@@ -75,7 +77,9 @@
         return carry
 
     lax.fori_loop(0, picked_ref[0], each_tile, 0)
-    near_out[...] = near_sum[...].astype(jnp.bfloat16)
+    own_k = place_ref[1]
+    keep_out[...] = near_sum[pl.ds(own_k * Z, Z)]
+    give_out[...] = near_sum[pl.ds((1 - own_k) * Z, Z)].astype(jnp.bfloat16)
     far_out[...] = far_sum[...].astype(jnp.bfloat16)
 
 
@@ -92,14 +96,17 @@
         axis=0,
     )
     far_send = jnp.concatenate([embeddings, vector_bf16], axis=0)
+    own_list = jnp.concatenate(
+        [block_pairs.reshape(-1), counts, jnp.zeros((128 - 2 * MAXP - 1,), jnp.int32)]
+    )
+    other_list = lax.ppermute(own_list, "k", [(0, 1), (1, 0)])
+    chip_lists = jnp.stack([own_list, other_list])
+    lists = lax.all_to_all(jnp.broadcast_to(chip_lists[None], (Y, K, 128)), "y", 0, 0)
+    lists, far_send = lax.optimization_barrier((lists.reshape(LISTS, 128), far_send))
     near_all = lax.all_gather(near_send, NEAR)
     far_all = lax.all_to_all(
         jnp.broadcast_to(far_send[None], (WAYS,) + far_send.shape), FAR, 0, 0
     )
-    own_list = jnp.concatenate(
-        [block_pairs.reshape(-1), counts, jnp.zeros((128 - 2 * MAXP - 1,), jnp.int32)]
-    )
-    lists = lax.all_gather(own_list, ("k", "y"))
     place = jnp.stack([lax.axis_index("y"), lax.axis_index("k")]).astype(jnp.int32)
     smem = pl.BlockSpec(memory_space=pltpu.SMEM)
     vmem = pl.BlockSpec(memory_space=pltpu.VMEM)
@@ -110,17 +117,23 @@
         out_specs=smem,
         name="select_pairs",
     )(place, lists)
-    near_part, far_part = pl.pallas_call(
+    near_keep, near_give, far_part = pl.pallas_call(
         tile_kernel,
-        out_shape=[jax.ShapeDtypeStruct((WAYS, AUG, BS), jnp.bfloat16)] * 2,
-        in_specs=[smem, vmem, vmem],
-        out_specs=[vmem, vmem],
+        out_shape=[
+            jax.ShapeDtypeStruct((Z, AUG, BS), jnp.float32),
+            jax.ShapeDtypeStruct((Z, AUG, BS), jnp.bfloat16),
+            jax.ShapeDtypeStruct((WAYS, AUG, BS), jnp.bfloat16),
+        ],
+        in_specs=[smem, smem, vmem, vmem],
+        out_specs=[vmem, vmem, vmem],
         scratch_shapes=[pltpu.VMEM((WAYS, AUG, BS), jnp.float32)] * 2,
         compiler_params=pltpu.CompilerParams(vmem_limit_bytes=48 * 1024 * 1024),
         name="tiles",
-    )(picked, near_all, far_all)
-    near_back = lax.all_to_all(near_part, NEAR, 0, 0)
+    )(place, picked, near_all, far_all)
     far_back = lax.all_to_all(far_part, FAR, 0, 0)
+    near_taken = lax.ppermute(near_give, "k", [(0, 1), (1, 0)])
+    near_pair = (near_keep + near_taken.astype(jnp.float32)).astype(jnp.bfloat16)
+    near_back = lax.all_to_all(near_pair, "z", 0, 0)
     total = jnp.sum(near_back.astype(jnp.float32), axis=0) + jnp.sum(
         far_back.astype(jnp.float32), axis=0
     )

time: 204 us -> 193 us (0.946)
  blocking collectives: 92.6 us -> 28.2 us
  waiting for transfers between devices: 40.4 us -> 81.5 us
  starting transfers between devices: 19.3 us -> 30.7 us
  Pallas kernels: 20.6 us -> 17.5 us
    all_gather x1 -> x0, blocking collectives: 47.4 us -> none  [on_device(): lists = lax.all_gather(own_list, ('k', 'y'))]
    all_to_all x1, waiting for transfers between devices: 19.3 us -> 56.5 us  [on_device(): lax.all_to_all(jnp.broadcast_to(far_send[None], (WAYS,) + far_send.shape)...]
    all_to_all x1, blocking collectives: 22.5 us -> 6.99 us  [on_device(): lax.all_to_all(jnp.broadcast_to(chip_lists[None], (Y, K, 128)), 'y', 0, 0)]
    all_to_all x1 -> x2, starting transfers between devices: 11.5 us -> 20.7 us  [the longest x1 13.9 us: on_device(): far_back = lax.all_to_all(far_part, FAR, 0, 0)]
    ppermute x0 -> x2, starting transfers between devices: none -> 5.32 us  [the longest x1 3.27 us: on_device(): other_list = lax.ppermute(own_list, 'k', [(0, 1), (1, 0)])]
    all_to_all x1, starting transfers between devices: 7.76 us -> 4.56 us  [on_device(): lax.all_to_all(jnp.broadcast_to(far_send[None], (WAYS,) + far_send.shape)...]
    pallas_call x1, Pallas kernels: 17 us -> 14.6 us  [on_device(): pl.pallas_call(tile_kernel, out_shape=[jax.ShapeDtypeStruct((Z, AUG, BS),...]
    ppermute x0 -> x2, waiting for transfers between devices: none -> 2.09 us  [the longest x1 1.35 us: on_device(): near_taken = lax.ppermute(near_give, 'k', [(0, 1), (1, 0)])]
  transfers between devices with their start and end apart: 3 -> 6, of which waited for: 2 -> 5; matrix products, arithmetic and copies ran while one was open for 2% -> 3% of each run, Pallas kernels for 2% -> 2%
where the time goes in v2:
time: 193 us; the launch traced here: 192 us
  waiting for transfers between devices  81.5 us (42%)
  starting transfers between devices  30.7 us (16%)
  blocking collectives  28.2 us (15%)
  Pallas kernels  17.5 us (9%)
  between operations  14.8 us (8%)
  other arithmetic  11.8 us (6%)
  local copies, waits for them, and re-layouts  6.25 us (3%)
    all_to_all x1, waiting for transfers between devices, on_device(): lax.all_to_all(jnp.broadcast_to(far_send[None], (WAYS,) + far_send.shape)...  56.5 us
    all_to_all x2, blocking collectives, on_device(): lax.all_to_all(jnp.broadcast_to(partial_gram, (WAYS, 8, 128)), group, 0, 0)  21.2 us
    all_to_all x1, waiting for transfers between devices, on_device(): near_back = lax.all_to_all(near_pair, 'z', 0, 0)  15 us
    pallas_call x1, Pallas kernels, on_device(): pl.pallas_call(tile_kernel, out_shape=[jax.ShapeDtypeStruct((Z, AUG, BS),...  14.6 us
    all_to_all x1, starting transfers between devices, on_device(): far_back = lax.all_to_all(far_part, FAR, 0, 0)  13.9 us
    all_to_all x1, waiting for transfers between devices, on_device(): far_back = lax.all_to_all(far_part, FAR, 0, 0)  7.88 us
    all_to_all x1, blocking collectives, on_device(): lax.all_to_all(jnp.broadcast_to(chip_lists[None], (Y, K, 128)), 'y', 0, 0)  6.99 us
    all_to_all x1, starting transfers between devices, on_device(): near_back = lax.all_to_all(near_pair, 'z', 0, 0)  6.89 us
  transfers between devices with their start and end apart: 6, of which 5 were waited for; matrix products, arithmetic and copies ran while one was open for 3% of the time, Pallas kernels for 2%

profile of v2, /device:TPU:1, one launch (start us, length us, event | category | flops | bytes accessed | tf_op | source)
XLA Modules:
  0.0 192.0 jit_solution(7818544264858308902)
XLA Ops:
  7.2 0.0 all-gather.3.cloned.1.call-start
  7.2 1.1 copy.18
  8.3 0.8 convert_element_type.16
  9.2 1.7 pad_maximum_fusion
  10.9 0.0 all-gather.3.cloned.1.call-update
  10.9 0.8 copy.17
  11.7 0.1 reshape.26
  12.5 0.1 pad_add_fusion.2
  12.6 3.3 %collective-permute-start = (s32[128]{0:T(128)S(1)}, s32[128]{0:T(128)S(1)}, u32[]{:S(2)}, u32[]{:S(2)}) collective-permute-start(s32[128]{0:T(128)S(1)} %pad_add_fusion.2), channel_id=1, source_target_pairs={{0,32},{32,0},{1,33},{33,1},{2,34},{34,2},{3,35},{35,3},{4,36},{36... | collective-permute-start | bytes 1544 | tf_op jit(solution)/shard_map/ppermute | solution.py:102
  15.8 0.1 fusion.7
  15.9 0.7 collective-permute-done
  16.7 7.0 %all_to_all.30 = s32[4,2,128]{2,1,0:T(2,128)} all-to-all(s32[4,2,128]{2,1,0:T(2,128)S(1)} %broadcast_in_dim.14), channel_id=1, replica_groups=mesh['x'=4,'k'=2,'z'=8,'y'=4] {'y'}, dimensions={0} | all-to-all | bytes 8192 | tf_op jit(solution)/shard_map/all_to_all | solution.py:104
  23.6 2.7 %broadcast_in_dim.15 = bf16[16,288,512]{2,1,0:T(8,128)(2,1)} broadcast(bf16[288,512]{1,0:T(8,128)(2,1)S(1)} %get-tuple-element.8), dimensions={1,2} | broadcast | bytes 5013504 | tf_op jit(solution)/shard_map/broadcast_in_dim | solution.py:108
  26.3 4.6 %all-to-all-start.1 = ((bf16[16,288,512]{2,1,0:T(8,128)(2,1)}), bf16[16,288,512]{2,1,0:T(8,128)(2,1)}, u32[]{:S(2)}, u32[]{:S(2)}) async-start(bf16[16,288,512]{2,1,0:T(8,128)(2,1)} %broadcast_in_dim.15), calls=%async_computation.1 | async-start | bytes 9437184 | tf_op jit(solution)/shard_map/all_to_all | solution.py:107
  30.9 0.7 pad_add_fusion.1.place_ref
  31.6 3.0 %select_pairs.1.picked_ref = s32[256]{0:T(256)} custom-call(s32[2]{0:T(128)} %pad_add_fusion.1.place_ref, s32[8,128]{1,0:T(8,128)} %bitcast.21), custom_call_target="tpu_custom_call" | custom-call | tf_op jit(solution)/shard_map/select_pairs/pallas_call | solution.py:113
  34.5 56.5 %all-to-all-done.1.far_ref = bf16[16,288,512]{2,1,0:T(8,128)(2,1)} async-done(((bf16[16,288,512]{2,1,0:T(8,128)(2,1)}), bf16[16,288,512]{2,1,0:T(8,128)(2,1)}, u32[]{:S(2)}, u32[]{:S(2)}) %all-to-all-start.1) | async-done | bytes 4718624 | tf_op jit(solution)/shard_map/all_to_all | solution.py:107
  91.1 0.0 all-gather.3.cloned.1.call-done
  91.1 0.0 copy-start
  91.1 0.7 copy-done
  91.7 0.0 copy-start.1
  91.7 0.7 copy-done.1
  92.4 14.6 %tiles.1 = (f32[8,48,512]{2,1,0:T(8,128)S(1)}, bf16[8,48,512]{2,1,0:T(8,128)(2,1)S(1)}, bf16[16,48,512]{2,1,0:T(8,128)(2,1)}) custom-call(s32[2]{0:T(128)S(1)} %copy-done.1, s32[256]{0:T(256)S(1)} %copy-done, bf16[16,288,512]{2,1,0:T(8,128)(2,1)} %bitcast.19, bf16[16,288,512]{2,1,0:T(8,128)(2,1)} %all-to-all-done.1.far_ref), custom_call_target="tpu_custom_call" | custom-call | tf_op jit(solution)/shard_map/tiles/pallas_call | solution.py:120
  107.0 13.9 %all-to-all-start.3 = ((bf16[16,48,512]{2,1,0:T(8,128)(2,1)}), bf16[16,48,512]{2,1,0:T(8,128)(2,1)S(1)}, u32[]{:S(2)}, u32[]{:S(2)}) async-start(bf16[16,48,512]{2,1,0:T(8,128)(2,1)} %get-tuple-element.11), calls=%async_computation.3 | async-start | bytes 1572864 | tf_op jit(solution)/shard_map/all_to_all | solution.py:133
  120.9 2.0 %collective-permute-start.1 = (bf16[8,48,512]{2,1,0:T(8,128)(2,1)S(1)}, bf16[8,48,512]{2,1,0:T(8,128)(2,1)S(1)}, u32[]{:S(2)}, u32[]{:S(2)}) collective-permute-start(bf16[8,48,512]{2,1,0:T(8,128)(2,1)S(1)} %get-tuple-element.10), channel_id=1, source_target_pairs={{0,32},{32,0},{1,33},{33,1},{2,34},{34,2},{3,35},{35,3},{4,36},{36... | collective-permute-start | bytes 1179656 | tf_op jit(solution)/shard_map/ppermute | solution.py:134
  122.9 1.3 collective-permute-done.1
  124.3 0.9 add_convert_fusion
  125.1 7.9 %all-to-all-done.3 = bf16[16,48,512]{2,1,0:T(8,128)(2,1)S(1)} async-done(((bf16[16,48,512]{2,1,0:T(8,128)(2,1)}), bf16[16,48,512]{2,1,0:T(8,128)(2,1)S(1)}, u32[]{:S(2)}, u32[]{:S(2)}) %all-to-all-start.3) | async-done | bytes 786464 | tf_op jit(solution)/shard_map/all_to_all | solution.py:133
  133.0 6.9 %all-to-all-start.2 = ((bf16[8,48,512]{2,1,0:T(8,128)(2,1)}), bf16[8,48,512]{2,1,0:T(8,128)(2,1)S(1)}, u32[]{:S(2)}, u32[]{:S(2)}) async-start(bf16[8,48,512]{2,1,0:T(8,128)(2,1)} %add_convert_fusion), calls=%async_computation.2 | async-start | bytes 786432 | tf_op jit(solution)/shard_map/all_to_all | solution.py:136
  139.9 0.1 convert_reduce_fusion
  140.0 15.0 %all-to-all-done.2 = bf16[8,48,512]{2,1,0:T(8,128)(2,1)S(1)} async-done(((bf16[8,48,512]{2,1,0:T(8,128)(2,1)}), bf16[8,48,512]{2,1,0:T(8,128)(2,1)S(1)}, u32[]{:S(2)}, u32[]{:S(2)}) %all-to-all-start.2) | async-done | bytes 393248 | tf_op jit(solution)/shard_map/all_to_all | solution.py:136
  155.0 0.1 convert_reduce_fusion.1
  155.0 0.2 fusion.1
  155.3 0.1 broadcast_in_dim.16
  155.3 9.7 %all_to_all.31 = f32[16,8,128]{2,1,0:T(8,128)S(1)} all-to-all(f32[16,8,128]{2,1,0:T(8,128)S(1)} %broadcast_in_dim.34), channel_id=1, replica_groups=mesh['x'=4,'k'=2,'z'=8,'y'=4] {'x','y'}, dimensions={0} | all-to-all | bytes 131072 | tf_op jit(solution)/shard_map/all_to_all | solution.py:147
  165.0 11.6 %all_to_all.32 = f32[16,8,128]{2,1,0:T(8,128)S(1)} all-to-all(f32[16,8,128]{2,1,0:T(8,128)S(1)} %broadcast_in_dim.35), channel_id=1, replica_groups=mesh['x'=4,'k'=2,'z'=8,'y'=4] {'k','z'}, dimensions={0} | all-to-all | bytes 131072 | tf_op jit(solution)/shard_map/all_to_all | solution.py:147
  176.6 0.1 div.31
  176.7 0.1 copy.19
  176.8 2.9 %cholesky.17 = f32[32,32]{1,0:T(8,128)S(1)} custom-call(f32[32,32]{1,0:T(8,128)S(1)} %fusion.4), custom_call_target="Cholesky" | custom-call | tf_op jit(solution)/shard_map/jit(cholesky)/cholesky | solution.py:150
  179.7 0.6 compare_reduce_fusion
  180.4 1.3 select_bitcast_fusion
  181.6 2.4 %custom-call.6 = f32[1,32,32]{1,2,0:T(8,128)S(1)} custom-call(f32[1,32,32]{2,1,0:T(8,128)S(1)} %get-tuple-element.12), custom_call_target="InvertDiagBlocksLowerTriangular" | custom-call | tf_op jit(solution)/shard_map/triangular_solve | solution.py:151
  184.1 0.2 fusion.2
  184.3 0.8 fusion
  (14 shorter events, 0.2 us)
Async XLA Ops:
  7.2 83.9 %all-gather.3.cloned.1.call-start = ((), (), s32[]{:S(2)}) async-start(), calls=%async_computation.6 | async-start | bytes 5013504 | tf_op jit(solution)/shard_map/all_gather | solution.py:106
  12.6 4.1 %collective-permute-start = (s32[128]{0:T(128)S(1)}, s32[128]{0:T(128)S(1)}, u32[]{:S(2)}, u32[]{:S(2)}) collective-permute-start(s32[128]{0:T(128)S(1)} %pad_add_fusion.2), channel_id=1, source_target_pairs={{0,32},{32,0},{1,33},{33,1},{2,34},{34,2},{3,35},{35,3},{4,36},{36... | collective-permute-start | bytes 1544 | tf_op jit(solution)/shard_map/ppermute | solution.py:102
  26.3 64.7 %all-to-all-start.1 = ((bf16[16,288,512]{2,1,0:T(8,128)(2,1)}), bf16[16,288,512]{2,1,0:T(8,128)(2,1)}, u32[]{:S(2)}, u32[]{:S(2)}) async-start(bf16[16,288,512]{2,1,0:T(8,128)(2,1)} %broadcast_in_dim.15), calls=%async_computation.1 | async-start | bytes 9437184 | tf_op jit(solution)/shard_map/all_to_all | solution.py:107
  91.1 0.7 copy-start
  91.7 0.7 copy-start.1
  107.0 26.0 %all-to-all-start.3 = ((bf16[16,48,512]{2,1,0:T(8,128)(2,1)}), bf16[16,48,512]{2,1,0:T(8,128)(2,1)S(1)}, u32[]{:S(2)}, u32[]{:S(2)}) async-start(bf16[16,48,512]{2,1,0:T(8,128)(2,1)} %get-tuple-element.11), calls=%async_computation.3 | async-start | bytes 1572864 | tf_op jit(solution)/shard_map/all_to_all | solution.py:133
  120.9 3.4 %collective-permute-start.1 = (bf16[8,48,512]{2,1,0:T(8,128)(2,1)S(1)}, bf16[8,48,512]{2,1,0:T(8,128)(2,1)S(1)}, u32[]{:S(2)}, u32[]{:S(2)}) collective-permute-start(bf16[8,48,512]{2,1,0:T(8,128)(2,1)S(1)} %get-tuple-element.10), channel_id=1, source_target_pairs={{0,32},{32,0},{1,33},{33,1},{2,34},{34,2},{3,35},{35,3},{4,36},{36... | collective-permute-start | bytes 1179656 | tf_op jit(solution)/shard_map/ppermute | solution.py:134
  133.0 22.0 %all-to-all-start.2 = ((bf16[8,48,512]{2,1,0:T(8,128)(2,1)}), bf16[8,48,512]{2,1,0:T(8,128)(2,1)S(1)}, u32[]{:S(2)}, u32[]{:S(2)}) async-start(bf16[8,48,512]{2,1,0:T(8,128)(2,1)} %add_convert_fusion), calls=%async_computation.2 | async-start | bytes 786432 | tf_op jit(solution)/shard_map/all_to_all | solution.py:136
Sparse Core Ops, SparseCore 0:
  11.1 46.9 all-gather.2

commit v3 on v2

--- a/solution.py
+++ b/solution.py
@@ -27,16 +27,21 @@
 def select_kernel(place_ref, lists_ref, picked_ref):
     own_y = place_ref[0]
     own_k = place_ref[1]
+    own_z = place_ref[2]
 
     def each_list(which, found):
         def each_slot(slot, found):
             row_block = lists_ref[which, 2 * slot]
             col_block = lists_ref[which, 2 * slot + 1]
-            near = ((row_block >> 5) & 1) * Z + ((row_block >> 2) & 7)
+            core = (((row_block >> 5) & 1) ^ own_k) * Z
+            row_z = (row_block >> 2) & 7
+            apart = row_z ^ own_z
+            near = core + ((row_z - own_z) & 7)
+            back = core + (apart & 1) * 4 + (apart & 2) + (apart >> 2)
             far = ((col_block >> 6) & 3) * Y + (col_block & 3)
             same = (row_block == col_block).astype(jnp.int32)
             mine = ((row_block & 3) == own_y) & (((col_block >> 5) & 1) == own_k)
-            picked_ref[found + 1] = same * 256 + near * 16 + far
+            picked_ref[found + 1] = ((same * 16 + back) * 16 + near) * 16 + far
             return found + mine.astype(jnp.int32)
 
         return lax.fori_loop(0, lists_ref[which, 2 * MAXP], each_slot, found)
@@ -44,19 +49,26 @@
     picked_ref[0] = lax.fori_loop(0, LISTS, each_list, jnp.int32(0))
 
 
-def tile_kernel(
-    place_ref, picked_ref, near_ref, far_ref, keep_out, give_out, far_out, near_sum, far_sum
-):
+def tile_kernel(picked_ref, far_hbm, *refs):
+    near_hbm = refs[:WAYS]
+    keep_out, give_out, far_out, near_ref, far_ref, near_sum, far_sum, sems = refs[WAYS:]
+    copies = [pltpu.make_async_copy(far_hbm, far_ref, sems.at[WAYS])]
+    for slot in range(WAYS):
+        copies.append(pltpu.make_async_copy(near_hbm[slot], near_ref.at[slot], sems.at[slot]))
+    for copy in copies:
+        copy.start()
     near_sum[...] = jnp.zeros_like(near_sum)
     far_sum[...] = jnp.zeros_like(far_sum)
     ones = (lax.broadcasted_iota(jnp.int32, (AUG - VEC, BS), 0) == 0).astype(jnp.bfloat16)
+    for copy in copies:
+        copy.wait()
 
     def each_tile(number, carry):
         code = picked_ref[number + 1]
-        same = code >> 8
+        back = (code >> 8) & 15
         near = (code >> 4) & 15
         far = code & 15
-        mirror = jnp.where(same == 1, 0.0, 1.0).astype(jnp.float32)
+        mirror = jnp.where((code >> 12) == 1, 0.0, 1.0).astype(jnp.float32)
         far_embed = far_ref[far, :EMB, :]
         near_vec = jnp.concatenate([near_ref[near, EMB:, :], ones], axis=0)
         far_vec = jnp.concatenate([far_ref[far, EMB:, :], ones], axis=0)
@@ -70,17 +82,24 @@
             near_terms = lax.dot_general(
                 far_vec, tile, (((1,), (1,)), ((), ())), preferred_element_type=jnp.float32
             )
-            near_sum[near, :, cut] += near_terms
+            near_sum[back, :, cut] += near_terms
             part = jnp.dot(near_vec[:, cut], tile, preferred_element_type=jnp.float32)
             far_terms = part if far_terms is None else far_terms + part
         far_sum[far] += far_terms * mirror
         return carry
 
     lax.fori_loop(0, picked_ref[0], each_tile, 0)
-    own_k = place_ref[1]
-    keep_out[...] = near_sum[pl.ds(own_k * Z, Z)]
-    give_out[...] = near_sum[pl.ds((1 - own_k) * Z, Z)].astype(jnp.bfloat16)
+    keep_out[...] = near_sum[:Z]
+    give_out[...] = near_sum[Z:].astype(jnp.bfloat16)
     far_out[...] = far_sum[...].astype(jnp.bfloat16)
+
+
+def shift(values, axis, size, by):
+    return lax.ppermute(values, axis, [(i, (i + by) % size) for i in range(size)])
+
+
+def swap(values, axis, size, bit):
+    return lax.ppermute(values, axis, [(i, i ^ bit) for i in range(size)])
 
 
 def on_device(embeddings, vectors, block_pairs, counts):
@@ -99,15 +118,17 @@
     own_list = jnp.concatenate(
         [block_pairs.reshape(-1), counts, jnp.zeros((128 - 2 * MAXP - 1,), jnp.int32)]
     )
-    other_list = lax.ppermute(own_list, "k", [(0, 1), (1, 0)])
-    chip_lists = jnp.stack([own_list, other_list])
-    lists = lax.all_to_all(jnp.broadcast_to(chip_lists[None], (Y, K, 128)), "y", 0, 0)
-    lists, far_send = lax.optimization_barrier((lists.reshape(LISTS, 128), far_send))
-    near_all = lax.all_gather(near_send, NEAR)
-    far_all = lax.all_to_all(
-        jnp.broadcast_to(far_send[None], (WAYS,) + far_send.shape), FAR, 0, 0
-    )
-    place = jnp.stack([lax.axis_index("y"), lax.axis_index("k")]).astype(jnp.int32)
+    chip_lists = jnp.stack([own_list, swap(own_list, "k", K, 1)])
+    lists = jnp.concatenate([chip_lists] + [shift(chip_lists, "y", Y, by) for by in (1, 2, 3)])
+    far_all = lax.all_gather(far_send, FAR)
+    ring = {0: near_send}
+    for step in range(1, Z // 2 + 1):
+        ring[Z - step] = shift(ring[(Z - step + 1) % Z], "z", Z, 1)
+        if step < Z // 2:
+            ring[step] = shift(ring[step - 1], "z", Z, -1)
+    near_blocks = [ring[i] for i in range(Z)]
+    near_blocks += [swap(block, "k", K, 1) for block in near_blocks]
+    place = jnp.stack([lax.axis_index(name) for name in ("y", "k", "z")]).astype(jnp.int32)
     smem = pl.BlockSpec(memory_space=pltpu.SMEM)
     vmem = pl.BlockSpec(memory_space=pltpu.VMEM)
     picked = pl.pallas_call(
@@ -124,19 +145,21 @@
             jax.ShapeDtypeStruct((Z, AUG, BS), jnp.bfloat16),
             jax.ShapeDtypeStruct((WAYS, AUG, BS), jnp.bfloat16),
         ],
-        in_specs=[smem, smem, vmem, vmem],
+        in_specs=[smem] + [pl.BlockSpec(memory_space=pl.ANY)] * (1 + WAYS),
         out_specs=[vmem, vmem, vmem],
-        scratch_shapes=[pltpu.VMEM((WAYS, AUG, BS), jnp.float32)] * 2,
+        scratch_shapes=[pltpu.VMEM((WAYS, EMB + VEC, BS), jnp.bfloat16)] * 2
+        + [pltpu.VMEM((WAYS, AUG, BS), jnp.float32)] * 2
+        + [pltpu.SemaphoreType.DMA((WAYS + 1,))],
         compiler_params=pltpu.CompilerParams(vmem_limit_bytes=48 * 1024 * 1024),
         name="tiles",
-    )(place, picked, near_all, far_all)
+    )(picked, far_all, *near_blocks)
     far_back = lax.all_to_all(far_part, FAR, 0, 0)
-    near_taken = lax.ppermute(near_give, "k", [(0, 1), (1, 0)])
-    near_pair = (near_keep + near_taken.astype(jnp.float32)).astype(jnp.bfloat16)
-    near_back = lax.all_to_all(near_pair, "z", 0, 0)
-    total = jnp.sum(near_back.astype(jnp.float32), axis=0) + jnp.sum(
-        far_back.astype(jnp.float32), axis=0
-    )
+    near_total = near_keep + swap(near_give, "k", K, 1).astype(jnp.float32)
+    for bit in (1, 2, 4):
+        left = near_total.shape[0] // 2
+        taken = swap(near_total[left:].astype(jnp.bfloat16), "z", Z, bit)
+        near_total = near_total[:left] + taken.astype(jnp.float32)
+    total = near_total[0] + jnp.sum(far_back.astype(jnp.float32), axis=0)
     walked = total[:VEC] / total[VEC : VEC + 1]
     points = BS * X * K * Z * Y
     local_gram = jnp.dot(

time: 193 us -> 165 us (0.85)
  waiting for transfers between devices: 81.5 us -> 44.7 us
  starting transfers between devices: 30.7 us -> 42.2 us
  local copies, waits for them, and re-layouts: 6.25 us -> 4.19 us
    all_to_all x2 -> x0, waiting for transfers between devices: 71.5 us -> none  [the longest x1 56.5 us: on_device(): lax.all_to_all(jnp.broadcast_to(far_send[None], (WAYS,) + far_send.shape)...]
    ppermute x2 -> x23, starting transfers between devices: 5.32 us -> 38.1 us  [the longest x13 22.1 us: swap(): return lax.ppermute(values, axis, [(i, i ^ bit) for i in range(size)])]
    ppermute x2 -> x23, waiting for transfers between devices: 2.09 us -> 34.5 us  [the longest x10 20.4 us: shift(): lax.ppermute(values, axis, [(i, (i + by) % size) for i in range(size)])]
    all_to_all x2 -> x0, starting transfers between devices: 11.4 us -> none  [the longest x1 6.89 us: on_device(): near_back = lax.all_to_all(near_pair, 'z', 0, 0)]
    all_gather x1, waiting for transfers between devices: 0.01 us -> 10 us  [on_device(): far_all = lax.all_gather(far_send, FAR)]
    all_to_all x1, starting transfers between devices: 13.9 us -> 4.08 us  [on_device(): far_back = lax.all_to_all(far_part, FAR, 0, 0)]
    all_to_all x1, waiting for transfers between devices: 7.88 us -> 0.19 us  [on_device(): far_back = lax.all_to_all(far_part, FAR, 0, 0)]
    all_to_all x2, blocking collectives: 21.2 us -> 28.6 us  [on_device(): lax.all_to_all(jnp.broadcast_to(partial_gram, (WAYS, 8, 128)), group, 0, 0)]
  transfers between devices with their start and end apart: 6 -> 25, of which waited for: 5 -> 12; matrix products, arithmetic and copies ran while one was open for 3% -> 2% of each run, Pallas kernels for 2% -> 2%
where the time goes in v3:
time: 165 us; the launch traced here: 164 us
  waiting for transfers between devices  44.7 us (27%)
  starting transfers between devices  42.2 us (26%)
  blocking collectives  28.6 us (17%)
  Pallas kernels  16.6 us (10%)
  between operations  14.9 us (9%)
  other arithmetic  11 us (7%)
  local copies, waits for them, and re-layouts  4.19 us (3%)
    all_to_all x2, blocking collectives, on_device(): lax.all_to_all(jnp.broadcast_to(partial_gram, (WAYS, 8, 128)), group, 0, 0)  28.6 us
    ppermute x13, starting transfers between devices, swap(): return lax.ppermute(values, axis, [(i, i ^ bit) for i in range(size)])  22.1 us
    ppermute x10, waiting for transfers between devices, shift(): lax.ppermute(values, axis, [(i, (i + by) % size) for i in range(size)])  20.4 us
    ppermute x10, starting transfers between devices, shift(): lax.ppermute(values, axis, [(i, (i + by) % size) for i in range(size)])  16.1 us
    ppermute x13, waiting for transfers between devices, swap(): return lax.ppermute(values, axis, [(i, i ^ bit) for i in range(size)])  14.1 us
    pallas_call x1, Pallas kernels, on_device(): pl.pallas_call(tile_kernel, out_shape=[jax.ShapeDtypeStruct((Z, AUG, BS),...  12.8 us
    all_gather x1, waiting for transfers between devices, on_device(): far_all = lax.all_gather(far_send, FAR)  10 us
    all_to_all x1, starting transfers between devices, on_device(): far_back = lax.all_to_all(far_part, FAR, 0, 0)  4.08 us
  transfers between devices with their start and end apart: 25, of which 12 were waited for; matrix products, arithmetic and copies ran while one was open for 2% of the time, Pallas kernels for 2%

profile of v3, /device:TPU:1, one launch (start us, length us, event | category | flops | bytes accessed | tf_op | source)
XLA Modules:
  0.0 163.6 jit_solution(15014104571439056751)
XLA Ops:
  7.2 0.0 all-gather.3.cloned.1.call-start
  7.2 0.8 convert_element_type.22
  8.1 1.1 copy.13
  9.2 1.7 %pad_maximum_fusion = (bf16[288,512]{1,0:T(8,128)(2,1)S(1)}, bf16[288,512]{1,0:T(8,128)(2,1)}) fusion(bf16[32,512]{1,0:T(8,128)(2,1)S(1)} %convert_element_type.22, bf16[256,512]{1,0:T(8,128)(2,1)S(1)} %maximum_multiply_fusion, bf16[256,512]{1,0:T(8,128)(2,1)} %param.4), kind=kLoop, calls=%fused_computation.4 | loop fusion | flops 1032192 | bytes 1146880 | tf_op jit(solution)/shard_map/concatenate | solution.py:109
  10.9 0.0 all-gather.3.cloned.1.call-update
  11.0 2.5 %collective-permute-start.7 = (bf16[288,512]{1,0:T(8,128)(2,1)S(1)}, bf16[288,512]{1,0:T(8,128)(2,1)S(1)}, u32[]{:S(2)}, u32[]{:S(2)}) collective-permute-start(bf16[288,512]{1,0:T(8,128)(2,1)S(1)} %get-tuple-element.12.refs_0_), channel_id=1, source_target_pairs={{0,4},{4,8},{8,12},{12,16},{16,20},{20,24},{24,28},{28,0},{1,5},{5... | collective-permute-start | bytes 884744 | tf_op jit(solution)/shard_map/ppermute | solution.py:98
  13.5 4.0 %collective-permute-start.4 = (bf16[288,512]{1,0:T(8,128)(2,1)S(1)}, bf16[288,512]{1,0:T(8,128)(2,1)S(1)}, u32[]{:S(2)}, u32[]{:S(2)}) collective-permute-start(bf16[288,512]{1,0:T(8,128)(2,1)S(1)} %get-tuple-element.12.refs_0_), channel_id=1, source_target_pairs={{0,28},{4,0},{8,4},{12,8},{16,12},{20,16},{24,20},{28,24},{1,29},{... | collective-permute-start | bytes 884744 | tf_op jit(solution)/shard_map/ppermute | solution.py:98
  17.5 6.6 %collective-permute-done.7.refs_7_ = bf16[288,512]{1,0:T(8,128)(2,1)S(1)} collective-permute-done((bf16[288,512]{1,0:T(8,128)(2,1)S(1)}, bf16[288,512]{1,0:T(8,128)(2,1)S(1)}, u32[]{:S(2)}, u32[]{:S(2)}) %collective-permute-start.7) | collective-permute-done | bytes 294944 | tf_op jit(solution)/shard_map/ppermute | solution.py:98
  24.8 0.8 copy.12
  25.6 0.1 reshape.21
  25.7 2.7 %collective-permute-start.5 = (bf16[288,512]{1,0:T(8,128)(2,1)S(1)}, bf16[288,512]{1,0:T(8,128)(2,1)S(1)}, u32[]{:S(2)}, u32[]{:S(2)}) collective-permute-start(bf16[288,512]{1,0:T(8,128)(2,1)S(1)} %collective-permute-done.4.refs_1_), channel_id=1, source_target_pairs={{0,28},{4,0},{8,4},{12,8},{16,12},{20,16},{24,20},{28,24},{1,29},{... | collective-permute-start | bytes 884744 | tf_op jit(solution)/shard_map/ppermute | solution.py:98
  28.5 4.3 %collective-permute-done.8.refs_6_ = bf16[288,512]{1,0:T(8,128)(2,1)S(1)} collective-permute-done((bf16[288,512]{1,0:T(8,128)(2,1)S(1)}, bf16[288,512]{1,0:T(8,128)(2,1)S(1)}, u32[]{:S(2)}, u32[]{:S(2)}) %collective-permute-start.8) | collective-permute-done | bytes 294944 | tf_op jit(solution)/shard_map/ppermute | solution.py:98
  32.8 0.0 collective-permute-start.9
  32.8 0.1 pad_add_fusion.2
  32.9 2.1 %collective-permute-start = (s32[128]{0:T(128)S(1)}, s32[128]{0:T(128)S(1)}, u32[]{:S(2)}, u32[]{:S(2)}) collective-permute-start(s32[128]{0:T(128)S(1)} %pad_add_fusion.2), channel_id=1, source_target_pairs={{0,32},{32,0},{1,33},{33,1},{2,34},{34,2},{3,35},{35,3},{4,36},{36... | collective-permute-start | bytes 1544 | tf_op jit(solution)/shard_map/ppermute | solution.py:102
  34.9 0.1 fusion.9
  35.0 0.7 collective-permute-done
  35.8 2.7 %collective-permute-start.3 = (s32[2,128]{1,0:T(2,128)S(1)}, s32[2,128]{1,0:T(2,128)S(1)}, u32[]{:S(2)}, u32[]{:S(2)}) collective-permute-start(s32[2,128]{1,0:T(2,128)S(1)} %pad_add_fusion), channel_id=1, source_target_pairs={{0,3},{1,0},{2,1},{3,2},{4,7},{5,4},{6,5},{7,6},{8,11},{9,8},{10,9... | collective-permute-start | bytes 3080 | tf_op jit(solution)/shard_map/ppermute | solution.py:98
  38.5 0.3 collective-permute-start.2
  38.8 0.7 collective-permute-start.1
  39.5 0.0 collective-permute-done.3
  39.5 1.1 collective-permute-start.11
  40.7 1.7 %collective-permute-done.2 = s32[2,128]{1,0:T(2,128)S(1)} collective-permute-done((s32[2,128]{1,0:T(2,128)S(1)}, s32[2,128]{1,0:T(2,128)S(1)}, u32[]{:S(2)}, u32[]{:S(2)}) %collective-permute-start.2) | collective-permute-done | bytes 1056 | tf_op jit(solution)/shard_map/ppermute | solution.py:98
  42.4 1.7 %collective-permute-start.18 = (bf16[288,512]{1,0:T(8,128)(2,1)S(1)}, bf16[288,512]{1,0:T(8,128)(2,1)S(1)}, u32[]{:S(2)}, u32[]{:S(2)}) collective-permute-start(bf16[288,512]{1,0:T(8,128)(2,1)S(1)} %collective-permute-done.7.refs_7_), channel_id=1, source_target_pairs={{0,32},{32,0},{1,33},{33,1},{2,34},{34,2},{3,35},{35,3},{4,36},{36... | collective-permute-start | bytes 884744 | tf_op jit(solution)/shard_map/ppermute | solution.py:102
  44.2 0.0 collective-permute-done.1
  44.2 0.4 collective-permute-start.12
  44.6 3.0 %collective-permute-start.6 = (bf16[288,512]{1,0:T(8,128)(2,1)S(1)}, bf16[288,512]{1,0:T(8,128)(2,1)S(1)}, u32[]{:S(2)}, u32[]{:S(2)}) collective-permute-start(bf16[288,512]{1,0:T(8,128)(2,1)S(1)} %collective-permute-done.5.refs_2_), channel_id=1, source_target_pairs={{0,28},{4,0},{8,4},{12,8},{16,12},{20,16},{24,20},{28,24},{1,29},{... | collective-permute-start | bytes 884744 | tf_op jit(solution)/shard_map/ppermute | solution.py:98
  47.6 0.4 collective-permute-start.17
  48.0 0.2 collective-permute-start.13
  48.2 0.4 collective-permute-start.16
  48.5 5.4 %collective-permute-done.6.refs_3_ = bf16[288,512]{1,0:T(8,128)(2,1)S(1)} collective-permute-done((bf16[288,512]{1,0:T(8,128)(2,1)S(1)}, bf16[288,512]{1,0:T(8,128)(2,1)S(1)}, u32[]{:S(2)}, u32[]{:S(2)}) %collective-permute-start.6) | collective-permute-done | bytes 294944 | tf_op jit(solution)/shard_map/ppermute | solution.py:98
  53.9 0.9 collective-permute-start.14
  54.8 2.3 %collective-permute-done.10.refs_4_ = bf16[288,512]{1,0:T(8,128)(2,1)S(1)} collective-permute-done((bf16[288,512]{1,0:T(8,128)(2,1)S(1)}, bf16[288,512]{1,0:T(8,128)(2,1)S(1)}, u32[]{:S(2)}, u32[]{:S(2)}) %collective-permute-start.10) | collective-permute-done | bytes 294944 | tf_op jit(solution)/shard_map/ppermute | solution.py:98
  57.1 1.1 collective-permute-start.15
  58.2 0.6 pad_add_fusion.1.place_ref
  58.8 1.3 concatenate.17.lists_ref
  60.0 3.8 %select_pairs.1.picked_ref = s32[256]{0:T(256)} custom-call(s32[3]{0:T(128)} %pad_add_fusion.1.place_ref, s32[8,128]{1,0:T(8,128)} %concatenate.17.lists_ref), custom_call_target="tpu_custom_call" | custom-call | tf_op jit(solution)/shard_map/select_pairs/pallas_call | solution.py:134
  63.9 10.0 %all-gather.3.cloned.1.call-done = bf16[4608,512]{1,0:T(8,128)(2,1)} async-done(((bf16[288,512]{1,0:T(8,128)(2,1)}), bf16[4608,512]{1,0:T(8,128)(2,1)}) %all-gather.3.cloned.1.call-update) | async-done | bytes 4718608 | tf_op jit(solution)/shard_map/all_gather | solution.py:123
  74.0 0.7 copy-done
  74.6 12.8 %tiles.1 = (f32[8,48,512]{2,1,0:T(8,128)S(1)}, bf16[8,48,512]{2,1,0:T(8,128)(2,1)S(1)}, bf16[16,48,512]{2,1,0:T(8,128)(2,1)}) custom-call(s32[256]{0:T(256)S(1)} %copy-done, bf16[16,288,512]{2,1,0:T(8,128)(2,1)} %bitcast.23, bf16[288,512]{1,0:T(8,128)(2,1)S(1)} %get-tuple-element.12.refs_0_, bf16[288,512]{1,0:T(8,128)(2,1)S(1)} %collective-permute-done.4.refs_1_, ...), custom_call_target="tpu_custom_call" | custom-call | tf_op jit(solution)/shard_map/tiles/pallas_call | solution.py:141
  87.4 3.9 %collective-permute-start.19 = (bf16[8,48,512]{2,1,0:T(8,128)(2,1)S(1)}, bf16[8,48,512]{2,1,0:T(8,128)(2,1)S(1)}, u32[]{:S(2)}, u32[]{:S(2)}) collective-permute-start(bf16[8,48,512]{2,1,0:T(8,128)(2,1)S(1)} %get-tuple-element.6), channel_id=1, source_target_pairs={{0,32},{32,0},{1,33},{33,1},{2,34},{34,2},{3,35},{35,3},{4,36},{36... | collective-permute-start | bytes 1179656 | tf_op jit(solution)/shard_map/ppermute | solution.py:102
  91.4 1.3 collective-permute-done.19
  92.7 0.1 convert_add_fusion
  92.9 3.6 %collective-permute-start.20 = (bf16[4,48,512]{2,1,0:T(8,128)(2,1)S(1)}, bf16[4,48,512]{2,1,0:T(8,128)(2,1)S(1)}, u32[]{:S(2)}, u32[]{:S(2)}) collective-permute-start(bf16[4,48,512]{2,1,0:T(8,128)(2,1)S(1)} %slice.76), channel_id=1, source_target_pairs={{0,4},{4,0},{8,12},{12,8},{16,20},{20,16},{24,28},{28,24},{1,5},{5... | collective-permute-start | bytes 589832 | tf_op jit(solution)/shard_map/ppermute | solution.py:102
  96.5 4.1 %all-to-all-start = ((bf16[16,48,512]{2,1,0:T(8,128)(2,1)}), bf16[16,48,512]{2,1,0:T(8,128)(2,1)S(1)}, u32[]{:S(2)}, u32[]{:S(2)}) async-start(bf16[16,48,512]{2,1,0:T(8,128)(2,1)} %get-tuple-element.7), calls=%async_computation | async-start | bytes 1572864 | tf_op jit(solution)/shard_map/all_to_all | solution.py:156
  100.6 1.1 collective-permute-done.20
  101.7 5.4 %collective-permute-start.21 = (bf16[2,48,512]{2,1,0:T(8,128)(2,1)S(1)}, bf16[2,48,512]{2,1,0:T(8,128)(2,1)S(1)}, u32[]{:S(2)}, u32[]{:S(2)}) collective-permute-start(bf16[2,48,512]{2,1,0:T(8,128)(2,1)S(1)} %slice.77), channel_id=1, source_target_pairs={{0,8},{4,12},{8,0},{12,4},{16,24},{20,28},{24,16},{28,20},{1,9},{5... | collective-permute-start | bytes 294920 | tf_op jit(solution)/shard_map/ppermute | solution.py:102
  107.1 5.1 %collective-permute-done.21 = bf16[2,48,512]{2,1,0:T(8,128)(2,1)S(1)} collective-permute-done((bf16[2,48,512]{2,1,0:T(8,128)(2,1)S(1)}, bf16[2,48,512]{2,1,0:T(8,128)(2,1)S(1)}, u32[]{:S(2)}, u32[]{:S(2)}) %collective-permute-start.21) | collective-permute-done | bytes 98336 | tf_op jit(solution)/shard_map/ppermute | solution.py:102
  112.2 0.9 collective-permute-start.22
  113.1 0.2 all-to-all-done
  113.3 0.1 convert_reduce_fusion
  113.4 5.8 %collective-permute-done.22 = bf16[1,48,512]{2,1,0:T(8,128)(2,1)S(1)} collective-permute-done((bf16[1,48,512]{2,1,0:T(8,128)(2,1)S(1)}, bf16[1,48,512]{2,1,0:T(8,128)(2,1)S(1)}, u32[]{:S(2)}, u32[]{:S(2)}) %collective-permute-start.22) | collective-permute-done | bytes 49184 | tf_op jit(solution)/shard_map/ppermute | solution.py:102
  119.2 0.2 fusion.3
  119.4 0.1 broadcast_in_dim.19
  119.5 13.0 %all_to_all.15 = f32[16,8,128]{2,1,0:T(8,128)S(1)} all-to-all(f32[16,8,128]{2,1,0:T(8,128)S(1)} %broadcast_in_dim.20), channel_id=1, replica_groups=mesh['x'=4,'k'=2,'z'=8,'y'=4] {'x','y'}, dimensions={0} | all-to-all | bytes 131072 | tf_op jit(solution)/shard_map/all_to_all | solution.py:170
  132.6 15.6 %all_to_all.16 = f32[16,8,128]{2,1,0:T(8,128)S(1)} all-to-all(f32[16,8,128]{2,1,0:T(8,128)S(1)} %broadcast_in_dim.21), channel_id=1, replica_groups=mesh['x'=4,'k'=2,'z'=8,'y'=4] {'k','z'}, dimensions={0} | all-to-all | bytes 131072 | tf_op jit(solution)/shard_map/all_to_all | solution.py:170
  148.2 0.1 div.31
  148.3 0.1 copy.14
  148.4 2.9 %cholesky.17 = f32[32,32]{1,0:T(8,128)S(1)} custom-call(f32[32,32]{1,0:T(8,128)S(1)} %fusion.6), custom_call_target="Cholesky" | custom-call | tf_op jit(solution)/shard_map/jit(cholesky)/cholesky | solution.py:173
  151.3 0.6 compare_reduce_fusion
  152.0 1.3 select_bitcast_fusion
  153.2 2.4 %custom-call.6 = f32[1,32,32]{1,2,0:T(8,128)S(1)} custom-call(f32[1,32,32]{2,1,0:T(8,128)S(1)} %get-tuple-element.8), custom_call_target="InvertDiagBlocksLowerTriangular" | custom-call | tf_op jit(solution)/shard_map/triangular_solve | solution.py:174
  155.6 0.2 fusion.4
  155.9 0.8 fusion.2
  (32 shorter events, 0.4 us)
Async XLA Ops:
  7.2 66.8 %all-gather.3.cloned.1.call-start = ((), (), s32[]{:S(2)}) async-start(), calls=%async_computation.3 | async-start | bytes 5013504 | tf_op jit(solution)/shard_map/all_gather | solution.py:123
  11.0 13.2 %collective-permute-start.7 = (bf16[288,512]{1,0:T(8,128)(2,1)S(1)}, bf16[288,512]{1,0:T(8,128)(2,1)S(1)}, u32[]{:S(2)}, u32[]{:S(2)}) collective-permute-start(bf16[288,512]{1,0:T(8,128)(2,1)S(1)} %get-tuple-element.12.refs_0_), channel_id=1, source_target_pairs={{0,4},{4,8},{8,12},{12,16},{16,20},{20,24},{24,28},{28,0},{1,5},{5... | collective-permute-start | bytes 884744 | tf_op jit(solution)/shard_map/ppermute | solution.py:98
  13.5 12.2 %collective-permute-start.4 = (bf16[288,512]{1,0:T(8,128)(2,1)S(1)}, bf16[288,512]{1,0:T(8,128)(2,1)S(1)}, u32[]{:S(2)}, u32[]{:S(2)}) collective-permute-start(bf16[288,512]{1,0:T(8,128)(2,1)S(1)} %get-tuple-element.12.refs_0_), channel_id=1, source_target_pairs={{0,28},{4,0},{8,4},{12,8},{16,12},{20,16},{24,20},{28,24},{1,29},{... | collective-permute-start | bytes 884744 | tf_op jit(solution)/shard_map/ppermute | solution.py:98
  24.2 8.6 %collective-permute-start.8 = (bf16[288,512]{1,0:T(8,128)(2,1)S(1)}, bf16[288,512]{1,0:T(8,128)(2,1)S(1)}, u32[]{:S(2)}, u32[]{:S(2)}) collective-permute-start(bf16[288,512]{1,0:T(8,128)(2,1)S(1)} %collective-permute-done.7.refs_7_), channel_id=1, source_target_pairs={{0,4},{4,8},{8,12},{12,16},{16,20},{20,24},{24,28},{28,0},{1,5},{5... | collective-permute-start | bytes 884744 | tf_op jit(solution)/shard_map/ppermute | solution.py:98
  25.7 18.9 %collective-permute-start.5 = (bf16[288,512]{1,0:T(8,128)(2,1)S(1)}, bf16[288,512]{1,0:T(8,128)(2,1)S(1)}, u32[]{:S(2)}, u32[]{:S(2)}) collective-permute-start(bf16[288,512]{1,0:T(8,128)(2,1)S(1)} %collective-permute-done.4.refs_1_), channel_id=1, source_target_pairs={{0,28},{4,0},{8,4},{12,8},{16,12},{20,16},{24,20},{28,24},{1,29},{... | collective-permute-start | bytes 884744 | tf_op jit(solution)/shard_map/ppermute | solution.py:98
  32.8 14.8 %collective-permute-start.9 = (bf16[288,512]{1,0:T(8,128)(2,1)S(1)}, bf16[288,512]{1,0:T(8,128)(2,1)S(1)}, u32[]{:S(2)}, u32[]{:S(2)}) collective-permute-start(bf16[288,512]{1,0:T(8,128)(2,1)S(1)} %collective-permute-done.8.refs_6_), channel_id=1, source_target_pairs={{0,4},{4,8},{8,12},{12,16},{16,20},{20,24},{24,28},{28,0},{1,5},{5... | collective-permute-start | bytes 884744 | tf_op jit(solution)/shard_map/ppermute | solution.py:98
  32.9 2.9 %collective-permute-start = (s32[128]{0:T(128)S(1)}, s32[128]{0:T(128)S(1)}, u32[]{:S(2)}, u32[]{:S(2)}) collective-permute-start(s32[128]{0:T(128)S(1)} %pad_add_fusion.2), channel_id=1, source_target_pairs={{0,32},{32,0},{1,33},{33,1},{2,34},{34,2},{3,35},{35,3},{4,36},{36... | collective-permute-start | bytes 1544 | tf_op jit(solution)/shard_map/ppermute | solution.py:102
  35.8 3.8 %collective-permute-start.3 = (s32[2,128]{1,0:T(2,128)S(1)}, s32[2,128]{1,0:T(2,128)S(1)}, u32[]{:S(2)}, u32[]{:S(2)}) collective-permute-start(s32[2,128]{1,0:T(2,128)S(1)} %pad_add_fusion), channel_id=1, source_target_pairs={{0,3},{1,0},{2,1},{3,2},{4,7},{5,4},{6,5},{7,6},{8,11},{9,8},{10,9... | collective-permute-start | bytes 3080 | tf_op jit(solution)/shard_map/ppermute | solution.py:98
  38.5 3.9 %collective-permute-start.2 = (s32[2,128]{1,0:T(2,128)S(1)}, s32[2,128]{1,0:T(2,128)S(1)}, u32[]{:S(2)}, u32[]{:S(2)}) collective-permute-start(s32[2,128]{1,0:T(2,128)S(1)} %pad_add_fusion), channel_id=1, source_target_pairs={{0,2},{1,3},{2,0},{3,1},{4,6},{5,7},{6,4},{7,5},{8,10},{9,11},{10,... | collective-permute-start | bytes 3080 | tf_op jit(solution)/shard_map/ppermute | solution.py:98
  38.8 5.3 %collective-permute-start.1 = (s32[2,128]{1,0:T(2,128)S(1)}, s32[2,128]{1,0:T(2,128)}, u32[]{:S(2)}, u32[]{:S(2)}) collective-permute-start(s32[2,128]{1,0:T(2,128)S(1)} %pad_add_fusion), channel_id=1, source_target_pairs={{0,1},{1,2},{2,3},{3,0},{4,5},{5,6},{6,7},{7,4},{8,9},{9,10},{10,1... | collective-permute-start | bytes 3080 | tf_op jit(solution)/shard_map/ppermute | solution.py:98
  39.5 8.0 %collective-permute-start.11 = (bf16[288,512]{1,0:T(8,128)(2,1)S(1)}, bf16[288,512]{1,0:T(8,128)(2,1)S(1)}, u32[]{:S(2)}, u32[]{:S(2)}) collective-permute-start(bf16[288,512]{1,0:T(8,128)(2,1)S(1)} %get-tuple-element.12.refs_0_), channel_id=1, source_target_pairs={{0,32},{32,0},{1,33},{33,1},{2,34},{34,2},{3,35},{35,3},{4,36},{36... | collective-permute-start | bytes 884744 | tf_op jit(solution)/shard_map/ppermute | solution.py:102
  42.4 5.6 %collective-permute-start.18 = (bf16[288,512]{1,0:T(8,128)(2,1)S(1)}, bf16[288,512]{1,0:T(8,128)(2,1)S(1)}, u32[]{:S(2)}, u32[]{:S(2)}) collective-permute-start(bf16[288,512]{1,0:T(8,128)(2,1)S(1)} %collective-permute-done.7.refs_7_), channel_id=1, source_target_pairs={{0,32},{32,0},{1,33},{33,1},{2,34},{34,2},{3,35},{35,3},{4,36},{36... | collective-permute-start | bytes 884744 | tf_op jit(solution)/shard_map/ppermute | solution.py:102
  44.2 4.0 %collective-permute-start.12 = (bf16[288,512]{1,0:T(8,128)(2,1)S(1)}, bf16[288,512]{1,0:T(8,128)(2,1)S(1)}, u32[]{:S(2)}, u32[]{:S(2)}) collective-permute-start(bf16[288,512]{1,0:T(8,128)(2,1)S(1)} %collective-permute-done.4.refs_1_), channel_id=1, source_target_pairs={{0,32},{32,0},{1,33},{33,1},{2,34},{34,2},{3,35},{35,3},{4,36},{36... | collective-permute-start | bytes 884744 | tf_op jit(solution)/shard_map/ppermute | solution.py:102
  44.6 9.3 %collective-permute-start.6 = (bf16[288,512]{1,0:T(8,128)(2,1)S(1)}, bf16[288,512]{1,0:T(8,128)(2,1)S(1)}, u32[]{:S(2)}, u32[]{:S(2)}) collective-permute-start(bf16[288,512]{1,0:T(8,128)(2,1)S(1)} %collective-permute-done.5.refs_2_), channel_id=1, source_target_pairs={{0,28},{4,0},{8,4},{12,8},{16,12},{20,16},{24,20},{28,24},{1,29},{... | collective-permute-start | bytes 884744 | tf_op jit(solution)/shard_map/ppermute | solution.py:98
  47.6 9.6 %collective-permute-start.10 = (bf16[288,512]{1,0:T(8,128)(2,1)S(1)}, bf16[288,512]{1,0:T(8,128)(2,1)S(1)}, u32[]{:S(2)}, u32[]{:S(2)}) collective-permute-start(bf16[288,512]{1,0:T(8,128)(2,1)S(1)} %collective-permute-done.9.refs_5_), channel_id=1, source_target_pairs={{0,4},{4,8},{8,12},{12,16},{16,20},{20,24},{24,28},{28,0},{1,5},{5... | collective-permute-start | bytes 884744 | tf_op jit(solution)/shard_map/ppermute | solution.py:98
  47.6 16.3 %collective-permute-start.17 = (bf16[288,512]{1,0:T(8,128)(2,1)S(1)}, bf16[288,512]{1,0:T(8,128)(2,1)S(1)}, u32[]{:S(2)}, u32[]{:S(2)}) collective-permute-start(bf16[288,512]{1,0:T(8,128)(2,1)S(1)} %collective-permute-done.8.refs_6_), channel_id=1, source_target_pairs={{0,32},{32,0},{1,33},{33,1},{2,34},{34,2},{3,35},{35,3},{4,36},{36... | collective-permute-start | bytes 884744 | tf_op jit(solution)/shard_map/ppermute | solution.py:102
  48.0 15.9 %collective-permute-start.13 = (bf16[288,512]{1,0:T(8,128)(2,1)S(1)}, bf16[288,512]{1,0:T(8,128)(2,1)}, u32[]{:S(2)}, u32[]{:S(2)}) collective-permute-start(bf16[288,512]{1,0:T(8,128)(2,1)S(1)} %collective-permute-done.5.refs_2_), channel_id=1, source_target_pairs={{0,32},{32,0},{1,33},{33,1},{2,34},{34,2},{3,35},{35,3},{4,36},{36... | collective-permute-start | bytes 884744 | tf_op jit(solution)/shard_map/ppermute | solution.py:102
  48.2 15.7 %collective-permute-start.16 = (bf16[288,512]{1,0:T(8,128)(2,1)S(1)}, bf16[288,512]{1,0:T(8,128)(2,1)}, u32[]{:S(2)}, u32[]{:S(2)}) collective-permute-start(bf16[288,512]{1,0:T(8,128)(2,1)S(1)} %collective-permute-done.9.refs_5_), channel_id=1, source_target_pairs={{0,32},{32,0},{1,33},{33,1},{2,34},{34,2},{3,35},{35,3},{4,36},{36... | collective-permute-start | bytes 884744 | tf_op jit(solution)/shard_map/ppermute | solution.py:102
  53.9 10.0 %collective-permute-start.14 = (bf16[288,512]{1,0:T(8,128)(2,1)S(1)}, bf16[288,512]{1,0:T(8,128)(2,1)}, u32[]{:S(2)}, u32[]{:S(2)}) collective-permute-start(bf16[288,512]{1,0:T(8,128)(2,1)S(1)} %collective-permute-done.6.refs_3_), channel_id=1, source_target_pairs={{0,32},{32,0},{1,33},{33,1},{2,34},{34,2},{3,35},{35,3},{4,36},{36... | collective-permute-start | bytes 884744 | tf_op jit(solution)/shard_map/ppermute | solution.py:102
  57.1 6.8 %collective-permute-start.15 = (bf16[288,512]{1,0:T(8,128)(2,1)S(1)}, bf16[288,512]{1,0:T(8,128)(2,1)}, u32[]{:S(2)}, u32[]{:S(2)}) collective-permute-start(bf16[288,512]{1,0:T(8,128)(2,1)S(1)} %collective-permute-done.10.refs_4_), channel_id=1, source_target_pairs={{0,32},{32,0},{1,33},{33,1},{2,34},{34,2},{3,35},{35,3},{4,36},{36... | collective-permute-start | bytes 884744 | tf_op jit(solution)/shard_map/ppermute | solution.py:102
  74.0 0.7 copy-start
  87.4 5.3 %collective-permute-start.19 = (bf16[8,48,512]{2,1,0:T(8,128)(2,1)S(1)}, bf16[8,48,512]{2,1,0:T(8,128)(2,1)S(1)}, u32[]{:S(2)}, u32[]{:S(2)}) collective-permute-start(bf16[8,48,512]{2,1,0:T(8,128)(2,1)S(1)} %get-tuple-element.6), channel_id=1, source_target_pairs={{0,32},{32,0},{1,33},{33,1},{2,34},{34,2},{3,35},{35,3},{4,36},{36... | collective-permute-start | bytes 1179656 | tf_op jit(solution)/shard_map/ppermute | solution.py:102
  92.9 8.7 %collective-permute-start.20 = (bf16[4,48,512]{2,1,0:T(8,128)(2,1)S(1)}, bf16[4,48,512]{2,1,0:T(8,128)(2,1)S(1)}, u32[]{:S(2)}, u32[]{:S(2)}) collective-permute-start(bf16[4,48,512]{2,1,0:T(8,128)(2,1)S(1)} %slice.76), channel_id=1, source_target_pairs={{0,4},{4,0},{8,12},{12,8},{16,20},{20,16},{24,28},{28,24},{1,5},{5... | collective-permute-start | bytes 589832 | tf_op jit(solution)/shard_map/ppermute | solution.py:102
  96.5 16.8 %all-to-all-start = ((bf16[16,48,512]{2,1,0:T(8,128)(2,1)}), bf16[16,48,512]{2,1,0:T(8,128)(2,1)S(1)}, u32[]{:S(2)}, u32[]{:S(2)}) async-start(bf16[16,48,512]{2,1,0:T(8,128)(2,1)} %get-tuple-element.7), calls=%async_computation | async-start | bytes 1572864 | tf_op jit(solution)/shard_map/all_to_all | solution.py:156
  101.7 10.5 %collective-permute-start.21 = (bf16[2,48,512]{2,1,0:T(8,128)(2,1)S(1)}, bf16[2,48,512]{2,1,0:T(8,128)(2,1)S(1)}, u32[]{:S(2)}, u32[]{:S(2)}) collective-permute-start(bf16[2,48,512]{2,1,0:T(8,128)(2,1)S(1)} %slice.77), channel_id=1, source_target_pairs={{0,8},{4,12},{8,0},{12,4},{16,24},{20,28},{24,16},{28,20},{1,9},{5... | collective-permute-start | bytes 294920 | tf_op jit(solution)/shard_map/ppermute | solution.py:102
  112.2 7.0 %collective-permute-start.22 = (bf16[1,48,512]{2,1,0:T(8,128)(2,1)S(1)}, bf16[1,48,512]{2,1,0:T(8,128)(2,1)S(1)}, u32[]{:S(2)}, u32[]{:S(2)}) collective-permute-start(bf16[1,48,512]{2,1,0:T(8,128)(2,1)S(1)} %slice.78), channel_id=1, source_target_pairs={{0,16},{4,20},{8,24},{12,28},{16,0},{20,4},{24,8},{28,12},{1,17},{... | collective-permute-start | bytes 147464 | tf_op jit(solution)/shard_map/ppermute | solution.py:102
Sparse Core Ops, SparseCore 0:
  11.1 62.8 all-gather.2

commit v4 on v3

--- a/solution.py
+++ b/solution.py
@@ -9,16 +9,17 @@
 from jax.sharding import Mesh
 from jax.sharding import PartitionSpec as P
 
-X, K, Z, Y = 4, 2, 8, 4
-COLS = Z * Y
-NEAR = ("k", "z")
+X, K, U, W, Y = 4, 2, 4, 2, 4
+Z = U * W
+NEAR = ("k", "u", "w")
 FAR = ("x", "y")
-EVERY = ("x", "k", "z", "y")
+EVERY = ("x", "k", "u", "w", "y")
 WAYS = 16
 BS = 512
 EMB = 256
 VEC = 32
 AUG = 48
+FIRST = 192
 MAXP = 24
 LISTS = K * Y
 SLOTS = 256
@@ -35,9 +36,8 @@
             col_block = lists_ref[which, 2 * slot + 1]
             core = (((row_block >> 5) & 1) ^ own_k) * Z
             row_z = (row_block >> 2) & 7
-            apart = row_z ^ own_z
             near = core + ((row_z - own_z) & 7)
-            back = core + (apart & 1) * 4 + (apart & 2) + (apart >> 2)
+            back = core + ((row_z ^ own_z) & 1) * U + (row_z >> 1)
             far = ((col_block >> 6) & 3) * Y + (col_block & 3)
             same = (row_block == col_block).astype(jnp.int32)
             mine = ((row_block & 3) == own_y) & (((col_block >> 5) & 1) == own_k)
@@ -49,10 +49,13 @@
     picked_ref[0] = lax.fori_loop(0, LISTS, each_list, jnp.int32(0))
 
 
-def tile_kernel(picked_ref, far_hbm, *refs):
+def tile_kernel(picked_ref, far_first, far_rest, *refs):
     near_hbm = refs[:WAYS]
     keep_out, give_out, far_out, near_ref, far_ref, near_sum, far_sum, sems = refs[WAYS:]
-    copies = [pltpu.make_async_copy(far_hbm, far_ref, sems.at[WAYS])]
+    copies = [
+        pltpu.make_async_copy(far_first, far_ref.at[:, :FIRST, :], sems.at[WAYS]),
+        pltpu.make_async_copy(far_rest, far_ref.at[:, FIRST:, :], sems.at[WAYS + 1]),
+    ]
     for slot in range(WAYS):
         copies.append(pltpu.make_async_copy(near_hbm[slot], near_ref.at[slot], sems.at[slot]))
     for copy in copies:
@@ -94,6 +97,32 @@
     far_out[...] = far_sum[...].astype(jnp.bfloat16)
 
 
+def finish_kernel(gram_ref, walked_ref, basis_out, factor_out, wide_ref):
+    row = lax.broadcasted_iota(jnp.int32, (VEC, 128), 0)
+    lane = lax.broadcasted_iota(jnp.int32, (VEC, 128), 1)
+    wide_ref[...] = (lane == row + VEC).astype(jnp.float32)
+    wide_ref[:, :VEC] = gram_ref[...]
+    wide = wide_ref[...]
+    factor = jnp.zeros((VEC, 128), jnp.float32)
+    for step in range(VEC):
+        pivot = wide[step : step + 1, step : step + 1]
+        root = lax.rsqrt(pivot)
+        root = root * (1.5 - 0.5 * pivot * root * root)
+        scaled = wide[step : step + 1, :] * root
+        column = jnp.broadcast_to(wide[:, step : step + 1] * root, (VEC, 128))
+        factor = jnp.where((lane == step) & (row >= step), column, factor)
+        lower = jnp.where(row > step, wide - column * scaled, wide)
+        wide = jnp.where(row == step, jnp.broadcast_to(scaled, (VEC, 128)), lower)
+    wide_ref[...] = wide
+    basis_out[...] = jnp.dot(
+        wide_ref[:, VEC : 2 * VEC],
+        walked_ref[...],
+        precision=lax.Precision.HIGHEST,
+        preferred_element_type=jnp.float32,
+    )
+    factor_out[...] = factor[:, :VEC]
+
+
 def shift(values, axis, size, by):
     return lax.ppermute(values, axis, [(i, (i + by) % size) for i in range(size)])
 
@@ -114,21 +143,24 @@
         ],
         axis=0,
     )
-    far_send = jnp.concatenate([embeddings, vector_bf16], axis=0)
+    far_tail = jnp.concatenate([embeddings[FIRST:], vector_bf16], axis=0)
     own_list = jnp.concatenate(
         [block_pairs.reshape(-1), counts, jnp.zeros((128 - 2 * MAXP - 1,), jnp.int32)]
     )
     chip_lists = jnp.stack([own_list, swap(own_list, "k", K, 1)])
     lists = jnp.concatenate([chip_lists] + [shift(chip_lists, "y", Y, by) for by in (1, 2, 3)])
-    far_all = lax.all_gather(far_send, FAR)
+    far_first = lax.all_gather(embeddings[:FIRST], FAR)
+    far_rest = lax.all_to_all(
+        jnp.broadcast_to(far_tail[None], (WAYS,) + far_tail.shape), FAR, 0, 0
+    )
     ring = {0: near_send}
     for step in range(1, Z // 2 + 1):
-        ring[Z - step] = shift(ring[(Z - step + 1) % Z], "z", Z, 1)
+        ring[Z - step] = shift(ring[(Z - step + 1) % Z], ("u", "w"), Z, 1)
         if step < Z // 2:
-            ring[step] = shift(ring[step - 1], "z", Z, -1)
+            ring[step] = shift(ring[step - 1], ("u", "w"), Z, -1)
     near_blocks = [ring[i] for i in range(Z)]
     near_blocks += [swap(block, "k", K, 1) for block in near_blocks]
-    place = jnp.stack([lax.axis_index(name) for name in ("y", "k", "z")]).astype(jnp.int32)
+    place = jnp.stack([lax.axis_index(name) for name in ("y", "k", ("u", "w"))]).astype(jnp.int32)
     smem = pl.BlockSpec(memory_space=pltpu.SMEM)
     vmem = pl.BlockSpec(memory_space=pltpu.VMEM)
     picked = pl.pallas_call(
@@ -145,21 +177,22 @@
             jax.ShapeDtypeStruct((Z, AUG, BS), jnp.bfloat16),
             jax.ShapeDtypeStruct((WAYS, AUG, BS), jnp.bfloat16),
         ],
-        in_specs=[smem] + [pl.BlockSpec(memory_space=pl.ANY)] * (1 + WAYS),
+        in_specs=[smem] + [pl.BlockSpec(memory_space=pl.ANY)] * (2 + WAYS),
         out_specs=[vmem, vmem, vmem],
         scratch_shapes=[pltpu.VMEM((WAYS, EMB + VEC, BS), jnp.bfloat16)] * 2
         + [pltpu.VMEM((WAYS, AUG, BS), jnp.float32)] * 2
-        + [pltpu.SemaphoreType.DMA((WAYS + 1,))],
+        + [pltpu.SemaphoreType.DMA((WAYS + 2,))],
         compiler_params=pltpu.CompilerParams(vmem_limit_bytes=48 * 1024 * 1024),
         name="tiles",
-    )(picked, far_all, *near_blocks)
+    )(picked, far_first, far_rest, *near_blocks)
     far_back = lax.all_to_all(far_part, FAR, 0, 0)
     near_total = near_keep + swap(near_give, "k", K, 1).astype(jnp.float32)
-    for bit in (1, 2, 4):
-        left = near_total.shape[0] // 2
-        taken = swap(near_total[left:].astype(jnp.bfloat16), "z", Z, bit)
-        near_total = near_total[:left] + taken.astype(jnp.float32)
-    total = near_total[0] + jnp.sum(far_back.astype(jnp.float32), axis=0)
+    near_taken = swap(near_total[U:].astype(jnp.bfloat16), "w", W, 1)
+    near_total = (near_total[:U] + near_taken.astype(jnp.float32)).astype(jnp.bfloat16)
+    near_back = lax.all_to_all(near_total, "u", 0, 0)
+    total = jnp.sum(near_back.astype(jnp.float32), axis=0) + jnp.sum(
+        far_back.astype(jnp.float32), axis=0
+    )
     walked = total[:VEC] / total[VEC : VEC + 1]
     points = BS * X * K * Z * Y
     local_gram = jnp.dot(
@@ -170,18 +203,22 @@
         shares = lax.all_to_all(jnp.broadcast_to(partial_gram, (WAYS, 8, 128)), group, 0, 0)
         partial_gram = jnp.sum(shares, axis=0, keepdims=True)
     gram_matrix = partial_gram.reshape(VEC, VEC) / points
-    gram_factor = jnp.linalg.cholesky(gram_matrix)
-    inverse = lax.linalg.triangular_solve(
-        gram_factor, jnp.eye(VEC, dtype=jnp.float32), left_side=True, lower=True
-    )
-    embedding_basis = jnp.dot(
-        inverse, walked, precision=lax.Precision.HIGHEST, preferred_element_type=jnp.float32
-    )
+    embedding_basis, gram_factor = pl.pallas_call(
+        finish_kernel,
+        out_shape=[
+            jax.ShapeDtypeStruct((VEC, BS), jnp.float32),
+            jax.ShapeDtypeStruct((VEC, VEC), jnp.float32),
+        ],
+        in_specs=[vmem, vmem],
+        out_specs=[vmem, vmem],
+        scratch_shapes=[pltpu.VMEM((VEC, 128), jnp.float32)],
+        name="finish",
+    )(gram_matrix, walked)
     return (embedding_basis, gram_factor)
 
 
 def solution(mesh):
-    fine = Mesh(mesh.devices.reshape(X, K, Z, Y), EVERY)
+    fine = Mesh(mesh.devices.reshape(X, K, U, W, Y), EVERY)
     in_specs = (P(None, EVERY), P(None, EVERY), P(EVERY, None), P(EVERY))
     out_specs = (P(None, EVERY), P())
     return jax.shard_map(

time: 165 us -> 172 us (1.042)
  starting transfers between devices: 42.2 us -> 51.3 us
  Pallas kernels: 16.6 us -> 24.9 us
  other arithmetic: 11 us -> 2.73 us
  local copies, waits for them, and re-layouts: 4.19 us -> 9.81 us
  waiting for transfers between devices: 44.7 us -> 40.4 us
  blocking collectives: 28.6 us -> 25.5 us
    all_to_all x0 -> x2, starting transfers between devices: none -> 15.7 us  [the longest x1 8.8 us: on_device(): near_back = lax.all_to_all(near_total, 'u', 0, 0)]
    ppermute x13 -> x11, starting transfers between devices: 22.1 us -> 12.4 us  [swap(): return lax.ppermute(values, axis, [(i, i ^ bit) for i in range(size)])]
    ppermute x13 -> x11, waiting for transfers between devices: 14.1 us -> 5.29 us  [swap(): return lax.ppermute(values, axis, [(i, i ^ bit) for i in range(size)])]
    all_to_all x0 -> x2, waiting for transfers between devices: none -> 8 us  [the longest x1 8 us: on_device(): near_back = lax.all_to_all(near_total, 'u', 0, 0)]
    another operation x6 -> x1, other arithmetic: 7.88 us -> 0.58 us  [on_device(): jnp.stack([lax.axis_index(name) for name in ('y', 'k', ('u', 'w'))])]
    ppermute x10, waiting for transfers between devices: 20.4 us -> 15.7 us  [shift(): lax.ppermute(values, axis, [(i, (i + by) % size) for i in range(size)])]
    pallas_call x0 -> x1, Pallas kernels: none -> 4.57 us  [on_device(): pl.pallas_call(finish_kernel, out_shape=[jax.ShapeDtypeStruct((VEC, BS),...]
    pallas_call x1, Pallas kernels: 12.8 us -> 16.7 us  [on_device(): pl.pallas_call(tile_kernel, out_shape=[jax.ShapeDtypeStruct((Z, AUG, BS),...]
  transfers between devices with their start and end apart: 25 -> 25, of which waited for: 12 -> 9; matrix products, arithmetic and copies ran while one was open for 2% -> 3% of each run, Pallas kernels for 2% -> 2%
where the time goes in v4:
time: 172 us; the launch traced here: 170 us
  starting transfers between devices  51.3 us (30%)
  waiting for transfers between devices  40.4 us (23%)
  blocking collectives  25.5 us (15%)
  Pallas kernels  24.9 us (14%)
  between operations  14.9 us (9%)
  local copies, waits for them, and re-layouts  9.81 us (6%)
  other arithmetic  2.73 us (2%)
    all_to_all x2, blocking collectives, on_device(): lax.all_to_all(jnp.broadcast_to(partial_gram, (WAYS, 8, 128)), group, 0, 0)  25.5 us
    ppermute x10, starting transfers between devices, shift(): lax.ppermute(values, axis, [(i, (i + by) % size) for i in range(size)])  18 us
    pallas_call x1, Pallas kernels, on_device(): pl.pallas_call(tile_kernel, out_shape=[jax.ShapeDtypeStruct((Z, AUG, BS),...  16.7 us
    ppermute x10, waiting for transfers between devices, shift(): lax.ppermute(values, axis, [(i, (i + by) % size) for i in range(size)])  15.7 us
    ppermute x11, starting transfers between devices, swap(): return lax.ppermute(values, axis, [(i, i ^ bit) for i in range(size)])  12.4 us
    all_to_all x1, starting transfers between devices, on_device(): near_back = lax.all_to_all(near_total, 'u', 0, 0)  8.8 us
    all_to_all x1, waiting for transfers between devices, on_device(): near_back = lax.all_to_all(near_total, 'u', 0, 0)  8 us
    all_gather x1, waiting for transfers between devices, on_device(): far_first = lax.all_gather(embeddings[:FIRST], FAR)  7.73 us
  transfers between devices with their start and end apart: 25, of which 9 were waited for; matrix products, arithmetic and copies ran while one was open for 3% of the time, Pallas kernels for 2%

profile of v4, /device:TPU:1, one launch (start us, length us, event | category | flops | bytes accessed | tf_op | source)
XLA Modules:
  0.0 169.7 jit_solution(4642000147938763122)
XLA Ops:
  7.2 0.0 slice-start
  7.2 0.0 all-gather.3.cloned.1.call-start
  7.2 1.6 slice.25
  8.9 0.0 all-gather.3.cloned.1.call-update
  8.9 1.1 copy.11
  10.0 0.8 convert_element_type.19
  10.9 2.5 %collective-permute-start.7 = (bf16[288,512]{1,0:T(8,128)(2,1)S(1)}, bf16[288,512]{1,0:T(8,128)(2,1)S(1)}, u32[]{:S(2)}, u32[]{:S(2)}) collective-permute-start(bf16[288,512]{1,0:T(8,128)(2,1)S(1)} %pad_maximum_fusion.refs_0_), channel_id=1, source_target_pairs={{0,4},{4,8},{8,12},{12,16},{16,20},{20,24},{24,28},{28,0},{1,5},{5... | collective-permute-start | bytes 884744 | tf_op jit(solution)/shard_map/ppermute | solution.py:127
  13.5 1.4 broadcast_in_dim.11
  14.8 6.9 %all-to-all-start = ((bf16[16,96,512]{2,1,0:T(8,128)(2,1)}), bf16[16,96,512]{2,1,0:T(8,128)(2,1)}, u32[]{:S(2)}, u32[]{:S(2)}) async-start(bf16[16,96,512]{2,1,0:T(8,128)(2,1)} %broadcast_in_dim.11), calls=%async_computation | async-start | bytes 3145728 | tf_op jit(solution)/shard_map/all_to_all | solution.py:153
  21.8 4.0 %collective-permute-start.4 = (bf16[288,512]{1,0:T(8,128)(2,1)S(1)}, bf16[288,512]{1,0:T(8,128)(2,1)S(1)}, u32[]{:S(2)}, u32[]{:S(2)}) collective-permute-start(bf16[288,512]{1,0:T(8,128)(2,1)S(1)} %pad_maximum_fusion.refs_0_), channel_id=1, source_target_pairs={{0,28},{4,0},{8,4},{12,8},{16,12},{20,16},{24,20},{28,24},{1,29},{... | collective-permute-start | bytes 884744 | tf_op jit(solution)/shard_map/ppermute | solution.py:127
  25.8 0.0 collective-permute-done.7.refs_7_
  26.5 0.1 copy.10
  26.6 0.1 reshape.13
  26.7 4.5 %collective-permute-done.4.refs_1_ = bf16[288,512]{1,0:T(8,128)(2,1)S(1)} collective-permute-done((bf16[288,512]{1,0:T(8,128)(2,1)S(1)}, bf16[288,512]{1,0:T(8,128)(2,1)S(1)}, u32[]{:S(2)}, u32[]{:S(2)}) %collective-permute-start.4) | collective-permute-done | bytes 294944 | tf_op jit(solution)/shard_map/ppermute | solution.py:127
  31.2 3.5 %collective-permute-start.5 = (bf16[288,512]{1,0:T(8,128)(2,1)S(1)}, bf16[288,512]{1,0:T(8,128)(2,1)S(1)}, u32[]{:S(2)}, u32[]{:S(2)}) collective-permute-start(bf16[288,512]{1,0:T(8,128)(2,1)S(1)} %collective-permute-done.4.refs_1_), channel_id=1, source_target_pairs={{0,28},{4,0},{8,4},{12,8},{16,12},{20,16},{24,20},{28,24},{1,29},{... | collective-permute-start | bytes 884744 | tf_op jit(solution)/shard_map/ppermute | solution.py:127
  34.7 0.1 pad_add_fusion.2
  34.8 2.1 %collective-permute-start = (s32[128]{0:T(128)S(1)}, s32[128]{0:T(128)S(1)}, u32[]{:S(2)}, u32[]{:S(2)}) collective-permute-start(s32[128]{0:T(128)S(1)} %pad_add_fusion.2), channel_id=1, source_target_pairs={{0,32},{32,0},{1,33},{33,1},{2,34},{34,2},{3,35},{35,3},{4,36},{36... | collective-permute-start | bytes 1544 | tf_op jit(solution)/shard_map/ppermute | solution.py:131
  36.8 0.1 fusion.5
  36.9 0.7 collective-permute-done
  37.7 2.5 %collective-permute-start.3 = (s32[2,128]{1,0:T(2,128)S(1)}, s32[2,128]{1,0:T(2,128)S(1)}, u32[]{:S(2)}, u32[]{:S(2)}) collective-permute-start(s32[2,128]{1,0:T(2,128)S(1)} %pad_add_fusion), channel_id=1, source_target_pairs={{0,3},{1,0},{2,1},{3,2},{4,7},{5,4},{6,5},{7,6},{8,11},{9,8},{10,9... | collective-permute-start | bytes 3080 | tf_op jit(solution)/shard_map/ppermute | solution.py:127
  40.1 0.6 collective-permute-start.2
  40.7 0.6 collective-permute-start.1
  41.3 0.0 collective-permute-done.3
  41.3 1.9 %collective-permute-start.11 = (bf16[288,512]{1,0:T(8,128)(2,1)S(1)}, bf16[288,512]{1,0:T(8,128)(2,1)S(1)}, u32[]{:S(2)}, u32[]{:S(2)}) collective-permute-start(bf16[288,512]{1,0:T(8,128)(2,1)S(1)} %pad_maximum_fusion.refs_0_), channel_id=1, source_target_pairs={{0,32},{32,0},{1,33},{33,1},{2,34},{34,2},{3,35},{35,3},{4,36},{36... | collective-permute-start | bytes 884744 | tf_op jit(solution)/shard_map/ppermute | solution.py:131
  43.2 5.5 %collective-permute-done.2 = s32[2,128]{1,0:T(2,128)S(1)} collective-permute-done((s32[2,128]{1,0:T(2,128)S(1)}, s32[2,128]{1,0:T(2,128)S(1)}, u32[]{:S(2)}, u32[]{:S(2)}) %collective-permute-start.2) | collective-permute-done | bytes 1056 | tf_op jit(solution)/shard_map/ppermute | solution.py:127
  48.7 0.4 collective-permute-start.18
  49.1 0.1 collective-permute-start.12
  49.2 4.2 %collective-permute-start.6 = (bf16[288,512]{1,0:T(8,128)(2,1)S(1)}, bf16[288,512]{1,0:T(8,128)(2,1)S(1)}, u32[]{:S(2)}, u32[]{:S(2)}) collective-permute-start(bf16[288,512]{1,0:T(8,128)(2,1)S(1)} %collective-permute-done.5.refs_2_), channel_id=1, source_target_pairs={{0,28},{4,0},{8,4},{12,8},{16,12},{20,16},{24,20},{28,24},{1,29},{... | collective-permute-start | bytes 884744 | tf_op jit(solution)/shard_map/ppermute | solution.py:127
  53.4 0.0 collective-permute-done.9.refs_5_
  53.5 0.8 collective-permute-start.17
  54.2 0.0 collective-permute-done.18.refs_15_
  54.2 0.1 collective-permute-start.13
  54.4 0.4 collective-permute-start.16
  54.8 4.6 %collective-permute-done.6.refs_3_ = bf16[288,512]{1,0:T(8,128)(2,1)S(1)} collective-permute-done((bf16[288,512]{1,0:T(8,128)(2,1)S(1)}, bf16[288,512]{1,0:T(8,128)(2,1)S(1)}, u32[]{:S(2)}, u32[]{:S(2)}) %collective-permute-start.6) | collective-permute-done | bytes 294944 | tf_op jit(solution)/shard_map/ppermute | solution.py:127
  59.4 1.3 collective-permute-start.14
  60.7 0.8 copy-done
  61.4 1.1 collective-permute-done.10.refs_4_
  62.5 1.6 collective-permute-start.15
  64.1 0.8 copy-done.2
  64.8 0.6 pad_add_fusion.1.place_ref
  65.4 0.6 concatenate.17.lists_ref
  66.0 3.5 %select_pairs.1.picked_ref = s32[256]{0:T(256)} custom-call(s32[3]{0:T(128)} %pad_add_fusion.1.place_ref, s32[8,128]{1,0:T(8,128)} %concatenate.17.lists_ref), custom_call_target="tpu_custom_call" | custom-call | tf_op jit(solution)/shard_map/select_pairs/pallas_call | solution.py:166
  69.6 0.0 collective-permute-done.17.refs_14_
  69.6 7.7 %all-gather.3.cloned.1.call-done = bf16[3072,512]{1,0:T(8,128)(2,1)} async-done(((bf16[192,512]{1,0:T(8,128)(2,1)}), bf16[3072,512]{1,0:T(8,128)(2,1)}) %all-gather.3.cloned.1.call-update) | async-done | bytes 3145744 | tf_op jit(solution)/shard_map/all_gather | solution.py:152
  77.4 1.0 copy-done.1
  78.3 1.0 copy-done.3
  79.3 0.7 copy-done.4
  80.0 16.7 %tiles.1 = (f32[8,48,512]{2,1,0:T(8,128)S(1)}, bf16[8,48,512]{2,1,0:T(8,128)(2,1)}, bf16[16,48,512]{2,1,0:T(8,128)(2,1)}) custom-call(s32[256]{0:T(256)S(1)} %copy-done.4, bf16[16,192,512]{2,1,0:T(8,128)(2,1)} %bitcast.11, bf16[16,96,512]{2,1,0:T(8,128)(2,1)} %all-to-all-done.far_rest, bf16[288,512]{1,0:T(8,128)(2,1)S(1)} %pad_maximum_fusion.refs_0_, ...), custom_call_target="tpu_custom_call" | custom-call | tf_op jit(solution)/shard_map/tiles/pallas_call | solution.py:173
  96.7 0.1 collective-permute-start.19
  96.8 5.2 %all-to-all-start.2 = ((bf16[16,48,512]{2,1,0:T(8,128)(2,1)}), bf16[16,48,512]{2,1,0:T(8,128)(2,1)S(1)}, u32[]{:S(2)}, u32[]{:S(2)}) async-start(bf16[16,48,512]{2,1,0:T(8,128)(2,1)} %get-tuple-element.7), calls=%async_computation.2 | async-start | bytes 1572864 | tf_op jit(solution)/shard_map/all_to_all | solution.py:188
  102.0 0.1 convert_add_fusion
  102.2 3.6 %collective-permute-start.20 = (bf16[4,48,512]{2,1,0:T(8,128)(2,1)S(1)}, bf16[4,48,512]{2,1,0:T(8,128)(2,1)S(1)}, u32[]{:S(2)}, u32[]{:S(2)}) collective-permute-start(bf16[4,48,512]{2,1,0:T(8,128)(2,1)S(1)} %slice.44), channel_id=1, source_target_pairs={{0,4},{4,0},{1,5},{5,1},{2,6},{6,2},{3,7},{7,3},{8,12},{12,8},{9,1... | collective-permute-start | bytes 589832 | tf_op jit(solution)/shard_map/ppermute | solution.py:131
  105.8 4.5 %collective-permute-done.20 = bf16[4,48,512]{2,1,0:T(8,128)(2,1)S(1)} collective-permute-done((bf16[4,48,512]{2,1,0:T(8,128)(2,1)S(1)}, bf16[4,48,512]{2,1,0:T(8,128)(2,1)S(1)}, u32[]{:S(2)}, u32[]{:S(2)}) %collective-permute-start.20) | collective-permute-done | bytes 196640 | tf_op jit(solution)/shard_map/ppermute | solution.py:131
  110.3 0.7 fusion
  111.1 3.7 %all-to-all-done.2 = bf16[16,48,512]{2,1,0:T(8,128)(2,1)S(1)} async-done(((bf16[16,48,512]{2,1,0:T(8,128)(2,1)}), bf16[16,48,512]{2,1,0:T(8,128)(2,1)S(1)}, u32[]{:S(2)}, u32[]{:S(2)}) %all-to-all-start.2) | async-done | bytes 786464 | tf_op jit(solution)/shard_map/all_to_all | solution.py:188
  114.8 8.8 %all-to-all-start.1 = ((bf16[4,48,512]{2,1,0:T(8,128)(2,1)}), bf16[4,48,512]{2,1,0:T(8,128)(2,1)S(1)}, u32[]{:S(2)}, u32[]{:S(2)}) async-start(bf16[4,48,512]{2,1,0:T(8,128)(2,1)} %fusion), calls=%async_computation.1 | async-start | bytes 393216 | tf_op jit(solution)/shard_map/all_to_all | solution.py:192
  123.6 0.1 convert_reduce_fusion
  123.7 8.0 %all-to-all-done.1 = bf16[4,48,512]{2,1,0:T(8,128)(2,1)S(1)} async-done(((bf16[4,48,512]{2,1,0:T(8,128)(2,1)}), bf16[4,48,512]{2,1,0:T(8,128)(2,1)S(1)}, u32[]{:S(2)}, u32[]{:S(2)}) %all-to-all-start.1) | async-done | bytes 196640 | tf_op jit(solution)/shard_map/all_to_all | solution.py:192
  131.8 0.2 fusion.2
  132.0 0.1 broadcast_in_dim.24
  132.0 10.6 %all_to_all.25 = f32[16,8,128]{2,1,0:T(8,128)S(1)} all-to-all(f32[16,8,128]{2,1,0:T(8,128)S(1)} %broadcast_in_dim.25), channel_id=1, replica_groups=mesh['x'=4,'k'=2,'u'=4,'w'=2,'y'=4] {'x','y'}, dimensions={0} | all-to-all | bytes 131072 | tf_op jit(solution)/shard_map/all_to_all | solution.py:203
  142.7 14.9 %all_to_all.26 = f32[16,8,128]{2,1,0:T(8,128)S(1)} all-to-all(f32[16,8,128]{2,1,0:T(8,128)S(1)} %broadcast_in_dim.26), channel_id=1, replica_groups=mesh['x'=4,'k'=2,'u'=4,'w'=2,'y'=4] {'k','u','w'}, dimensions={0} | all-to-all | bytes 131072 | tf_op jit(solution)/shard_map/all_to_all | solution.py:203
  157.6 0.7 div.23.gram_ref
  158.3 4.6 %finish.1 = (f32[32,512]{1,0:T(8,128)}, f32[32,32]{1,0:T(8,128)}) custom-call(f32[32,32]{1,0:T(8,128)} %div.23.gram_ref, f32[32,512]{1,0:T(8,128)} %copy-done.5), custom_call_target="tpu_custom_call" | custom-call | tf_op jit(solution)/shard_map/finish/pallas_call | solution.py:206
  (40 shorter events, 0.3 us)
Async XLA Ops:
  7.2 6.3 %slice-start = ((bf16[256,512]{1,0:T(8,128)(2,1)}), bf16[64,512]{1,0:T(8,128)(2,1)S(1)}, s32[]{:S(2)}) async-start(bf16[256,512]{1,0:T(8,128)(2,1)} %param.4), calls=%async_computation.6 | async-start | bytes 131072 | tf_op jit(solution)/shard_map/slice | solution.py:146
  7.2 70.2 %all-gather.3.cloned.1.call-start = ((), (), s32[]{:S(2)}) async-start(), calls=%async_computation.5 | async-start | bytes 3342336 | tf_op jit(solution)/shard_map/all_gather | solution.py:152
  10.9 14.9 %collective-permute-start.7 = (bf16[288,512]{1,0:T(8,128)(2,1)S(1)}, bf16[288,512]{1,0:T(8,128)(2,1)S(1)}, u32[]{:S(2)}, u32[]{:S(2)}) collective-permute-start(bf16[288,512]{1,0:T(8,128)(2,1)S(1)} %pad_maximum_fusion.refs_0_), channel_id=1, source_target_pairs={{0,4},{4,8},{8,12},{12,16},{16,20},{20,24},{24,28},{28,0},{1,5},{5... | collective-permute-start | bytes 884744 | tf_op jit(solution)/shard_map/ppermute | solution.py:127
  14.8 11.6 %copy-start.6 = (s32[24,2]{0,1:T(2,128)S(1)}, s32[24,2]{0,1:T(2,128)}, u32[]{:S(2)}) copy-start(s32[24,2]{0,1:T(2,128)} %param.6) | copy-start | bytes 580
  14.8 54.8 %all-to-all-start = ((bf16[16,96,512]{2,1,0:T(8,128)(2,1)}), bf16[16,96,512]{2,1,0:T(8,128)(2,1)}, u32[]{:S(2)}, u32[]{:S(2)}) async-start(bf16[16,96,512]{2,1,0:T(8,128)(2,1)} %broadcast_in_dim.11), calls=%async_computation | async-start | bytes 3145728 | tf_op jit(solution)/shard_map/all_to_all | solution.py:153
  21.8 9.4 %collective-permute-start.4 = (bf16[288,512]{1,0:T(8,128)(2,1)S(1)}, bf16[288,512]{1,0:T(8,128)(2,1)S(1)}, u32[]{:S(2)}, u32[]{:S(2)}) collective-permute-start(bf16[288,512]{1,0:T(8,128)(2,1)S(1)} %pad_maximum_fusion.refs_0_), channel_id=1, source_target_pairs={{0,28},{4,0},{8,4},{12,8},{16,12},{20,16},{24,20},{28,24},{1,29},{... | collective-permute-start | bytes 884744 | tf_op jit(solution)/shard_map/ppermute | solution.py:127
  25.8 8.9 %collective-permute-start.8 = (bf16[288,512]{1,0:T(8,128)(2,1)S(1)}, bf16[288,512]{1,0:T(8,128)(2,1)S(1)}, u32[]{:S(2)}, u32[]{:S(2)}) collective-permute-start(bf16[288,512]{1,0:T(8,128)(2,1)S(1)} %collective-permute-done.7.refs_7_), channel_id=1, source_target_pairs={{0,4},{4,8},{8,12},{12,16},{16,20},{20,24},{24,28},{28,0},{1,5},{5... | collective-permute-start | bytes 884744 | tf_op jit(solution)/shard_map/ppermute | solution.py:127
  31.2 18.0 %collective-permute-start.5 = (bf16[288,512]{1,0:T(8,128)(2,1)S(1)}, bf16[288,512]{1,0:T(8,128)(2,1)S(1)}, u32[]{:S(2)}, u32[]{:S(2)}) collective-permute-start(bf16[288,512]{1,0:T(8,128)(2,1)S(1)} %collective-permute-done.4.refs_1_), channel_id=1, source_target_pairs={{0,28},{4,0},{8,4},{12,8},{16,12},{20,16},{24,20},{28,24},{1,29},{... | collective-permute-start | bytes 884744 | tf_op jit(solution)/shard_map/ppermute | solution.py:127
  34.7 18.7 %collective-permute-start.9 = (bf16[288,512]{1,0:T(8,128)(2,1)S(1)}, bf16[288,512]{1,0:T(8,128)(2,1)S(1)}, u32[]{:S(2)}, u32[]{:S(2)}) collective-permute-start(bf16[288,512]{1,0:T(8,128)(2,1)S(1)} %collective-permute-done.8.refs_6_), channel_id=1, source_target_pairs={{0,4},{4,8},{8,12},{12,16},{16,20},{20,24},{24,28},{28,0},{1,5},{5... | collective-permute-start | bytes 884744 | tf_op jit(solution)/shard_map/ppermute | solution.py:127
  34.8 2.9 %collective-permute-start = (s32[128]{0:T(128)S(1)}, s32[128]{0:T(128)S(1)}, u32[]{:S(2)}, u32[]{:S(2)}) collective-permute-start(s32[128]{0:T(128)S(1)} %pad_add_fusion.2), channel_id=1, source_target_pairs={{0,32},{32,0},{1,33},{33,1},{2,34},{34,2},{3,35},{35,3},{4,36},{36... | collective-permute-start | bytes 1544 | tf_op jit(solution)/shard_map/ppermute | solution.py:131
  37.7 3.6 %collective-permute-start.3 = (s32[2,128]{1,0:T(2,128)S(1)}, s32[2,128]{1,0:T(2,128)S(1)}, u32[]{:S(2)}, u32[]{:S(2)}) collective-permute-start(s32[2,128]{1,0:T(2,128)S(1)} %pad_add_fusion), channel_id=1, source_target_pairs={{0,3},{1,0},{2,1},{3,2},{4,7},{5,4},{6,5},{7,6},{8,11},{9,8},{10,9... | collective-permute-start | bytes 3080 | tf_op jit(solution)/shard_map/ppermute | solution.py:127
  40.1 8.5 %collective-permute-start.2 = (s32[2,128]{1,0:T(2,128)S(1)}, s32[2,128]{1,0:T(2,128)S(1)}, u32[]{:S(2)}, u32[]{:S(2)}) collective-permute-start(s32[2,128]{1,0:T(2,128)S(1)} %pad_add_fusion), channel_id=1, source_target_pairs={{0,2},{1,3},{2,0},{3,1},{4,6},{5,7},{6,4},{7,5},{8,10},{9,11},{10,... | collective-permute-start | bytes 3080 | tf_op jit(solution)/shard_map/ppermute | solution.py:127
  40.7 8.4 %collective-permute-start.1 = (s32[2,128]{1,0:T(2,128)S(1)}, s32[2,128]{1,0:T(2,128)S(1)}, u32[]{:S(2)}, u32[]{:S(2)}) collective-permute-start(s32[2,128]{1,0:T(2,128)S(1)} %pad_add_fusion), channel_id=1, source_target_pairs={{0,1},{1,2},{2,3},{3,0},{4,5},{5,6},{6,7},{7,4},{8,9},{9,10},{10,1... | collective-permute-start | bytes 3080 | tf_op jit(solution)/shard_map/ppermute | solution.py:127
  41.3 12.2 %collective-permute-start.11 = (bf16[288,512]{1,0:T(8,128)(2,1)S(1)}, bf16[288,512]{1,0:T(8,128)(2,1)S(1)}, u32[]{:S(2)}, u32[]{:S(2)}) collective-permute-start(bf16[288,512]{1,0:T(8,128)(2,1)S(1)} %pad_maximum_fusion.refs_0_), channel_id=1, source_target_pairs={{0,32},{32,0},{1,33},{33,1},{2,34},{34,2},{3,35},{35,3},{4,36},{36... | collective-permute-start | bytes 884744 | tf_op jit(solution)/shard_map/ppermute | solution.py:131
  48.7 5.6 %collective-permute-start.18 = (bf16[288,512]{1,0:T(8,128)(2,1)S(1)}, bf16[288,512]{1,0:T(8,128)(2,1)S(1)}, u32[]{:S(2)}, u32[]{:S(2)}) collective-permute-start(bf16[288,512]{1,0:T(8,128)(2,1)S(1)} %collective-permute-done.7.refs_7_), channel_id=1, source_target_pairs={{0,32},{32,0},{1,33},{33,1},{2,34},{34,2},{3,35},{35,3},{4,36},{36... | collective-permute-start | bytes 884744 | tf_op jit(solution)/shard_map/ppermute | solution.py:131
  49.1 5.3 %collective-permute-start.12 = (bf16[288,512]{1,0:T(8,128)(2,1)S(1)}, bf16[288,512]{1,0:T(8,128)(2,1)S(1)}, u32[]{:S(2)}, u32[]{:S(2)}) collective-permute-start(bf16[288,512]{1,0:T(8,128)(2,1)S(1)} %collective-permute-done.4.refs_1_), channel_id=1, source_target_pairs={{0,32},{32,0},{1,33},{33,1},{2,34},{34,2},{3,35},{35,3},{4,36},{36... | collective-permute-start | bytes 884744 | tf_op jit(solution)/shard_map/ppermute | solution.py:131
  49.2 10.2 %collective-permute-start.6 = (bf16[288,512]{1,0:T(8,128)(2,1)S(1)}, bf16[288,512]{1,0:T(8,128)(2,1)S(1)}, u32[]{:S(2)}, u32[]{:S(2)}) collective-permute-start(bf16[288,512]{1,0:T(8,128)(2,1)S(1)} %collective-permute-done.5.refs_2_), channel_id=1, source_target_pairs={{0,28},{4,0},{8,4},{12,8},{16,12},{20,16},{24,20},{28,24},{1,29},{... | collective-permute-start | bytes 884744 | tf_op jit(solution)/shard_map/ppermute | solution.py:127
  53.4 9.0 %collective-permute-start.10 = (bf16[288,512]{1,0:T(8,128)(2,1)S(1)}, bf16[288,512]{1,0:T(8,128)(2,1)S(1)}, u32[]{:S(2)}, u32[]{:S(2)}) collective-permute-start(bf16[288,512]{1,0:T(8,128)(2,1)S(1)} %collective-permute-done.9.refs_5_), channel_id=1, source_target_pairs={{0,4},{4,8},{8,12},{12,16},{16,20},{20,24},{24,28},{28,0},{1,5},{5... | collective-permute-start | bytes 884744 | tf_op jit(solution)/shard_map/ppermute | solution.py:127
  53.5 16.1 %collective-permute-start.17 = (bf16[288,512]{1,0:T(8,128)(2,1)S(1)}, bf16[288,512]{1,0:T(8,128)(2,1)}, u32[]{:S(2)}, u32[]{:S(2)}) collective-permute-start(bf16[288,512]{1,0:T(8,128)(2,1)S(1)} %collective-permute-done.8.refs_6_), channel_id=1, source_target_pairs={{0,32},{32,0},{1,33},{33,1},{2,34},{34,2},{3,35},{35,3},{4,36},{36... | collective-permute-start | bytes 884744 | tf_op jit(solution)/shard_map/ppermute | solution.py:131
  54.2 15.3 %collective-permute-start.13 = (bf16[288,512]{1,0:T(8,128)(2,1)S(1)}, bf16[288,512]{1,0:T(8,128)(2,1)}, u32[]{:S(2)}, u32[]{:S(2)}) collective-permute-start(bf16[288,512]{1,0:T(8,128)(2,1)S(1)} %collective-permute-done.5.refs_2_), channel_id=1, source_target_pairs={{0,32},{32,0},{1,33},{33,1},{2,34},{34,2},{3,35},{35,3},{4,36},{36... | collective-permute-start | bytes 884744 | tf_op jit(solution)/shard_map/ppermute | solution.py:131
  54.4 15.2 %collective-permute-start.16 = (bf16[288,512]{1,0:T(8,128)(2,1)S(1)}, bf16[288,512]{1,0:T(8,128)(2,1)}, u32[]{:S(2)}, u32[]{:S(2)}) collective-permute-start(bf16[288,512]{1,0:T(8,128)(2,1)S(1)} %collective-permute-done.9.refs_5_), channel_id=1, source_target_pairs={{0,32},{32,0},{1,33},{33,1},{2,34},{34,2},{3,35},{35,3},{4,36},{36... | collective-permute-start | bytes 884744 | tf_op jit(solution)/shard_map/ppermute | solution.py:131
  59.4 10.2 %collective-permute-start.14 = (bf16[288,512]{1,0:T(8,128)(2,1)S(1)}, bf16[288,512]{1,0:T(8,128)(2,1)}, u32[]{:S(2)}, u32[]{:S(2)}) collective-permute-start(bf16[288,512]{1,0:T(8,128)(2,1)S(1)} %collective-permute-done.6.refs_3_), channel_id=1, source_target_pairs={{0,32},{32,0},{1,33},{33,1},{2,34},{34,2},{3,35},{35,3},{4,36},{36... | collective-permute-start | bytes 884744 | tf_op jit(solution)/shard_map/ppermute | solution.py:131
  60.7 0.8 copy-start
  62.5 7.1 %collective-permute-start.15 = (bf16[288,512]{1,0:T(8,128)(2,1)S(1)}, bf16[288,512]{1,0:T(8,128)(2,1)}, u32[]{:S(2)}, u32[]{:S(2)}) collective-permute-start(bf16[288,512]{1,0:T(8,128)(2,1)S(1)} %collective-permute-done.10.refs_4_), channel_id=1, source_target_pairs={{0,32},{32,0},{1,33},{33,1},{2,34},{34,2},{3,35},{35,3},{4,36},{36... | collective-permute-start | bytes 884744 | tf_op jit(solution)/shard_map/ppermute | solution.py:131
  64.1 0.8 copy-start.2
  77.3 1.0 copy-start.1
  78.3 1.0 copy-start.3
  79.3 0.7 copy-start.4
  96.7 5.3 %collective-permute-start.19 = (bf16[8,48,512]{2,1,0:T(8,128)(2,1)}, bf16[8,48,512]{2,1,0:T(8,128)(2,1)S(1)}, u32[]{:S(2)}, u32[]{:S(2)}) collective-permute-start(bf16[8,48,512]{2,1,0:T(8,128)(2,1)} %get-tuple-element.6), channel_id=1, source_target_pairs={{0,32},{32,0},{1,33},{33,1},{2,34},{34,2},{3,35},{35,3},{4,36},{36... | collective-permute-start | bytes 1179656 | tf_op jit(solution)/shard_map/ppermute | solution.py:131
  96.8 17.9 %all-to-all-start.2 = ((bf16[16,48,512]{2,1,0:T(8,128)(2,1)}), bf16[16,48,512]{2,1,0:T(8,128)(2,1)S(1)}, u32[]{:S(2)}, u32[]{:S(2)}) async-start(bf16[16,48,512]{2,1,0:T(8,128)(2,1)} %get-tuple-element.7), calls=%async_computation.2 | async-start | bytes 1572864 | tf_op jit(solution)/shard_map/all_to_all | solution.py:188
  102.2 8.1 %collective-permute-start.20 = (bf16[4,48,512]{2,1,0:T(8,128)(2,1)S(1)}, bf16[4,48,512]{2,1,0:T(8,128)(2,1)S(1)}, u32[]{:S(2)}, u32[]{:S(2)}) collective-permute-start(bf16[4,48,512]{2,1,0:T(8,128)(2,1)S(1)} %slice.44), channel_id=1, source_target_pairs={{0,4},{4,0},{1,5},{5,1},{2,6},{6,2},{3,7},{7,3},{8,12},{12,8},{9,1... | collective-permute-start | bytes 589832 | tf_op jit(solution)/shard_map/ppermute | solution.py:131
  114.8 16.9 %all-to-all-start.1 = ((bf16[4,48,512]{2,1,0:T(8,128)(2,1)}), bf16[4,48,512]{2,1,0:T(8,128)(2,1)S(1)}, u32[]{:S(2)}, u32[]{:S(2)}) async-start(bf16[4,48,512]{2,1,0:T(8,128)(2,1)} %fusion), calls=%async_computation.1 | async-start | bytes 393216 | tf_op jit(solution)/shard_map/all_to_all | solution.py:192
  131.8 26.5 %copy-start.5 = (f32[32,512]{1,0:T(8,128)}, f32[32,512]{1,0:T(8,128)S(1)}, u32[]{:S(2)}) copy-start(f32[32,512]{1,0:T(8,128)S(1)} %slice_divide_fusion.walked_ref) | copy-start | bytes 196612
Sparse Core Ops, SparseCore 0:
  10.5 66.8 all-gather.2

commit v5 on v4

v5 whole, which is shorter than its diff:
```python
import functools
import math

import jax
import jax.numpy as jnp
from jax import lax
from jax.experimental import pallas as pl
from jax.experimental.pallas import tpu as pltpu
from jax.sharding import Mesh
from jax.sharding import PartitionSpec as P

X, K, Z, Y = 4, 2, 8, 4
FAR = ("x", "k", "y")
EVERY = ("x", "k", "z", "y")
FARS = X * K * Y
BS = 512
EMB = 256
VEC = 32
AUG = 48
MAXP = 24
SLOTS = 128


def select_kernel(place_ref, lists_ref, picked_ref):
    own_y = place_ref[0]
    own_k = place_ref[1]
    own_z = place_ref[2]

    def each_list(which, found):
        def each_slot(slot, found):
            row_block = lists_ref[which, 2 * slot]
            col_block = lists_ref[which, 2 * slot + 1]
            row_z = (row_block >> 2) & 7
            near = (row_z - own_z) & 7
            apart = row_z ^ own_z
            back = (apart & 1) * 4 + (apart & 2) + (apart >> 2)
            col_row = col_block >> 5
            far = col_row * Y + (col_block & 3)
            home = ((col_row & 1) ^ own_k) * (X * Y) + (col_row >> 1) * Y + (col_block & 3)
            same = (row_block == col_block).astype(jnp.int32)
            picked_ref[found + 1] = (((same * 8 + back) * 8 + near) * FARS + home) * FARS + far
            return found + ((row_block & 3) == own_y).astype(jnp.int32)

        return lax.fori_loop(0, lists_ref[which, 2 * MAXP], each_slot, found)

    picked_ref[0] = lax.fori_loop(0, Y, each_list, jnp.int32(0))


def tile_kernel(picked_ref, far_hbm, *refs):
    near_hbm = refs[:Z]
    near_keep, near_give, far_keep, far_give, near_ref, far_ref, near_sum, far_sum, sems = refs[Z:]
    copies = [pltpu.make_async_copy(far_hbm, far_ref, sems.at[Z])]
    for slot in range(Z):
        copies.append(pltpu.make_async_copy(near_hbm[slot], near_ref.at[slot], sems.at[slot]))
    for copy in copies:
        copy.start()
    near_sum[...] = jnp.zeros_like(near_sum)
    far_sum[...] = jnp.zeros_like(far_sum)
    ones = (lax.broadcasted_iota(jnp.int32, (AUG - VEC, BS), 0) == 0).astype(jnp.bfloat16)
    for copy in copies:
        copy.wait()

    def each_tile(number, carry):
        code = picked_ref[number + 1]
        far = code & 31
        home = (code >> 5) & 31
        near = (code >> 10) & 7
        back = (code >> 13) & 7
        mirror = jnp.where((code >> 16) == 1, 0.0, 1.0).astype(jnp.float32)
        far_embed = far_ref[far, :EMB, :]
        near_vec = jnp.concatenate([near_ref[near, EMB:, :], ones], axis=0)
        far_vec = jnp.concatenate([far_ref[far, EMB:, :], ones], axis=0)
        far_terms = None
        for half in range(2):
            cut = slice(half * 256, half * 256 + 256)
            scores = jnp.dot(
                near_ref[near, :EMB, cut], far_embed, preferred_element_type=jnp.float32
            )
            tile = (0.5 * jnp.tanh(scores) + 0.5).astype(jnp.bfloat16)
            near_terms = lax.dot_general(
                far_vec, tile, (((1,), (1,)), ((), ())), preferred_element_type=jnp.float32
            )
            near_sum[back, :, cut] += near_terms
            part = jnp.dot(near_vec[:, cut], tile, preferred_element_type=jnp.float32)
            far_terms = part if far_terms is None else far_terms + part
        far_sum[home] += far_terms * mirror
        return carry

    lax.fori_loop(0, picked_ref[0], each_tile, 0)
    near_keep[...] = near_sum[: Z // 2]
    near_give[...] = near_sum[Z // 2 :].astype(jnp.bfloat16)
    far_keep[...] = far_sum[: X * Y]
    far_give[...] = far_sum[X * Y :].astype(jnp.bfloat16)


def finish_kernel(gram_ref, walked_ref, basis_out, factor_out, wide_ref):
    row = lax.broadcasted_iota(jnp.int32, (VEC, 128), 0)
    lane = lax.broadcasted_iota(jnp.int32, (VEC, 128), 1)
    wide_ref[...] = (lane == row + VEC).astype(jnp.float32)
    wide_ref[:, :VEC] = gram_ref[...]
    wide = wide_ref[...]
    factor = jnp.zeros((VEC, 128), jnp.float32)
    for step in range(VEC):
        pivot = wide[step : step + 1, step : step + 1]
        root = lax.rsqrt(pivot)
        root = root * (1.5 - 0.5 * pivot * root * root)
        scaled = wide[step : step + 1, :] * root
        column = jnp.broadcast_to(wide[:, step : step + 1] * root, (VEC, 128))
        factor = jnp.where((lane == step) & (row >= step), column, factor)
        lower = jnp.where(row > step, wide - column * scaled, wide)
        wide = jnp.where(row == step, jnp.broadcast_to(scaled, (VEC, 128)), lower)
    wide_ref[...] = wide
    basis_out[...] = jnp.dot(
        wide_ref[:, VEC : 2 * VEC],
        walked_ref[...],
        precision=lax.Precision.HIGHEST,
        preferred_element_type=jnp.float32,
    )
    factor_out[...] = factor[:, :VEC]


def shift(values, axis, size, by):
    return lax.ppermute(values, axis, [(i, (i + by) % size) for i in range(size)])


def swap(values, axis, size, bit):
    return lax.ppermute(values, axis, [(i, i ^ bit) for i in range(size)])


def on_device(embeddings, vectors, block_pairs, counts):
    score_scale = 0.5 / math.sqrt(EMB)
    vector_bf16 = vectors.astype(jnp.bfloat16)
    far_send = lax.optimization_barrier(jnp.concatenate([embeddings, vector_bf16], axis=0))
    far_all = lax.all_gather(far_send, FAR)
    turned = embeddings.T
    near_send = jnp.concatenate(
        [
            jnp.concatenate([turned[:256], turned[256:]], axis=1)
            * jnp.asarray(score_scale, jnp.bfloat16),
            vector_bf16,
        ],
        axis=0,
    )
    ring = {0: near_send}
    for step in range(1, Z // 2 + 1):
        ring[Z - step] = shift(ring[(Z - step + 1) % Z], "z", Z, 1)
        if step < Z // 2:
            ring[step] = shift(ring[step - 1], "z", Z, -1)
    near_blocks = [ring[i] for i in range(Z)]
    own_list = jnp.concatenate(
        [block_pairs.reshape(-1), counts, jnp.zeros((128 - 2 * MAXP - 1,), jnp.int32)]
    )
    lists = jnp.stack([own_list] + [shift(own_list, "y", Y, by) for by in (1, 2, 3)])
    place = jnp.stack([lax.axis_index(name) for name in ("y", "k", "z")]).astype(jnp.int32)
    smem = pl.BlockSpec(memory_space=pltpu.SMEM)
    vmem = pl.BlockSpec(memory_space=pltpu.VMEM)
    picked = pl.pallas_call(
        select_kernel,
        out_shape=jax.ShapeDtypeStruct((SLOTS,), jnp.int32),
        in_specs=[smem, smem],
        out_specs=smem,
        name="select_pairs",
    )(place, lists)
    near_total, near_give, far_total, far_give = pl.pallas_call(
        tile_kernel,
        out_shape=[
            jax.ShapeDtypeStruct((Z // 2, AUG, BS), jnp.float32),
            jax.ShapeDtypeStruct((Z // 2, AUG, BS), jnp.bfloat16),
            jax.ShapeDtypeStruct((X * Y, AUG, BS), jnp.float32),
            jax.ShapeDtypeStruct((X * Y, AUG, BS), jnp.bfloat16),
        ],
        in_specs=[smem] + [pl.BlockSpec(memory_space=pl.ANY)] * (1 + Z),
        out_specs=[vmem] * 4,
        scratch_shapes=[
            pltpu.VMEM((Z, EMB + VEC, BS), jnp.bfloat16),
            pltpu.VMEM((FARS, EMB + VEC, BS), jnp.bfloat16),
            pltpu.VMEM((Z, AUG, BS), jnp.float32),
            pltpu.VMEM((FARS, AUG, BS), jnp.float32),
            pltpu.SemaphoreType.DMA((Z + 1,)),
        ],
        compiler_params=pltpu.CompilerParams(vmem_limit_bytes=48 * 1024 * 1024),
        name="tiles",
    )(picked, far_all, *near_blocks)
    far_taken = swap(far_give, "k", K, 1)
    far_pair = (far_total + far_taken.astype(jnp.float32)).astype(jnp.bfloat16)
    far_back = lax.all_to_all(far_pair, ("x", "y"), 0, 0)
    for bit in (1, 2, 4):
        left = near_total.shape[0] if bit == 1 else near_total.shape[0] // 2
        give = near_give if bit == 1 else near_total[left:].astype(jnp.bfloat16)
        near_total = near_total[:left] + swap(give, "z", Z, bit).astype(jnp.float32)
    total = near_total[0] + jnp.sum(far_back.astype(jnp.float32), axis=0)
    walked = total[:VEC] / total[VEC : VEC + 1]
    points = BS * X * K * Z * Y
    local_gram = jnp.dot(
        walked, walked.T, precision=lax.Precision.HIGHEST, preferred_element_type=jnp.float32
    )
    partial_gram = local_gram.reshape(1, 8, 128)
    for group in (("x", "y"), ("k", "z")):
        shares = lax.all_to_all(jnp.broadcast_to(partial_gram, (16, 8, 128)), group, 0, 0)
        partial_gram = jnp.sum(shares, axis=0, keepdims=True)
    gram_matrix = partial_gram.reshape(VEC, VEC) / points
    embedding_basis, gram_factor = pl.pallas_call(
        finish_kernel,
        out_shape=[
            jax.ShapeDtypeStruct((VEC, BS), jnp.float32),
            jax.ShapeDtypeStruct((VEC, VEC), jnp.float32),
        ],
        in_specs=[vmem, vmem],
        out_specs=[vmem, vmem],
        scratch_shapes=[pltpu.VMEM((VEC, 128), jnp.float32)],
        name="finish",
    )(gram_matrix, walked)
    return (embedding_basis, gram_factor)


def solution(mesh):
    fine = Mesh(mesh.devices.reshape(X, K, Z, Y), EVERY)
    in_specs = (P(None, EVERY), P(None, EVERY), P(EVERY, None), P(EVERY))
    out_specs = (P(None, EVERY), P())
    return jax.shard_map(
        on_device, mesh=fine, in_specs=in_specs, out_specs=out_specs, check_vma=False
    )
```

time: 172 us -> 161 us (0.936); the launches traced: 170 us -> 162 us
  starting transfers between devices: 51.3 us -> 38.3 us
  local copies, waits for them, and re-layouts: 9.81 us -> 2.75 us
  waiting for transfers between devices: 40.4 us -> 46.9 us
  blocking collectives: 25.5 us -> 30.2 us
  other arithmetic: 2.73 us -> 4.54 us
    all_gather x1, waiting for transfers between devices: 7.73 us -> 27.4 us  [on_device(): far_all = lax.all_gather(far_send, FAR)]
    all_to_all x3 -> x1, starting transfers between devices: 20.9 us -> 3.61 us  [on_device(): far_back = lax.all_to_all(far_pair, ('x', 'y'), 0, 0)]
    all_to_all x3 -> x1, waiting for transfers between devices: 11.7 us -> 0.01 us  [on_device(): far_back = lax.all_to_all(far_pair, ('x', 'y'), 0, 0)]
    ppermute x11 -> x4, starting transfers between devices: 12.4 us -> 17.1 us  [swap(): return lax.ppermute(values, axis, [(i, i ^ bit) for i in range(size)])]
    all_to_all x2, blocking collectives: 25.5 us -> 30.2 us  [on_device(): lax.all_to_all(jnp.broadcast_to(partial_gram, (16, 8, 128)), group, 0, 0)]
    unnamed x16 -> x10, local copies, waits for them, and re-layouts: 5.29 us -> 1.84 us
    ppermute x11 -> x4, waiting for transfers between devices: 5.29 us -> 4.02 us  [swap(): return lax.ppermute(values, axis, [(i, i ^ bit) for i in range(size)])]
  transfers between devices with their start and end apart: 25 -> 16, of which waited for: 9 -> 7; matrix products, arithmetic and copies ran while one was open for 3% -> 2% of each run, Pallas kernels for 2% -> 2%
where the time goes in v5:
time: 161 us; the launch traced here: 162 us
  waiting for transfers between devices  46.9 us (29%)
  starting transfers between devices  38.3 us (24%)
  blocking collectives  30.2 us (19%)
  Pallas kernels  23.8 us (15%)
  between operations  14.9 us (9%)
  other arithmetic  4.54 us (3%)
  local copies, waits for them, and re-layouts  2.75 us (2%)
    all_to_all x2, blocking collectives, on_device(): lax.all_to_all(jnp.broadcast_to(partial_gram, (16, 8, 128)), group, 0, 0)  30.2 us
    all_gather x1, waiting for transfers between devices, on_device(): far_all = lax.all_gather(far_send, FAR)  27.4 us
    ppermute x10, starting transfers between devices, shift(): lax.ppermute(values, axis, [(i, (i + by) % size) for i in range(size)])  17.5 us
    ppermute x4, starting transfers between devices, swap(): return lax.ppermute(values, axis, [(i, i ^ bit) for i in range(size)])  17.1 us
    pallas_call x1, Pallas kernels, on_device(): pl.pallas_call(tile_kernel, out_shape=[jax.ShapeDtypeStruct((Z // 2, AUG,...  16.6 us
    ppermute x10, waiting for transfers between devices, shift(): lax.ppermute(values, axis, [(i, (i + by) % size) for i in range(size)])  15.4 us
    pallas_call x1, Pallas kernels, on_device(): pl.pallas_call(finish_kernel, out_shape=[jax.ShapeDtypeStruct((VEC, BS),...  4.57 us
    ppermute x4, waiting for transfers between devices, swap(): return lax.ppermute(values, axis, [(i, i ^ bit) for i in range(size)])  4.02 us
  transfers between devices with their start and end apart: 16, of which 7 were waited for; matrix products, arithmetic and copies ran while one was open for 2% of the time, Pallas kernels for 2%

profile of v5, /device:TPU:1, one launch (start us, length us, event | category | flops | bytes accessed | tf_op | source)
XLA Modules:
  0.0 161.5 jit_solution(16743353875349513566)
XLA Ops:
  7.2 0.0 copy-start.2
  7.2 0.0 copy-start.3
  7.2 0.0 all-gather.3.cloned.1.call-start
  7.2 0.9 convert_element_type.23
  8.1 1.1 copy.11
  9.3 0.0 copy-done.2
  9.3 0.7 pad_maximum_fusion
  10.0 0.0 all-gather.3.cloned.1.call-update
  10.1 2.5 %collective-permute-start.6 = (bf16[288,512]{1,0:T(8,128)(2,1)S(1)}, bf16[288,512]{1,0:T(8,128)(2,1)S(1)}, u32[]{:S(2)}, u32[]{:S(2)}) collective-permute-start(bf16[288,512]{1,0:T(8,128)(2,1)S(1)} %get-tuple-element.12.refs_0_), channel_id=1, source_target_pairs={{0,4},{4,8},{8,12},{12,16},{16,20},{20,24},{24,28},{28,0},{1,5},{5... | collective-permute-start | bytes 884744 | tf_op jit(solution)/shard_map/ppermute | solution.py:123
  12.6 4.0 %collective-permute-start.3 = (bf16[288,512]{1,0:T(8,128)(2,1)S(1)}, bf16[288,512]{1,0:T(8,128)(2,1)S(1)}, u32[]{:S(2)}, u32[]{:S(2)}) collective-permute-start(bf16[288,512]{1,0:T(8,128)(2,1)S(1)} %get-tuple-element.12.refs_0_), channel_id=1, source_target_pairs={{0,28},{4,0},{8,4},{12,8},{16,12},{20,16},{24,20},{28,24},{1,29},{... | collective-permute-start | bytes 884744 | tf_op jit(solution)/shard_map/ppermute | solution.py:123
  16.6 6.6 %collective-permute-done.6.refs_7_ = bf16[288,512]{1,0:T(8,128)(2,1)S(1)} collective-permute-done((bf16[288,512]{1,0:T(8,128)(2,1)S(1)}, bf16[288,512]{1,0:T(8,128)(2,1)S(1)}, u32[]{:S(2)}, u32[]{:S(2)}) %collective-permute-start.6) | collective-permute-done | bytes 294944 | tf_op jit(solution)/shard_map/ppermute | solution.py:123
  23.3 0.0 collective-permute-start.7
  23.3 0.0 collective-permute-done.3.refs_1_
  23.3 2.7 %collective-permute-start.4 = (bf16[288,512]{1,0:T(8,128)(2,1)S(1)}, bf16[288,512]{1,0:T(8,128)(2,1)S(1)}, u32[]{:S(2)}, u32[]{:S(2)}) collective-permute-start(bf16[288,512]{1,0:T(8,128)(2,1)S(1)} %collective-permute-done.3.refs_1_), channel_id=1, source_target_pairs={{0,28},{4,0},{8,4},{12,8},{16,12},{20,16},{24,20},{28,24},{1,29},{... | collective-permute-start | bytes 884744 | tf_op jit(solution)/shard_map/ppermute | solution.py:123
  26.0 5.9 %collective-permute-done.7.refs_6_ = bf16[288,512]{1,0:T(8,128)(2,1)S(1)} collective-permute-done((bf16[288,512]{1,0:T(8,128)(2,1)S(1)}, bf16[288,512]{1,0:T(8,128)(2,1)S(1)}, u32[]{:S(2)}, u32[]{:S(2)}) %collective-permute-start.7) | collective-permute-done | bytes 294944 | tf_op jit(solution)/shard_map/ppermute | solution.py:123
  31.9 0.0 collective-permute-start.8
  32.5 0.0 copy-done.3
  32.5 0.1 copy.10
  32.6 0.1 reshape.12
  32.7 0.1 pad_add_fusion.2
  32.8 2.9 %collective-permute-start.1 = (s32[128]{0:T(128)S(1)}, s32[128]{0:T(128)S(1)}, u32[]{:S(2)}, u32[]{:S(2)}) collective-permute-start(s32[128]{0:T(128)S(1)} %pad_add_fusion.2), channel_id=1, source_target_pairs={{0,2},{1,3},{2,0},{3,1},{4,6},{5,7},{6,4},{7,5},{8,10},{9,11},{10,... | collective-permute-start | bytes 1544 | tf_op jit(solution)/shard_map/ppermute | solution.py:123
  35.7 0.4 collective-permute-start
  36.1 2.3 %collective-permute-start.2 = (s32[128]{0:T(128)S(1)}, s32[128]{0:T(128)S(1)}, u32[]{:S(2)}, u32[]{:S(2)}) collective-permute-start(s32[128]{0:T(128)S(1)} %pad_add_fusion.2), channel_id=1, source_target_pairs={{0,3},{1,0},{2,1},{3,2},{4,7},{5,4},{6,5},{7,6},{8,11},{9,8},{10,9... | collective-permute-start | bytes 1544 | tf_op jit(solution)/shard_map/ppermute | solution.py:123
  38.4 0.0 collective-permute-done.4.refs_2_
  38.4 2.7 %collective-permute-start.5 = (bf16[288,512]{1,0:T(8,128)(2,1)S(1)}, bf16[288,512]{1,0:T(8,128)(2,1)S(1)}, u32[]{:S(2)}, u32[]{:S(2)}) collective-permute-start(bf16[288,512]{1,0:T(8,128)(2,1)S(1)} %collective-permute-done.4.refs_2_), channel_id=1, source_target_pairs={{0,28},{4,0},{8,4},{12,8},{16,12},{20,16},{24,20},{28,24},{1,29},{... | collective-permute-start | bytes 884744 | tf_op jit(solution)/shard_map/ppermute | solution.py:123
  41.1 0.0 collective-permute-done.8.refs_5_
  41.1 0.0 collective-permute-start.9
  41.1 0.1 fusion.6
  41.2 0.7 pad_add_fusion.1.place_ref
  41.8 0.0 collective-permute-done.1
  41.8 0.0 collective-permute-done
  41.8 0.0 collective-permute-done.2
  41.9 0.6 pad_add_fusion.lists_ref
  42.4 2.6 %select_pairs.1.picked_ref = s32[128]{0:T(128)} custom-call(s32[3]{0:T(128)} %pad_add_fusion.1.place_ref, s32[4,128]{1,0:T(4,128)} %pad_add_fusion.lists_ref), custom_call_target="tpu_custom_call" | custom-call | tf_op jit(solution)/shard_map/select_pairs/pallas_call | solution.py:157
  45.0 0.0 collective-permute-done.5.refs_3_
  45.1 2.8 %collective-permute-done.9.refs_4_ = bf16[288,512]{1,0:T(8,128)(2,1)S(1)} collective-permute-done((bf16[288,512]{1,0:T(8,128)(2,1)S(1)}, bf16[288,512]{1,0:T(8,128)(2,1)S(1)}, u32[]{:S(2)}, u32[]{:S(2)}) %collective-permute-start.9) | collective-permute-done | bytes 294944 | tf_op jit(solution)/shard_map/ppermute | solution.py:123
  47.9 27.4 %all-gather.3.cloned.1.call-done = bf16[9216,512]{1,0:T(8,128)(2,1)} async-done(((bf16[288,512]{1,0:T(8,128)(2,1)}), bf16[9216,512]{1,0:T(8,128)(2,1)}) %all-gather.3.cloned.1.call-update) | async-done | bytes 9437200 | tf_op jit(solution)/shard_map/all_gather | solution.py:134
  75.3 0.0 copy-start
  75.3 0.7 copy-done
  76.0 16.6 %tiles.1 = (f32[4,48,512]{2,1,0:T(8,128)S(1)}, bf16[4,48,512]{2,1,0:T(8,128)(2,1)S(1)}, f32[16,48,512]{2,1,0:T(8,128)S(1)}, bf16[16,48,512]{2,1,0:T(8,128)(2,1)S(1)}) custom-call(s32[128]{0:T(128)S(1)} %copy-done, bf16[32,288,512]{2,1,0:T(8,128)(2,1)} %bitcast.17, bf16[288,512]{1,0:T(8,128)(2,1)S(1)} %get-tuple-element.12.refs_0_, ...), custom_call_target="tpu_custom_call" | custom-call | tf_op jit(solution)/shard_map/tiles/pallas_call | solution.py:164
  92.6 0.1 collective-permute-start.13
  92.7 5.2 %collective-permute-start.10 = (bf16[4,48,512]{2,1,0:T(8,128)(2,1)S(1)}, bf16[4,48,512]{2,1,0:T(8,128)(2,1)S(1)}, u32[]{:S(2)}, u32[]{:S(2)}) collective-permute-start(bf16[4,48,512]{2,1,0:T(8,128)(2,1)S(1)} %get-tuple-element.7), channel_id=1, source_target_pairs={{0,4},{4,0},{8,12},{12,8},{16,20},{20,16},{24,28},{28,24},{1,5},{5... | collective-permute-start | bytes 589832 | tf_op jit(solution)/shard_map/ppermute | solution.py:127
  97.9 0.0 collective-permute-done.13
  97.9 1.2 add_convert_fusion
  99.1 3.6 %all-to-all-start = ((bf16[16,48,512]{2,1,0:T(8,128)(2,1)}), bf16[16,48,512]{2,1,0:T(8,128)(2,1)S(1)}, u32[]{:S(2)}, u32[]{:S(2)}) async-start(bf16[16,48,512]{2,1,0:T(8,128)(2,1)} %add_convert_fusion), calls=%async_computation | async-start | bytes 1572864 | tf_op jit(solution)/shard_map/all_to_all | solution.py:186
  102.7 0.1 collective-permute-done.10
  102.9 1.9 %collective-permute-start.11 = (bf16[2,48,512]{2,1,0:T(8,128)(2,1)S(1)}, bf16[2,48,512]{2,1,0:T(8,128)(2,1)S(1)}, u32[]{:S(2)}, u32[]{:S(2)}) collective-permute-start(bf16[2,48,512]{2,1,0:T(8,128)(2,1)S(1)} %slice.51), channel_id=1, source_target_pairs={{0,8},{4,12},{8,0},{12,4},{16,24},{20,28},{24,16},{28,20},{1,9},{5... | collective-permute-start | bytes 294920 | tf_op jit(solution)/shard_map/ppermute | solution.py:127
  104.8 2.6 %collective-permute-done.11 = bf16[2,48,512]{2,1,0:T(8,128)(2,1)S(1)} collective-permute-done((bf16[2,48,512]{2,1,0:T(8,128)(2,1)S(1)}, bf16[2,48,512]{2,1,0:T(8,128)(2,1)S(1)}, u32[]{:S(2)}, u32[]{:S(2)}) %collective-permute-start.11) | collective-permute-done | bytes 98336 | tf_op jit(solution)/shard_map/ppermute | solution.py:127
  107.4 10.0 %collective-permute-start.12 = (bf16[1,48,512]{2,1,0:T(8,128)(2,1)S(1)}, bf16[1,48,512]{2,1,0:T(8,128)(2,1)S(1)}, u32[]{:S(2)}, u32[]{:S(2)}) collective-permute-start(bf16[1,48,512]{2,1,0:T(8,128)(2,1)S(1)} %slice.52), channel_id=1, source_target_pairs={{0,16},{4,20},{8,24},{12,28},{16,0},{20,4},{24,8},{28,12},{1,17},{... | collective-permute-start | bytes 147464 | tf_op jit(solution)/shard_map/ppermute | solution.py:127
  117.4 0.0 all-to-all-done
  117.4 0.1 convert_reduce_fusion
  117.5 1.4 collective-permute-done.12
  118.9 0.0 copy-start.1
  118.9 0.2 fusion.3
  119.1 0.1 broadcast_in_dim.17
  119.2 13.0 %all_to_all.15 = f32[16,8,128]{2,1,0:T(8,128)S(1)} all-to-all(f32[16,8,128]{2,1,0:T(8,128)S(1)} %broadcast_in_dim.18), channel_id=1, replica_groups=mesh['x'=4,'k'=2,'z'=8,'y'=4] {'x','y'}, dimensions={0} | all-to-all | bytes 131072 | tf_op jit(solution)/shard_map/all_to_all | solution.py:199
  132.2 17.2 %all_to_all.16 = f32[16,8,128]{2,1,0:T(8,128)S(1)} all-to-all(f32[16,8,128]{2,1,0:T(8,128)S(1)} %broadcast_in_dim.19), channel_id=1, replica_groups=mesh['x'=4,'k'=2,'z'=8,'y'=4] {'k','z'}, dimensions={0} | all-to-all | bytes 131072 | tf_op jit(solution)/shard_map/all_to_all | solution.py:199
  149.4 0.7 div.23.gram_ref
  150.1 0.0 copy-done.1
  150.1 4.6 %finish.1 = (f32[32,512]{1,0:T(8,128)}, f32[32,32]{1,0:T(8,128)}) custom-call(f32[32,32]{1,0:T(8,128)} %div.23.gram_ref, f32[32,512]{1,0:T(8,128)} %copy-done.1), custom_call_target="tpu_custom_call" | custom-call | tf_op jit(solution)/shard_map/finish/pallas_call | solution.py:202
  (15 shorter events, 0.3 us)
Async XLA Ops:
  7.2 2.1 %copy-start.2 = (bf16[256,512]{1,0:T(8,128)(2,1)S(1)}, bf16[256,512]{1,0:T(8,128)(2,1)}, u32[]{:S(2)}) copy-start(bf16[256,512]{1,0:T(8,128)(2,1)} %param.4) | copy-start | bytes 786436
  7.2 25.4 %copy-start.3 = (s32[24,2]{0,1:T(2,128)S(1)}, s32[24,2]{0,1:T(2,128)}, u32[]{:S(2)}) copy-start(s32[24,2]{0,1:T(2,128)} %param.6) | copy-start | bytes 580
  7.2 68.1 %all-gather.3.cloned.1.call-start = ((), (), s32[]{:S(2)}) async-start(), calls=%async_computation.3 | async-start | bytes 9732096 | tf_op jit(solution)/shard_map/all_gather | solution.py:134
  10.1 13.2 %collective-permute-start.6 = (bf16[288,512]{1,0:T(8,128)(2,1)S(1)}, bf16[288,512]{1,0:T(8,128)(2,1)S(1)}, u32[]{:S(2)}, u32[]{:S(2)}) collective-permute-start(bf16[288,512]{1,0:T(8,128)(2,1)S(1)} %get-tuple-element.12.refs_0_), channel_id=1, source_target_pairs={{0,4},{4,8},{8,12},{12,16},{16,20},{20,24},{24,28},{28,0},{1,5},{5... | collective-permute-start | bytes 884744 | tf_op jit(solution)/shard_map/ppermute | solution.py:123
  12.6 10.7 %collective-permute-start.3 = (bf16[288,512]{1,0:T(8,128)(2,1)S(1)}, bf16[288,512]{1,0:T(8,128)(2,1)S(1)}, u32[]{:S(2)}, u32[]{:S(2)}) collective-permute-start(bf16[288,512]{1,0:T(8,128)(2,1)S(1)} %get-tuple-element.12.refs_0_), channel_id=1, source_target_pairs={{0,28},{4,0},{8,4},{12,8},{16,12},{20,16},{24,20},{28,24},{1,29},{... | collective-permute-start | bytes 884744 | tf_op jit(solution)/shard_map/ppermute | solution.py:123
  23.3 8.6 %collective-permute-start.7 = (bf16[288,512]{1,0:T(8,128)(2,1)S(1)}, bf16[288,512]{1,0:T(8,128)(2,1)S(1)}, u32[]{:S(2)}, u32[]{:S(2)}) collective-permute-start(bf16[288,512]{1,0:T(8,128)(2,1)S(1)} %collective-permute-done.6.refs_7_), channel_id=1, source_target_pairs={{0,4},{4,8},{8,12},{12,16},{16,20},{20,24},{24,28},{28,0},{1,5},{5... | collective-permute-start | bytes 884744 | tf_op jit(solution)/shard_map/ppermute | solution.py:123
  23.3 15.1 %collective-permute-start.4 = (bf16[288,512]{1,0:T(8,128)(2,1)S(1)}, bf16[288,512]{1,0:T(8,128)(2,1)S(1)}, u32[]{:S(2)}, u32[]{:S(2)}) collective-permute-start(bf16[288,512]{1,0:T(8,128)(2,1)S(1)} %collective-permute-done.3.refs_1_), channel_id=1, source_target_pairs={{0,28},{4,0},{8,4},{12,8},{16,12},{20,16},{24,20},{28,24},{1,29},{... | collective-permute-start | bytes 884744 | tf_op jit(solution)/shard_map/ppermute | solution.py:123
  31.9 9.2 %collective-permute-start.8 = (bf16[288,512]{1,0:T(8,128)(2,1)S(1)}, bf16[288,512]{1,0:T(8,128)(2,1)S(1)}, u32[]{:S(2)}, u32[]{:S(2)}) collective-permute-start(bf16[288,512]{1,0:T(8,128)(2,1)S(1)} %collective-permute-done.7.refs_6_), channel_id=1, source_target_pairs={{0,4},{4,8},{8,12},{12,16},{16,20},{20,24},{24,28},{28,0},{1,5},{5... | collective-permute-start | bytes 884744 | tf_op jit(solution)/shard_map/ppermute | solution.py:123
  32.8 9.0 %collective-permute-start.1 = (s32[128]{0:T(128)S(1)}, s32[128]{0:T(128)S(1)}, u32[]{:S(2)}, u32[]{:S(2)}) collective-permute-start(s32[128]{0:T(128)S(1)} %pad_add_fusion.2), channel_id=1, source_target_pairs={{0,2},{1,3},{2,0},{3,1},{4,6},{5,7},{6,4},{7,5},{8,10},{9,11},{10,... | collective-permute-start | bytes 1544 | tf_op jit(solution)/shard_map/ppermute | solution.py:123
  35.7 6.1 %collective-permute-start = (s32[128]{0:T(128)S(1)}, s32[128]{0:T(128)S(1)}, u32[]{:S(2)}, u32[]{:S(2)}) collective-permute-start(s32[128]{0:T(128)S(1)} %pad_add_fusion.2), channel_id=1, source_target_pairs={{0,1},{1,2},{2,3},{3,0},{4,5},{5,6},{6,7},{7,4},{8,9},{9,10},{10,1... | collective-permute-start | bytes 1544 | tf_op jit(solution)/shard_map/ppermute | solution.py:123
  36.1 5.7 %collective-permute-start.2 = (s32[128]{0:T(128)S(1)}, s32[128]{0:T(128)S(1)}, u32[]{:S(2)}, u32[]{:S(2)}) collective-permute-start(s32[128]{0:T(128)S(1)} %pad_add_fusion.2), channel_id=1, source_target_pairs={{0,3},{1,0},{2,1},{3,2},{4,7},{5,4},{6,5},{7,6},{8,11},{9,8},{10,9... | collective-permute-start | bytes 1544 | tf_op jit(solution)/shard_map/ppermute | solution.py:123
  38.4 6.6 %collective-permute-start.5 = (bf16[288,512]{1,0:T(8,128)(2,1)S(1)}, bf16[288,512]{1,0:T(8,128)(2,1)S(1)}, u32[]{:S(2)}, u32[]{:S(2)}) collective-permute-start(bf16[288,512]{1,0:T(8,128)(2,1)S(1)} %collective-permute-done.4.refs_2_), channel_id=1, source_target_pairs={{0,28},{4,0},{8,4},{12,8},{16,12},{20,16},{24,20},{28,24},{1,29},{... | collective-permute-start | bytes 884744 | tf_op jit(solution)/shard_map/ppermute | solution.py:123
  41.1 6.8 %collective-permute-start.9 = (bf16[288,512]{1,0:T(8,128)(2,1)S(1)}, bf16[288,512]{1,0:T(8,128)(2,1)S(1)}, u32[]{:S(2)}, u32[]{:S(2)}) collective-permute-start(bf16[288,512]{1,0:T(8,128)(2,1)S(1)} %collective-permute-done.8.refs_5_), channel_id=1, source_target_pairs={{0,4},{4,8},{8,12},{12,16},{16,20},{20,24},{24,28},{28,0},{1,5},{5... | collective-permute-start | bytes 884744 | tf_op jit(solution)/shard_map/ppermute | solution.py:123
  75.3 0.7 copy-start
  92.6 5.3 %collective-permute-start.13 = (bf16[16,48,512]{2,1,0:T(8,128)(2,1)S(1)}, bf16[16,48,512]{2,1,0:T(8,128)(2,1)S(1)}, u32[]{:S(2)}, u32[]{:S(2)}) collective-permute-start(bf16[16,48,512]{2,1,0:T(8,128)(2,1)S(1)} %get-tuple-element.9), channel_id=1, source_target_pairs={{0,32},{32,0},{1,33},{33,1},{2,34},{34,2},{3,35},{35,3},{4,36},{36... | collective-permute-start | bytes 2359304 | tf_op jit(solution)/shard_map/ppermute | solution.py:127
  92.7 10.1 %collective-permute-start.10 = (bf16[4,48,512]{2,1,0:T(8,128)(2,1)S(1)}, bf16[4,48,512]{2,1,0:T(8,128)(2,1)S(1)}, u32[]{:S(2)}, u32[]{:S(2)}) collective-permute-start(bf16[4,48,512]{2,1,0:T(8,128)(2,1)S(1)} %get-tuple-element.7), channel_id=1, source_target_pairs={{0,4},{4,0},{8,12},{12,8},{16,20},{20,16},{24,28},{28,24},{1,5},{5... | collective-permute-start | bytes 589832 | tf_op jit(solution)/shard_map/ppermute | solution.py:127
  99.1 18.3 %all-to-all-start = ((bf16[16,48,512]{2,1,0:T(8,128)(2,1)}), bf16[16,48,512]{2,1,0:T(8,128)(2,1)S(1)}, u32[]{:S(2)}, u32[]{:S(2)}) async-start(bf16[16,48,512]{2,1,0:T(8,128)(2,1)} %add_convert_fusion), calls=%async_computation | async-start | bytes 1572864 | tf_op jit(solution)/shard_map/all_to_all | solution.py:186
  102.9 4.5 %collective-permute-start.11 = (bf16[2,48,512]{2,1,0:T(8,128)(2,1)S(1)}, bf16[2,48,512]{2,1,0:T(8,128)(2,1)S(1)}, u32[]{:S(2)}, u32[]{:S(2)}) collective-permute-start(bf16[2,48,512]{2,1,0:T(8,128)(2,1)S(1)} %slice.51), channel_id=1, source_target_pairs={{0,8},{4,12},{8,0},{12,4},{16,24},{20,28},{24,16},{28,20},{1,9},{5... | collective-permute-start | bytes 294920 | tf_op jit(solution)/shard_map/ppermute | solution.py:127
  107.4 11.4 %collective-permute-start.12 = (bf16[1,48,512]{2,1,0:T(8,128)(2,1)S(1)}, bf16[1,48,512]{2,1,0:T(8,128)(2,1)S(1)}, u32[]{:S(2)}, u32[]{:S(2)}) collective-permute-start(bf16[1,48,512]{2,1,0:T(8,128)(2,1)S(1)} %slice.52), channel_id=1, source_target_pairs={{0,16},{4,20},{8,24},{12,28},{16,0},{20,4},{24,8},{28,12},{1,17},{... | collective-permute-start | bytes 147464 | tf_op jit(solution)/shard_map/ppermute | solution.py:127
  118.9 31.2 %copy-start.1 = (f32[32,512]{1,0:T(8,128)}, f32[32,512]{1,0:T(8,128)S(1)}, u32[]{:S(2)}) copy-start(f32[32,512]{1,0:T(8,128)S(1)} %slice_divide_fusion.walked_ref) | copy-start | bytes 196612
Sparse Core Ops, SparseCore 0:
  10.6 64.6 all-gather.2

commit v6 on v5

--- a/solution.py
+++ b/solution.py
@@ -15,6 +15,7 @@
 FARS = X * K * Y
 BS = 512
 EMB = 256
+HALF = 256
 VEC = 32
 AUG = 48
 MAXP = 24
@@ -46,49 +47,56 @@
     picked_ref[0] = lax.fori_loop(0, Y, each_list, jnp.int32(0))
 
 
-def tile_kernel(picked_ref, far_hbm, *refs):
-    near_hbm = refs[:Z]
-    near_keep, near_give, far_keep, far_give, near_ref, far_ref, near_sum, far_sum, sems = refs[Z:]
+def tile_kernel(last, picked_ref, far_hbm, *refs):
+    near_hbm, refs = refs[:Z], refs[Z:]
+    if last:
+        near_before, near_keep, near_give, far_keep, far_give = refs[:5]
+        near_ref, far_ref, near_sum, far_sum, sems = refs[5:]
+    else:
+        near_sum, far_keep, far_give, near_ref, far_ref, far_sum, sems = refs
     copies = [pltpu.make_async_copy(far_hbm, far_ref, sems.at[Z])]
     for slot in range(Z):
         copies.append(pltpu.make_async_copy(near_hbm[slot], near_ref.at[slot], sems.at[slot]))
     for copy in copies:
         copy.start()
-    near_sum[...] = jnp.zeros_like(near_sum)
+    near_sum[...] = near_before[...] if last else jnp.zeros_like(near_sum)
     far_sum[...] = jnp.zeros_like(far_sum)
     ones = (lax.broadcasted_iota(jnp.int32, (AUG - VEC, BS), 0) == 0).astype(jnp.bfloat16)
     for copy in copies:
         copy.wait()
-
-    def each_tile(number, carry):
-        code = picked_ref[number + 1]
+    found = picked_ref[0]
+
+    def one_tile(number):
+        live = number < found
+        code = jnp.where(live, picked_ref[number + 1], 0)
         far = code & 31
         home = (code >> 5) & 31
         near = (code >> 10) & 7
         back = (code >> 13) & 7
-        mirror = jnp.where((code >> 16) == 1, 0.0, 1.0).astype(jnp.float32)
-        far_embed = far_ref[far, :EMB, :]
+        keep = jnp.where(live, 1.0, 0.0).astype(jnp.float32)
+        mirror = jnp.where(live & ((code >> 16) == 0), 1.0, 0.0).astype(jnp.float32)
         near_vec = jnp.concatenate([near_ref[near, EMB:, :], ones], axis=0)
-        far_vec = jnp.concatenate([far_ref[far, EMB:, :], ones], axis=0)
-        far_terms = None
-        for half in range(2):
-            cut = slice(half * 256, half * 256 + 256)
-            scores = jnp.dot(
-                near_ref[near, :EMB, cut], far_embed, preferred_element_type=jnp.float32
-            )
-            tile = (0.5 * jnp.tanh(scores) + 0.5).astype(jnp.bfloat16)
-            near_terms = lax.dot_general(
-                far_vec, tile, (((1,), (1,)), ((), ())), preferred_element_type=jnp.float32
-            )
-            near_sum[back, :, cut] += near_terms
-            part = jnp.dot(near_vec[:, cut], tile, preferred_element_type=jnp.float32)
-            far_terms = part if far_terms is None else far_terms + part
-        far_sum[home] += far_terms * mirror
+        far_vec = jnp.concatenate([far_ref[far, EMB:, :], ones[:, :HALF]], axis=0)
+        scores = jnp.dot(
+            far_ref[far, :EMB, :], near_ref[near, :EMB, :], preferred_element_type=jnp.float32
+        )
+        tile = (0.5 * jnp.tanh(scores) + 0.5).astype(jnp.bfloat16)
+        far_terms = lax.dot_general(
+            near_vec, tile, (((1,), (1,)), ((), ())), preferred_element_type=jnp.float32
+        )
+        near_terms = jnp.dot(far_vec, tile, preferred_element_type=jnp.float32)
+        return back, near_terms * keep, home, far_terms * mirror
+
+    def each_pair(number, carry):
+        for back, near_terms, home, far_terms in [one_tile(2 * number), one_tile(2 * number + 1)]:
+            near_sum[back] += near_terms
+            far_sum[home] += far_terms
         return carry
 
-    lax.fori_loop(0, picked_ref[0], each_tile, 0)
-    near_keep[...] = near_sum[: Z // 2]
-    near_give[...] = near_sum[Z // 2 :].astype(jnp.bfloat16)
+    lax.fori_loop(0, (found + 1) >> 1, each_pair, 0)
+    if last:
+        near_keep[...] = near_sum[: Z // 2]
+        near_give[...] = near_sum[Z // 2 :].astype(jnp.bfloat16)
     far_keep[...] = far_sum[: X * Y]
     far_give[...] = far_sum[X * Y :].astype(jnp.bfloat16)
 
@@ -130,17 +138,12 @@
 def on_device(embeddings, vectors, block_pairs, counts):
     score_scale = 0.5 / math.sqrt(EMB)
     vector_bf16 = vectors.astype(jnp.bfloat16)
-    far_send = lax.optimization_barrier(jnp.concatenate([embeddings, vector_bf16], axis=0))
-    far_all = lax.all_gather(far_send, FAR)
-    turned = embeddings.T
-    near_send = jnp.concatenate(
-        [
-            jnp.concatenate([turned[:256], turned[256:]], axis=1)
-            * jnp.asarray(score_scale, jnp.bfloat16),
-            vector_bf16,
-        ],
-        axis=0,
-    )
+    turned = embeddings.T * jnp.asarray(score_scale, jnp.bfloat16)
+    far_halves = []
+    for cut in (slice(0, HALF), slice(HALF, BS)):
+        far_send = jnp.concatenate([turned[cut], vector_bf16[:, cut]], axis=0)
+        far_halves.append(lax.all_gather(far_send, FAR))
+    near_send = jnp.concatenate([embeddings, vector_bf16], axis=0)
     ring = {0: near_send}
     for step in range(1, Z // 2 + 1):
         ring[Z - step] = shift(ring[(Z - step + 1) % Z], "z", Z, 1)
@@ -161,28 +164,44 @@
         out_specs=smem,
         name="select_pairs",
     )(place, lists)
-    near_total, near_give, far_total, far_give = pl.pallas_call(
-        tile_kernel,
-        out_shape=[
-            jax.ShapeDtypeStruct((Z // 2, AUG, BS), jnp.float32),
-            jax.ShapeDtypeStruct((Z // 2, AUG, BS), jnp.bfloat16),
-            jax.ShapeDtypeStruct((X * Y, AUG, BS), jnp.float32),
-            jax.ShapeDtypeStruct((X * Y, AUG, BS), jnp.bfloat16),
-        ],
-        in_specs=[smem] + [pl.BlockSpec(memory_space=pl.ANY)] * (1 + Z),
-        out_specs=[vmem] * 4,
-        scratch_shapes=[
-            pltpu.VMEM((Z, EMB + VEC, BS), jnp.bfloat16),
-            pltpu.VMEM((FARS, EMB + VEC, BS), jnp.bfloat16),
-            pltpu.VMEM((Z, AUG, BS), jnp.float32),
-            pltpu.VMEM((FARS, AUG, BS), jnp.float32),
-            pltpu.SemaphoreType.DMA((Z + 1,)),
-        ],
-        compiler_params=pltpu.CompilerParams(vmem_limit_bytes=48 * 1024 * 1024),
-        name="tiles",
-    )(picked, far_all, *near_blocks)
-    far_taken = swap(far_give, "k", K, 1)
-    far_pair = (far_total + far_taken.astype(jnp.float32)).astype(jnp.bfloat16)
+    far_outs = [
+        jax.ShapeDtypeStruct((X * Y, AUG, HALF), jnp.float32),
+        jax.ShapeDtypeStruct((X * Y, AUG, HALF), jnp.bfloat16),
+    ]
+    whole_near = jax.ShapeDtypeStruct((Z, AUG, BS), jnp.float32)
+    half_near = [
+        jax.ShapeDtypeStruct((Z // 2, AUG, BS), jnp.float32),
+        jax.ShapeDtypeStruct((Z // 2, AUG, BS), jnp.bfloat16),
+    ]
+    near_before = []
+    far_pairs = []
+    for last in (False, True):
+        outs = (half_near if last else [whole_near]) + far_outs
+        held = [pltpu.VMEM((Z, AUG, BS), jnp.float32)] if last else []
+        results = pl.pallas_call(
+            functools.partial(tile_kernel, last),
+            out_shape=outs,
+            in_specs=[smem]
+            + [pl.BlockSpec(memory_space=pl.ANY)] * (1 + Z)
+            + [vmem] * len(near_before),
+            out_specs=[vmem] * len(outs),
+            scratch_shapes=[
+                pltpu.VMEM((Z, EMB + VEC, BS), jnp.bfloat16),
+                pltpu.VMEM((FARS, EMB + VEC, HALF), jnp.bfloat16),
+            ]
+            + held
+            + [
+                pltpu.VMEM((FARS, AUG, HALF), jnp.float32),
+                pltpu.SemaphoreType.DMA((Z + 1,)),
+            ],
+            compiler_params=pltpu.CompilerParams(vmem_limit_bytes=48 * 1024 * 1024),
+            name="tiles_last" if last else "tiles_first",
+        )(picked, far_halves[last], *near_blocks, *near_before)
+        near_before = list(results[:-2])
+        far_taken = swap(results[-1], "k", K, 1)
+        far_pairs.append((results[-2] + far_taken.astype(jnp.float32)).astype(jnp.bfloat16))
+    near_total, near_give = near_before
+    far_pair = jnp.concatenate(far_pairs, axis=2)
     far_back = lax.all_to_all(far_pair, ("x", "y"), 0, 0)
     for bit in (1, 2, 4):
         left = near_total.shape[0] if bit == 1 else near_total.shape[0] // 2

time: 161 us -> 198 us (1.23)
  waiting for transfers between devices: 46.9 us -> 91.8 us
  starting transfers between devices: 38.3 us -> 28.5 us
  local copies, waits for them, and re-layouts: 2.75 us -> 4.78 us
    all_gather x1 -> x2, waiting for transfers between devices: 27.4 us -> 63 us  [on_device(): far_halves.append(lax.all_gather(far_send, FAR))]
    ppermute x4 -> x5, starting transfers between devices: 17.1 us -> 3.98 us  [swap(): return lax.ppermute(values, axis, [(i, i ^ bit) for i in range(size)])]
    ppermute x4 -> x5, waiting for transfers between devices: 4.02 us -> 8.72 us  [swap(): return lax.ppermute(values, axis, [(i, i ^ bit) for i in range(size)])]
    all_to_all x1, waiting for transfers between devices: 0.01 us -> 4.04 us  [on_device(): far_back = lax.all_to_all(far_pair, ('x', 'y'), 0, 0)]
    all_to_all x1, starting transfers between devices: 3.61 us -> 7.48 us  [on_device(): far_back = lax.all_to_all(far_pair, ('x', 'y'), 0, 0)]
    unnamed x10 -> x16, local copies, waits for them, and re-layouts: 1.84 us -> 3.87 us
    pallas_call x1 -> x2, Pallas kernels: 16.6 us -> 16.2 us  [on_device(): pl.pallas_call(functools.partial(tile_kernel, last), out_shape=outs, in_s...]
  transfers between devices with their start and end apart: 16 -> 18, of which waited for: 7 -> 9; matrix products, arithmetic and copies ran while one was open for 2% -> 2% of each run, Pallas kernels for 2% -> 9%
where the time goes in v6:
time: 198 us
  waiting for transfers between devices  91.8 us (46%)
  blocking collectives  28.6 us (14%)
  starting transfers between devices  28.5 us (14%)
  Pallas kernels  22.8 us (12%)
  between operations  14.9 us (8%)
  other arithmetic  6.09 us (3%)
  local copies, waits for them, and re-layouts  4.78 us (2%)
    all_gather x2, waiting for transfers between devices, on_device(): far_halves.append(lax.all_gather(far_send, FAR))  63 us
    all_to_all x2, blocking collectives, on_device(): lax.all_to_all(jnp.broadcast_to(partial_gram, (16, 8, 128)), group, 0, 0)  28.6 us
    ppermute x10, starting transfers between devices, shift(): lax.ppermute(values, axis, [(i, (i + by) % size) for i in range(size)])  16.9 us
    pallas_call x2, Pallas kernels, on_device(): pl.pallas_call(functools.partial(tile_kernel, last), out_shape=outs, in_s...  16.2 us
    ppermute x10, waiting for transfers between devices, shift(): lax.ppermute(values, axis, [(i, (i + by) % size) for i in range(size)])  15.9 us
    ppermute x5, waiting for transfers between devices, swap(): return lax.ppermute(values, axis, [(i, i ^ bit) for i in range(size)])  8.72 us
    all_to_all x1, starting transfers between devices, on_device(): far_back = lax.all_to_all(far_pair, ('x', 'y'), 0, 0)  7.48 us
    pallas_call x1, Pallas kernels, on_device(): pl.pallas_call(finish_kernel, out_shape=[jax.ShapeDtypeStruct((VEC, BS),...  4.57 us
  transfers between devices with their start and end apart: 18, of which 9 were waited for; matrix products, arithmetic and copies ran while one was open for 2% of the time, Pallas kernels for 9%

profile of v6, /device:TPU:1, one launch (start us, length us, event | category | flops | bytes accessed | tf_op | source)
XLA Modules:
  0.0 197.6 jit_solution(4920994565457134521)
XLA Ops:
  7.2 0.0 copy-start.5
  7.2 0.0 all-gather.7.cloned.1.call-start
  7.2 0.9 convert_element_type.29
  8.1 1.1 copy.19
  9.3 0.7 pad_maximum_fusion.3
  9.9 0.0 all-gather.7.cloned.1.call-update
  10.0 0.0 all-gather.5.cloned.1.call-start
  10.0 0.7 pad_maximum_fusion.2
  10.7 0.0 all-gather.5.cloned.1.call-update
  10.8 2.5 %collective-permute-start.6 = (bf16[288,512]{1,0:T(8,128)(2,1)S(1)}, bf16[288,512]{1,0:T(8,128)(2,1)S(1)}, u32[]{:S(2)}, u32[]{:S(2)}) collective-permute-start(bf16[288,512]{1,0:T(8,128)(2,1)S(1)} %pad_maximum_fusion.1.refs_0_), channel_id=1, source_target_pairs={{0,4},{4,8},{8,12},{12,16},{16,20},{20,24},{24,28},{28,0},{1,5},{5... | collective-permute-start | bytes 884744 | tf_op jit(solution)/shard_map/ppermute | solution.py:131
  13.3 4.0 %collective-permute-start.3 = (bf16[288,512]{1,0:T(8,128)(2,1)S(1)}, bf16[288,512]{1,0:T(8,128)(2,1)S(1)}, u32[]{:S(2)}, u32[]{:S(2)}) collective-permute-start(bf16[288,512]{1,0:T(8,128)(2,1)S(1)} %pad_maximum_fusion.1.refs_0_), channel_id=1, source_target_pairs={{0,28},{4,0},{8,4},{12,8},{16,12},{20,16},{24,20},{28,24},{1,29},{... | collective-permute-start | bytes 884744 | tf_op jit(solution)/shard_map/ppermute | solution.py:131
  17.3 6.6 %collective-permute-done.6.refs_7_ = bf16[288,512]{1,0:T(8,128)(2,1)S(1)} collective-permute-done((bf16[288,512]{1,0:T(8,128)(2,1)S(1)}, bf16[288,512]{1,0:T(8,128)(2,1)S(1)}, u32[]{:S(2)}, u32[]{:S(2)}) %collective-permute-start.6) | collective-permute-done | bytes 294944 | tf_op jit(solution)/shard_map/ppermute | solution.py:131
  24.0 0.0 collective-permute-start.7
  24.0 0.0 collective-permute-done.3.refs_1_
  24.0 2.7 %collective-permute-start.4 = (bf16[288,512]{1,0:T(8,128)(2,1)S(1)}, bf16[288,512]{1,0:T(8,128)(2,1)S(1)}, u32[]{:S(2)}, u32[]{:S(2)}) collective-permute-start(bf16[288,512]{1,0:T(8,128)(2,1)S(1)} %collective-permute-done.3.refs_1_), channel_id=1, source_target_pairs={{0,28},{4,0},{8,4},{12,8},{16,12},{20,16},{24,20},{28,24},{1,29},{... | collective-permute-start | bytes 884744 | tf_op jit(solution)/shard_map/ppermute | solution.py:131
  26.7 5.8 %collective-permute-done.7.refs_6_ = bf16[288,512]{1,0:T(8,128)(2,1)S(1)} collective-permute-done((bf16[288,512]{1,0:T(8,128)(2,1)S(1)}, bf16[288,512]{1,0:T(8,128)(2,1)S(1)}, u32[]{:S(2)}, u32[]{:S(2)}) %collective-permute-start.7) | collective-permute-done | bytes 294944 | tf_op jit(solution)/shard_map/ppermute | solution.py:131
  32.5 0.0 collective-permute-start.8
  32.5 0.1 copy.18
  32.5 0.1 reshape.12
  33.3 0.1 pad_add_fusion.2
  33.4 1.3 collective-permute-start
  34.7 2.6 %collective-permute-start.1 = (s32[128]{0:T(128)S(1)}, s32[128]{0:T(128)S(1)}, u32[]{:S(2)}, u32[]{:S(2)}) collective-permute-start(s32[128]{0:T(128)S(1)} %pad_add_fusion.2), channel_id=1, source_target_pairs={{0,2},{1,3},{2,0},{3,1},{4,6},{5,7},{6,4},{7,5},{8,10},{9,11},{10,... | collective-permute-start | bytes 1544 | tf_op jit(solution)/shard_map/ppermute | solution.py:131
  37.3 1.1 collective-permute-start.2
  38.4 0.0 collective-permute-done.4.refs_2_
  38.4 2.7 %collective-permute-start.5 = (bf16[288,512]{1,0:T(8,128)(2,1)S(1)}, bf16[288,512]{1,0:T(8,128)(2,1)S(1)}, u32[]{:S(2)}, u32[]{:S(2)}) collective-permute-start(bf16[288,512]{1,0:T(8,128)(2,1)S(1)} %collective-permute-done.4.refs_2_), channel_id=1, source_target_pairs={{0,28},{4,0},{8,4},{12,8},{16,12},{20,16},{24,20},{28,24},{1,29},{... | collective-permute-start | bytes 884744 | tf_op jit(solution)/shard_map/ppermute | solution.py:131
  41.1 0.0 collective-permute-done.8.refs_5_
  41.1 0.0 collective-permute-start.9
  41.1 0.1 fusion.7
  41.1 0.7 pad_add_fusion.1.place_ref
  41.8 0.0 collective-permute-done
  41.8 0.0 collective-permute-done.1
  41.8 0.0 collective-permute-done.2
  41.8 0.6 pad_add_fusion.lists_ref
  42.4 2.0 %select_pairs.1.picked_ref = s32[128]{0:T(128)} custom-call(s32[3]{0:T(128)} %pad_add_fusion.1.place_ref, s32[4,128]{1,0:T(4,128)} %pad_add_fusion.lists_ref), custom_call_target="tpu_custom_call" | custom-call | tf_op jit(solution)/shard_map/select_pairs/pallas_call | solution.py:160
  44.4 0.3 collective-permute-done.5.refs_3_
  44.7 3.1 %collective-permute-done.9.refs_4_ = bf16[288,512]{1,0:T(8,128)(2,1)S(1)} collective-permute-done((bf16[288,512]{1,0:T(8,128)(2,1)S(1)}, bf16[288,512]{1,0:T(8,128)(2,1)S(1)}, u32[]{:S(2)}, u32[]{:S(2)}) %collective-permute-start.9) | collective-permute-done | bytes 294944 | tf_op jit(solution)/shard_map/ppermute | solution.py:131
  47.9 18.8 %all-gather.7.cloned.1.call-done = bf16[9216,256]{1,0:T(8,128)(2,1)} async-done(((bf16[288,256]{1,0:T(8,128)(2,1)}), bf16[9216,256]{1,0:T(8,128)(2,1)}) %all-gather.7.cloned.1.call-update) | async-done | bytes 4718608 | tf_op jit(solution)/shard_map/all_gather | solution.py:145
  66.7 0.7 copy-done.2
  67.3 8.1 %tiles_first.1 = (f32[8,48,512]{2,1,0:T(8,128)S(1)}, f32[16,48,256]{2,1,0:T(8,128)S(1)}, bf16[16,48,256]{2,1,0:T(8,128)(2,1)}) custom-call(s32[128]{0:T(128)S(1)} %copy-done.2, bf16[32,288,256]{2,1,0:T(8,128)(2,1)} %bitcast.19, bf16[288,512]{1,0:T(8,128)(2,1)S(1)} %pad_maximum_fusion.1.refs_0_, bf16[288,512]{1,0:T(8,128)(2,1)S(1)} %collective-permute-done.3.refs_1_, ...), custom_call_target="tpu_custom_call" | custom-call | tf_op jit(solution)/shard_map/tiles_first/pallas_call | solution.py:181
  75.5 0.9 copy-done
  76.4 44.2 %all-gather.5.cloned.1.call-done = bf16[9216,256]{1,0:T(8,128)(2,1)} async-done(((bf16[288,256]{1,0:T(8,128)(2,1)}), bf16[9216,256]{1,0:T(8,128)(2,1)}) %all-gather.5.cloned.1.call-update) | async-done | bytes 4718608 | tf_op jit(solution)/shard_map/all_gather | solution.py:145
  120.6 1.1 copy-done.1
  121.7 8.1 %tiles_last.1 = (f32[4,48,512]{2,1,0:T(8,128)S(1)}, bf16[4,48,512]{2,1,0:T(8,128)(2,1)}, f32[16,48,256]{2,1,0:T(8,128)S(1)}, bf16[16,48,256]{2,1,0:T(8,128)(2,1)S(1)}) custom-call(s32[128]{0:T(128)S(1)} %copy-done.3, bf16[32,288,256]{2,1,0:T(8,128)(2,1)} %bitcast.20, bf16[288,512]{1,0:T(8,128)(2,1)S(1)} %pad_maximum_fusion.1.refs_0_, ...), custom_call_target="tpu_custom_call" | custom-call | tf_op jit(solution)/shard_map/tiles_last/pallas_call | solution.py:181
  129.8 0.1 collective-permute-start.14
  129.9 2.0 %collective-permute-start.10 = (bf16[4,48,512]{2,1,0:T(8,128)(2,1)}, bf16[4,48,512]{2,1,0:T(8,128)(2,1)S(1)}, u32[]{:S(2)}, u32[]{:S(2)}) collective-permute-start(bf16[4,48,512]{2,1,0:T(8,128)(2,1)} %get-tuple-element.11), channel_id=1, source_target_pairs={{0,4},{4,0},{8,12},{12,8},{16,20},{20,16},{24,28},{28,24},{1,5},{5... | collective-permute-start | bytes 589832 | tf_op jit(solution)/shard_map/ppermute | solution.py:135
  132.0 0.0 collective-permute-done.13
  132.0 1.1 add_convert_fusion.1
  133.1 0.0 collective-permute-done.14
  133.1 0.1 add_convert_fusion
  133.2 1.0 pad_maximum_fusion
  134.2 7.5 %all-to-all-start = ((bf16[16,48,512]{2,1,0:T(8,128)(2,1)}), bf16[16,48,512]{2,1,0:T(8,128)(2,1)S(1)}, u32[]{:S(2)}, u32[]{:S(2)}) async-start(bf16[16,48,512]{2,1,0:T(8,128)(2,1)} %pad_maximum_fusion), calls=%async_computation | async-start | bytes 1572864 | tf_op jit(solution)/shard_map/all_to_all | solution.py:205
  141.7 0.0 collective-permute-done.10
  141.7 1.0 collective-permute-start.11
  142.8 6.7 %collective-permute-done.11 = bf16[2,48,512]{2,1,0:T(8,128)(2,1)S(1)} collective-permute-done((bf16[2,48,512]{2,1,0:T(8,128)(2,1)S(1)}, bf16[2,48,512]{2,1,0:T(8,128)(2,1)S(1)}, u32[]{:S(2)}, u32[]{:S(2)}) %collective-permute-start.11) | collective-permute-done | bytes 98336 | tf_op jit(solution)/shard_map/ppermute | solution.py:135
  149.6 0.8 collective-permute-start.12
  150.4 4.0 %all-to-all-done = bf16[16,48,512]{2,1,0:T(8,128)(2,1)S(1)} async-done(((bf16[16,48,512]{2,1,0:T(8,128)(2,1)}), bf16[16,48,512]{2,1,0:T(8,128)(2,1)S(1)}, u32[]{:S(2)}, u32[]{:S(2)}) %all-to-all-start) | async-done | bytes 786464 | tf_op jit(solution)/shard_map/all_to_all | solution.py:205
  154.4 0.1 convert_reduce_fusion
  154.5 2.0 %collective-permute-done.12 = bf16[1,48,512]{2,1,0:T(8,128)(2,1)S(1)} collective-permute-done((bf16[1,48,512]{2,1,0:T(8,128)(2,1)S(1)}, bf16[1,48,512]{2,1,0:T(8,128)(2,1)S(1)}, u32[]{:S(2)}, u32[]{:S(2)}) %collective-permute-start.12) | collective-permute-done | bytes 49184 | tf_op jit(solution)/shard_map/ppermute | solution.py:135
  156.6 0.2 fusion.4
  156.8 0.1 broadcast_in_dim.17
  156.9 12.7 %all_to_all.15 = f32[16,8,128]{2,1,0:T(8,128)S(1)} all-to-all(f32[16,8,128]{2,1,0:T(8,128)S(1)} %broadcast_in_dim.18), channel_id=1, replica_groups=mesh['x'=4,'k'=2,'z'=8,'y'=4] {'x','y'}, dimensions={0} | all-to-all | bytes 131072 | tf_op jit(solution)/shard_map/all_to_all | solution.py:218
  169.6 15.9 %all_to_all.16 = f32[16,8,128]{2,1,0:T(8,128)S(1)} all-to-all(f32[16,8,128]{2,1,0:T(8,128)S(1)} %broadcast_in_dim.19), channel_id=1, replica_groups=mesh['x'=4,'k'=2,'z'=8,'y'=4] {'k','z'}, dimensions={0} | all-to-all | bytes 131072 | tf_op jit(solution)/shard_map/all_to_all | solution.py:218
  185.5 0.7 div.23.gram_ref
  186.2 4.6 %finish.1 = (f32[32,512]{1,0:T(8,128)}, f32[32,32]{1,0:T(8,128)}) custom-call(f32[32,32]{1,0:T(8,128)} %div.23.gram_ref, f32[32,512]{1,0:T(8,128)} %copy-done.4), custom_call_target="tpu_custom_call" | custom-call | tf_op jit(solution)/shard_map/finish/pallas_call | solution.py:221
  (28 shorter events, 0.3 us)
Async XLA Ops:
  7.2 3.6 %copy-start.5 = (bf16[256,512]{1,0:T(8,128)(2,1)S(1)}, bf16[256,512]{1,0:T(8,128)(2,1)}, u32[]{:S(2)}) copy-start(bf16[256,512]{1,0:T(8,128)(2,1)} %param.4) | copy-start | bytes 786436
  7.2 59.5 %all-gather.7.cloned.1.call-start = ((), (), s32[]{:S(2)}) async-start(), calls=%async_computation.4 | async-start | bytes 4866048 | tf_op jit(solution)/shard_map/all_gather | solution.py:145
  8.1 24.4 %copy-start.6 = (s32[24,2]{0,1:T(2,128)S(1)}, s32[24,2]{0,1:T(2,128)}, u32[]{:S(2)}) copy-start(s32[24,2]{0,1:T(2,128)} %param.6) | copy-start | bytes 580
  10.0 110.6 %all-gather.5.cloned.1.call-start = ((), (), s32[]{:S(2)}) async-start(), calls=%async_computation.3 | async-start | bytes 4866048 | tf_op jit(solution)/shard_map/all_gather | solution.py:145
  10.8 13.2 %collective-permute-start.6 = (bf16[288,512]{1,0:T(8,128)(2,1)S(1)}, bf16[288,512]{1,0:T(8,128)(2,1)S(1)}, u32[]{:S(2)}, u32[]{:S(2)}) collective-permute-start(bf16[288,512]{1,0:T(8,128)(2,1)S(1)} %pad_maximum_fusion.1.refs_0_), channel_id=1, source_target_pairs={{0,4},{4,8},{8,12},{12,16},{16,20},{20,24},{24,28},{28,0},{1,5},{5... | collective-permute-start | bytes 884744 | tf_op jit(solution)/shard_map/ppermute | solution.py:131
  13.3 10.7 %collective-permute-start.3 = (bf16[288,512]{1,0:T(8,128)(2,1)S(1)}, bf16[288,512]{1,0:T(8,128)(2,1)S(1)}, u32[]{:S(2)}, u32[]{:S(2)}) collective-permute-start(bf16[288,512]{1,0:T(8,128)(2,1)S(1)} %pad_maximum_fusion.1.refs_0_), channel_id=1, source_target_pairs={{0,28},{4,0},{8,4},{12,8},{16,12},{20,16},{24,20},{28,24},{1,29},{... | collective-permute-start | bytes 884744 | tf_op jit(solution)/shard_map/ppermute | solution.py:131
  24.0 8.5 %collective-permute-start.7 = (bf16[288,512]{1,0:T(8,128)(2,1)S(1)}, bf16[288,512]{1,0:T(8,128)(2,1)S(1)}, u32[]{:S(2)}, u32[]{:S(2)}) collective-permute-start(bf16[288,512]{1,0:T(8,128)(2,1)S(1)} %collective-permute-done.6.refs_7_), channel_id=1, source_target_pairs={{0,4},{4,8},{8,12},{12,16},{16,20},{20,24},{24,28},{28,0},{1,5},{5... | collective-permute-start | bytes 884744 | tf_op jit(solution)/shard_map/ppermute | solution.py:131
  24.0 14.4 %collective-permute-start.4 = (bf16[288,512]{1,0:T(8,128)(2,1)S(1)}, bf16[288,512]{1,0:T(8,128)(2,1)S(1)}, u32[]{:S(2)}, u32[]{:S(2)}) collective-permute-start(bf16[288,512]{1,0:T(8,128)(2,1)S(1)} %collective-permute-done.3.refs_1_), channel_id=1, source_target_pairs={{0,28},{4,0},{8,4},{12,8},{16,12},{20,16},{24,20},{28,24},{1,29},{... | collective-permute-start | bytes 884744 | tf_op jit(solution)/shard_map/ppermute | solution.py:131
  32.5 8.6 %collective-permute-start.8 = (bf16[288,512]{1,0:T(8,128)(2,1)S(1)}, bf16[288,512]{1,0:T(8,128)(2,1)S(1)}, u32[]{:S(2)}, u32[]{:S(2)}) collective-permute-start(bf16[288,512]{1,0:T(8,128)(2,1)S(1)} %collective-permute-done.7.refs_6_), channel_id=1, source_target_pairs={{0,4},{4,8},{8,12},{12,16},{16,20},{20,24},{24,28},{28,0},{1,5},{5... | collective-permute-start | bytes 884744 | tf_op jit(solution)/shard_map/ppermute | solution.py:131
  33.4 8.4 %collective-permute-start = (s32[128]{0:T(128)S(1)}, s32[128]{0:T(128)S(1)}, u32[]{:S(2)}, u32[]{:S(2)}) collective-permute-start(s32[128]{0:T(128)S(1)} %pad_add_fusion.2), channel_id=1, source_target_pairs={{0,1},{1,2},{2,3},{3,0},{4,5},{5,6},{6,7},{7,4},{8,9},{9,10},{10,1... | collective-permute-start | bytes 1544 | tf_op jit(solution)/shard_map/ppermute | solution.py:131
  34.7 7.1 %collective-permute-start.1 = (s32[128]{0:T(128)S(1)}, s32[128]{0:T(128)S(1)}, u32[]{:S(2)}, u32[]{:S(2)}) collective-permute-start(s32[128]{0:T(128)S(1)} %pad_add_fusion.2), channel_id=1, source_target_pairs={{0,2},{1,3},{2,0},{3,1},{4,6},{5,7},{6,4},{7,5},{8,10},{9,11},{10,... | collective-permute-start | bytes 1544 | tf_op jit(solution)/shard_map/ppermute | solution.py:131
  37.3 4.5 %collective-permute-start.2 = (s32[128]{0:T(128)S(1)}, s32[128]{0:T(128)S(1)}, u32[]{:S(2)}, u32[]{:S(2)}) collective-permute-start(s32[128]{0:T(128)S(1)} %pad_add_fusion.2), channel_id=1, source_target_pairs={{0,3},{1,0},{2,1},{3,2},{4,7},{5,4},{6,5},{7,6},{8,11},{9,8},{10,9... | collective-permute-start | bytes 1544 | tf_op jit(solution)/shard_map/ppermute | solution.py:131
  38.4 6.3 %collective-permute-start.5 = (bf16[288,512]{1,0:T(8,128)(2,1)S(1)}, bf16[288,512]{1,0:T(8,128)(2,1)S(1)}, u32[]{:S(2)}, u32[]{:S(2)}) collective-permute-start(bf16[288,512]{1,0:T(8,128)(2,1)S(1)} %collective-permute-done.4.refs_2_), channel_id=1, source_target_pairs={{0,28},{4,0},{8,4},{12,8},{16,12},{20,16},{24,20},{28,24},{1,29},{... | collective-permute-start | bytes 884744 | tf_op jit(solution)/shard_map/ppermute | solution.py:131
  41.1 6.8 %collective-permute-start.9 = (bf16[288,512]{1,0:T(8,128)(2,1)S(1)}, bf16[288,512]{1,0:T(8,128)(2,1)S(1)}, u32[]{:S(2)}, u32[]{:S(2)}) collective-permute-start(bf16[288,512]{1,0:T(8,128)(2,1)S(1)} %collective-permute-done.8.refs_5_), channel_id=1, source_target_pairs={{0,4},{4,8},{8,12},{12,16},{16,20},{20,24},{24,28},{28,0},{1,5},{5... | collective-permute-start | bytes 884744 | tf_op jit(solution)/shard_map/ppermute | solution.py:131
  66.7 0.7 copy-start.2
  67.3 53.3 %copy-start.3 = (s32[128]{0:T(128)S(1)}, s32[128]{0:T(128)}, u32[]{:S(2)}) copy-start(s32[128]{0:T(128)} %select_pairs.1.picked_ref) | copy-start | bytes 1540
  75.5 0.9 copy-start
  76.4 55.6 %collective-permute-start.13 = (bf16[16,48,256]{2,1,0:T(8,128)(2,1)}, bf16[16,48,256]{2,1,0:T(8,128)(2,1)}, u32[]{:S(2)}, u32[]{:S(2)}) collective-permute-start(bf16[16,48,256]{2,1,0:T(8,128)(2,1)} %get-tuple-element.13), channel_id=1, source_target_pairs={{0,32},{32,0},{1,33},{33,1},{2,34},{34,2},{3,35},{35,3},{4,36},{36... | collective-permute-start | bytes 1179656 | tf_op jit(solution)/shard_map/ppermute | solution.py:135
  120.6 1.1 copy-start.1
  129.8 3.2 %collective-permute-start.14 = (bf16[16,48,256]{2,1,0:T(8,128)(2,1)S(1)}, bf16[16,48,256]{2,1,0:T(8,128)(2,1)S(1)}, u32[]{:S(2)}, u32[]{:S(2)}) collective-permute-start(bf16[16,48,256]{2,1,0:T(8,128)(2,1)S(1)} %get-tuple-element.15), channel_id=1, source_target_pairs={{0,32},{32,0},{1,33},{33,1},{2,34},{34,2},{3,35},{35,3},{4,36},{36... | collective-permute-start | bytes 1179656 | tf_op jit(solution)/shard_map/ppermute | solution.py:135
  129.9 11.7 %collective-permute-start.10 = (bf16[4,48,512]{2,1,0:T(8,128)(2,1)}, bf16[4,48,512]{2,1,0:T(8,128)(2,1)S(1)}, u32[]{:S(2)}, u32[]{:S(2)}) collective-permute-start(bf16[4,48,512]{2,1,0:T(8,128)(2,1)} %get-tuple-element.11), channel_id=1, source_target_pairs={{0,4},{4,0},{8,12},{12,8},{16,20},{20,16},{24,28},{28,24},{1,5},{5... | collective-permute-start | bytes 589832 | tf_op jit(solution)/shard_map/ppermute | solution.py:135
  134.2 20.2 %all-to-all-start = ((bf16[16,48,512]{2,1,0:T(8,128)(2,1)}), bf16[16,48,512]{2,1,0:T(8,128)(2,1)S(1)}, u32[]{:S(2)}, u32[]{:S(2)}) async-start(bf16[16,48,512]{2,1,0:T(8,128)(2,1)} %pad_maximum_fusion), calls=%async_computation | async-start | bytes 1572864 | tf_op jit(solution)/shard_map/all_to_all | solution.py:205
  141.7 7.8 %collective-permute-start.11 = (bf16[2,48,512]{2,1,0:T(8,128)(2,1)S(1)}, bf16[2,48,512]{2,1,0:T(8,128)(2,1)S(1)}, u32[]{:S(2)}, u32[]{:S(2)}) collective-permute-start(bf16[2,48,512]{2,1,0:T(8,128)(2,1)S(1)} %slice.61), channel_id=1, source_target_pairs={{0,8},{4,12},{8,0},{12,4},{16,24},{20,28},{24,16},{28,20},{1,9},{5... | collective-permute-start | bytes 294920 | tf_op jit(solution)/shard_map/ppermute | solution.py:135
  149.6 7.0 %collective-permute-start.12 = (bf16[1,48,512]{2,1,0:T(8,128)(2,1)S(1)}, bf16[1,48,512]{2,1,0:T(8,128)(2,1)S(1)}, u32[]{:S(2)}, u32[]{:S(2)}) collective-permute-start(bf16[1,48,512]{2,1,0:T(8,128)(2,1)S(1)} %slice.62), channel_id=1, source_target_pairs={{0,16},{4,20},{8,24},{12,28},{16,0},{20,4},{24,8},{28,12},{1,17},{... | collective-permute-start | bytes 147464 | tf_op jit(solution)/shard_map/ppermute | solution.py:135
  156.6 29.6 %copy-start.4 = (f32[32,512]{1,0:T(8,128)}, f32[32,512]{1,0:T(8,128)S(1)}, u32[]{:S(2)}) copy-start(f32[32,512]{1,0:T(8,128)S(1)} %slice_divide_fusion.walked_ref) | copy-start | bytes 196612
Sparse Core Ops, SparseCore 0:
  10.6 56.0 all-gather.6
  69.3 51.2 all-gather.4

commit v7 on v5

--- a/solution.py
+++ b/solution.py
@@ -19,6 +19,8 @@
 AUG = 48
 MAXP = 24
 SLOTS = 128
+PAIR = 2
+AHEAD = 2
 
 
 def select_kernel(place_ref, lists_ref, picked_ref):
@@ -49,44 +51,82 @@
 def tile_kernel(picked_ref, far_hbm, *refs):
     near_hbm = refs[:Z]
     near_keep, near_give, far_keep, far_give, near_ref, far_ref, near_sum, far_sum, sems = refs[Z:]
-    copies = [pltpu.make_async_copy(far_hbm, far_ref, sems.at[Z])]
-    for slot in range(Z):
-        copies.append(pltpu.make_async_copy(near_hbm[slot], near_ref.at[slot], sems.at[slot]))
+    found = picked_ref[0]
+
+    def code_of(number):
+        return jnp.where(number < found, picked_ref[number + 1], 0)
+
+    def fetches(step):
+        ring = lax.rem(step, AHEAD + 1) * PAIR
+        return [
+            pltpu.make_async_copy(
+                far_hbm.at[code_of(step * PAIR + lane) & 31],
+                far_ref.at[ring + lane],
+                sems.at[Z + ring + lane],
+            )
+            for lane in range(PAIR)
+        ]
+
+    copies = [
+        pltpu.make_async_copy(near_hbm[slot], near_ref.at[slot], sems.at[slot]) for slot in range(Z)
+    ]
     for copy in copies:
         copy.start()
+    for step in range(AHEAD):
+        for copy in fetches(jnp.int32(step)):
+            copy.start()
     near_sum[...] = jnp.zeros_like(near_sum)
     far_sum[...] = jnp.zeros_like(far_sum)
     ones = (lax.broadcasted_iota(jnp.int32, (AUG - VEC, BS), 0) == 0).astype(jnp.bfloat16)
     for copy in copies:
         copy.wait()
 
-    def each_tile(number, carry):
-        code = picked_ref[number + 1]
-        far = code & 31
+    def one_tile(step, lane):
+        number = step * PAIR + lane
+        live = number < found
+        code = code_of(number)
+        far = lax.rem(step, AHEAD + 1) * PAIR + lane
         home = (code >> 5) & 31
         near = (code >> 10) & 7
         back = (code >> 13) & 7
-        mirror = jnp.where((code >> 16) == 1, 0.0, 1.0).astype(jnp.float32)
+        keep = jnp.where(live, 1.0, 0.0).astype(jnp.float32)
+        mirror = jnp.where(live & ((code >> 16) == 0), 1.0, 0.0).astype(jnp.float32)
         far_embed = far_ref[far, :EMB, :]
         near_vec = jnp.concatenate([near_ref[near, EMB:, :], ones], axis=0)
         far_vec = jnp.concatenate([far_ref[far, EMB:, :], ones], axis=0)
-        far_terms = None
-        for half in range(2):
-            cut = slice(half * 256, half * 256 + 256)
-            scores = jnp.dot(
-                near_ref[near, :EMB, cut], far_embed, preferred_element_type=jnp.float32
-            )
-            tile = (0.5 * jnp.tanh(scores) + 0.5).astype(jnp.bfloat16)
-            near_terms = lax.dot_general(
-                far_vec, tile, (((1,), (1,)), ((), ())), preferred_element_type=jnp.float32
-            )
-            near_sum[back, :, cut] += near_terms
-            part = jnp.dot(near_vec[:, cut], tile, preferred_element_type=jnp.float32)
-            far_terms = part if far_terms is None else far_terms + part
-        far_sum[home] += far_terms * mirror
+        scores = jnp.concatenate(
+            [
+                jnp.dot(
+                    near_ref[near, :EMB, half * 256 : half * 256 + 256],
+                    far_embed,
+                    preferred_element_type=jnp.float32,
+                )
+                for half in range(2)
+            ],
+            axis=0,
+        )
+        tile = (0.5 * jnp.tanh(scores) + 0.5).astype(jnp.bfloat16)
+        near_terms = lax.dot_general(
+            far_vec, tile, (((1,), (1,)), ((), ())), preferred_element_type=jnp.float32
+        )
+        far_terms = jnp.dot(near_vec, tile, preferred_element_type=jnp.float32)
+        return back, near_terms * keep, home, far_terms * mirror
+
+    def each_step(step, carry):
+        for copy in fetches(step + AHEAD):
+            copy.start()
+        for copy in fetches(step):
+            copy.wait()
+        for back, near_terms, home, far_terms in [one_tile(step, lane) for lane in range(PAIR)]:
+            near_sum[back] += near_terms
+            far_sum[home] += far_terms
         return carry
 
-    lax.fori_loop(0, picked_ref[0], each_tile, 0)
+    steps = lax.div(found + PAIR - 1, PAIR)
+    lax.fori_loop(0, steps, each_step, 0)
+    for late in range(AHEAD):
+        for copy in fetches(steps + late):
+            copy.wait()
     near_keep[...] = near_sum[: Z // 2]
     near_give[...] = near_sum[Z // 2 :].astype(jnp.bfloat16)
     far_keep[...] = far_sum[: X * Y]
@@ -173,10 +213,10 @@
         out_specs=[vmem] * 4,
         scratch_shapes=[
             pltpu.VMEM((Z, EMB + VEC, BS), jnp.bfloat16),
-            pltpu.VMEM((FARS, EMB + VEC, BS), jnp.bfloat16),
+            pltpu.VMEM((PAIR * (AHEAD + 1), EMB + VEC, BS), jnp.bfloat16),
             pltpu.VMEM((Z, AUG, BS), jnp.float32),
             pltpu.VMEM((FARS, AUG, BS), jnp.float32),
-            pltpu.SemaphoreType.DMA((Z + 1,)),
+            pltpu.SemaphoreType.DMA((Z + PAIR * (AHEAD + 1),)),
         ],
         compiler_params=pltpu.CompilerParams(vmem_limit_bytes=48 * 1024 * 1024),
         name="tiles",

time: 161 us -> 155 us (0.963)
  Pallas kernels: 23.8 us -> 18.6 us
  starting transfers between devices: 38.3 us -> 34.2 us
  waiting for transfers between devices: 46.9 us -> 48.7 us
    ppermute x4, starting transfers between devices: 17.1 us -> 9.32 us  [swap(): return lax.ppermute(values, axis, [(i, i ^ bit) for i in range(size)])]
    pallas_call x1, Pallas kernels: 16.6 us -> 11.5 us  [on_device(): pl.pallas_call(tile_kernel, out_shape=[jax.ShapeDtypeStruct((Z // 2, AUG,...]
    all_to_all x1, starting transfers between devices: 3.61 us -> 7.33 us  [on_device(): far_back = lax.all_to_all(far_pair, ('x', 'y'), 0, 0)]
  transfers between devices with their start and end apart: 16 -> 16, of which waited for: 7 -> 8; matrix products, arithmetic and copies ran while one was open for 2% -> 2% of each run, Pallas kernels for 2% -> 2%
where the time goes in v7:
time: 155 us; the launch traced here: 154 us
  waiting for transfers between devices  48.7 us (31%)
  starting transfers between devices  34.2 us (22%)
  blocking collectives  30.4 us (20%)
  Pallas kernels  18.6 us (12%)
  between operations  14.9 us (10%)
  other arithmetic  4.55 us (3%)
  local copies, waits for them, and re-layouts  2.75 us (2%)
    all_to_all x2, blocking collectives, on_device(): lax.all_to_all(jnp.broadcast_to(partial_gram, (16, 8, 128)), group, 0, 0)  30.4 us
    all_gather x1, waiting for transfers between devices, on_device(): far_all = lax.all_gather(far_send, FAR)  27.4 us
    ppermute x10, starting transfers between devices, shift(): lax.ppermute(values, axis, [(i, (i + by) % size) for i in range(size)])  17.5 us
    ppermute x10, waiting for transfers between devices, shift(): lax.ppermute(values, axis, [(i, (i + by) % size) for i in range(size)])  15.4 us
    pallas_call x1, Pallas kernels, on_device(): pl.pallas_call(tile_kernel, out_shape=[jax.ShapeDtypeStruct((Z // 2, AUG,...  11.5 us
    ppermute x4, starting transfers between devices, swap(): return lax.ppermute(values, axis, [(i, i ^ bit) for i in range(size)])  9.32 us
    all_to_all x1, starting transfers between devices, on_device(): far_back = lax.all_to_all(far_pair, ('x', 'y'), 0, 0)  7.33 us
    pallas_call x1, Pallas kernels, on_device(): pl.pallas_call(finish_kernel, out_shape=[jax.ShapeDtypeStruct((VEC, BS),...  4.57 us
  transfers between devices with their start and end apart: 16, of which 8 were waited for; matrix products, arithmetic and copies ran while one was open for 2% of the time, Pallas kernels for 2%

profile of v7, /device:TPU:1, one launch (start us, length us, event | category | flops | bytes accessed | tf_op | source)
XLA Modules:
  0.0 154.3 jit_solution(12633696323760242036)
XLA Ops:
  7.2 0.0 copy-start.2
  7.2 0.0 copy-start.3
  7.2 0.0 all-gather.3.cloned.1.call-start
  7.2 0.9 convert_element_type.23
  8.1 1.1 copy.11
  9.3 0.0 copy-done.2
  9.3 0.7 pad_maximum_fusion
  10.0 0.0 all-gather.3.cloned.1.call-update
  10.1 2.5 %collective-permute-start.6 = (bf16[288,512]{1,0:T(8,128)(2,1)S(1)}, bf16[288,512]{1,0:T(8,128)(2,1)S(1)}, u32[]{:S(2)}, u32[]{:S(2)}) collective-permute-start(bf16[288,512]{1,0:T(8,128)(2,1)S(1)} %get-tuple-element.12.refs_0_), channel_id=1, source_target_pairs={{0,4},{4,8},{8,12},{12,16},{16,20},{20,24},{24,28},{28,0},{1,5},{5... | collective-permute-start | bytes 884744 | tf_op jit(solution)/shard_map/ppermute | solution.py:163
  12.6 4.0 %collective-permute-start.3 = (bf16[288,512]{1,0:T(8,128)(2,1)S(1)}, bf16[288,512]{1,0:T(8,128)(2,1)S(1)}, u32[]{:S(2)}, u32[]{:S(2)}) collective-permute-start(bf16[288,512]{1,0:T(8,128)(2,1)S(1)} %get-tuple-element.12.refs_0_), channel_id=1, source_target_pairs={{0,28},{4,0},{8,4},{12,8},{16,12},{20,16},{24,20},{28,24},{1,29},{... | collective-permute-start | bytes 884744 | tf_op jit(solution)/shard_map/ppermute | solution.py:163
  16.6 6.6 %collective-permute-done.6.refs_7_ = bf16[288,512]{1,0:T(8,128)(2,1)S(1)} collective-permute-done((bf16[288,512]{1,0:T(8,128)(2,1)S(1)}, bf16[288,512]{1,0:T(8,128)(2,1)S(1)}, u32[]{:S(2)}, u32[]{:S(2)}) %collective-permute-start.6) | collective-permute-done | bytes 294944 | tf_op jit(solution)/shard_map/ppermute | solution.py:163
  23.3 0.0 collective-permute-start.7
  23.3 0.0 collective-permute-done.3.refs_1_
  23.3 2.7 %collective-permute-start.4 = (bf16[288,512]{1,0:T(8,128)(2,1)S(1)}, bf16[288,512]{1,0:T(8,128)(2,1)S(1)}, u32[]{:S(2)}, u32[]{:S(2)}) collective-permute-start(bf16[288,512]{1,0:T(8,128)(2,1)S(1)} %collective-permute-done.3.refs_1_), channel_id=1, source_target_pairs={{0,28},{4,0},{8,4},{12,8},{16,12},{20,16},{24,20},{28,24},{1,29},{... | collective-permute-start | bytes 884744 | tf_op jit(solution)/shard_map/ppermute | solution.py:163
  26.0 5.9 %collective-permute-done.7.refs_6_ = bf16[288,512]{1,0:T(8,128)(2,1)S(1)} collective-permute-done((bf16[288,512]{1,0:T(8,128)(2,1)S(1)}, bf16[288,512]{1,0:T(8,128)(2,1)S(1)}, u32[]{:S(2)}, u32[]{:S(2)}) %collective-permute-start.7) | collective-permute-done | bytes 294944 | tf_op jit(solution)/shard_map/ppermute | solution.py:163
  31.9 0.0 collective-permute-start.8
  32.5 0.0 copy-done.3
  32.5 0.1 copy.10
  32.6 0.1 reshape.12
  32.7 0.1 pad_add_fusion.2
  32.8 2.9 %collective-permute-start.1 = (s32[128]{0:T(128)S(1)}, s32[128]{0:T(128)S(1)}, u32[]{:S(2)}, u32[]{:S(2)}) collective-permute-start(s32[128]{0:T(128)S(1)} %pad_add_fusion.2), channel_id=1, source_target_pairs={{0,2},{1,3},{2,0},{3,1},{4,6},{5,7},{6,4},{7,5},{8,10},{9,11},{10,... | collective-permute-start | bytes 1544 | tf_op jit(solution)/shard_map/ppermute | solution.py:163
  35.7 0.4 collective-permute-start
  36.1 2.3 %collective-permute-start.2 = (s32[128]{0:T(128)S(1)}, s32[128]{0:T(128)S(1)}, u32[]{:S(2)}, u32[]{:S(2)}) collective-permute-start(s32[128]{0:T(128)S(1)} %pad_add_fusion.2), channel_id=1, source_target_pairs={{0,3},{1,0},{2,1},{3,2},{4,7},{5,4},{6,5},{7,6},{8,11},{9,8},{10,9... | collective-permute-start | bytes 1544 | tf_op jit(solution)/shard_map/ppermute | solution.py:163
  38.4 0.0 collective-permute-done.4.refs_2_
  38.4 2.7 %collective-permute-start.5 = (bf16[288,512]{1,0:T(8,128)(2,1)S(1)}, bf16[288,512]{1,0:T(8,128)(2,1)S(1)}, u32[]{:S(2)}, u32[]{:S(2)}) collective-permute-start(bf16[288,512]{1,0:T(8,128)(2,1)S(1)} %collective-permute-done.4.refs_2_), channel_id=1, source_target_pairs={{0,28},{4,0},{8,4},{12,8},{16,12},{20,16},{24,20},{28,24},{1,29},{... | collective-permute-start | bytes 884744 | tf_op jit(solution)/shard_map/ppermute | solution.py:163
  41.1 0.0 collective-permute-done.8.refs_5_
  41.1 0.0 collective-permute-start.9
  41.1 0.1 fusion.6
  41.2 0.7 pad_add_fusion.1.place_ref
  41.8 0.0 collective-permute-done.1
  41.8 0.0 collective-permute-done
  41.8 0.0 collective-permute-done.2
  41.9 0.6 pad_add_fusion.lists_ref
  42.4 2.6 %select_pairs.1.picked_ref = s32[128]{0:T(128)} custom-call(s32[3]{0:T(128)} %pad_add_fusion.1.place_ref, s32[4,128]{1,0:T(4,128)} %pad_add_fusion.lists_ref), custom_call_target="tpu_custom_call" | custom-call | tf_op jit(solution)/shard_map/select_pairs/pallas_call | solution.py:197
  45.0 0.0 collective-permute-done.5.refs_3_
  45.1 2.8 %collective-permute-done.9.refs_4_ = bf16[288,512]{1,0:T(8,128)(2,1)S(1)} collective-permute-done((bf16[288,512]{1,0:T(8,128)(2,1)S(1)}, bf16[288,512]{1,0:T(8,128)(2,1)S(1)}, u32[]{:S(2)}, u32[]{:S(2)}) %collective-permute-start.9) | collective-permute-done | bytes 294944 | tf_op jit(solution)/shard_map/ppermute | solution.py:163
  47.9 27.4 %all-gather.3.cloned.1.call-done = bf16[9216,512]{1,0:T(8,128)(2,1)} async-done(((bf16[288,512]{1,0:T(8,128)(2,1)}), bf16[9216,512]{1,0:T(8,128)(2,1)}) %all-gather.3.cloned.1.call-update) | async-done | bytes 9437200 | tf_op jit(solution)/shard_map/all_gather | solution.py:174
  75.3 0.0 copy-start
  75.3 0.7 copy-done
  76.0 11.5 %tiles.1 = (f32[4,48,512]{2,1,0:T(8,128)S(1)}, bf16[4,48,512]{2,1,0:T(8,128)(2,1)S(1)}, f32[16,48,512]{2,1,0:T(8,128)S(1)}, bf16[16,48,512]{2,1,0:T(8,128)(2,1)S(1)}) custom-call(s32[128]{0:T(128)S(1)} %copy-done, bf16[32,288,512]{2,1,0:T(8,128)(2,1)} %bitcast.17, bf16[288,512]{1,0:T(8,128)(2,1)S(1)} %get-tuple-element.12.refs_0_, ...), custom_call_target="tpu_custom_call" | custom-call | tf_op jit(solution)/shard_map/tiles/pallas_call | solution.py:204
  87.4 0.3 collective-permute-start.13
  87.8 1.1 collective-permute-start.10
  88.9 0.9 collective-permute-done.13
  89.8 1.2 add_convert_fusion
  91.0 7.3 %all-to-all-start = ((bf16[16,48,512]{2,1,0:T(8,128)(2,1)}), bf16[16,48,512]{2,1,0:T(8,128)(2,1)S(1)}, u32[]{:S(2)}, u32[]{:S(2)}) async-start(bf16[16,48,512]{2,1,0:T(8,128)(2,1)} %add_convert_fusion), calls=%async_computation | async-start | bytes 1572864 | tf_op jit(solution)/shard_map/all_to_all | solution.py:226
  98.4 0.0 collective-permute-done.10
  98.4 0.1 convert_add_fusion
  98.5 1.2 collective-permute-start.11
  99.6 3.3 %collective-permute-done.11 = bf16[2,48,512]{2,1,0:T(8,128)(2,1)S(1)} collective-permute-done((bf16[2,48,512]{2,1,0:T(8,128)(2,1)S(1)}, bf16[2,48,512]{2,1,0:T(8,128)(2,1)S(1)}, u32[]{:S(2)}, u32[]{:S(2)}) %collective-permute-start.11) | collective-permute-done | bytes 98336 | tf_op jit(solution)/shard_map/ppermute | solution.py:167
  103.0 6.7 %collective-permute-start.12 = (bf16[1,48,512]{2,1,0:T(8,128)(2,1)S(1)}, bf16[1,48,512]{2,1,0:T(8,128)(2,1)S(1)}, u32[]{:S(2)}, u32[]{:S(2)}) collective-permute-start(bf16[1,48,512]{2,1,0:T(8,128)(2,1)S(1)} %slice.52), channel_id=1, source_target_pairs={{0,16},{4,20},{8,24},{12,28},{16,0},{20,4},{24,8},{28,12},{1,17},{... | collective-permute-start | bytes 147464 | tf_op jit(solution)/shard_map/ppermute | solution.py:167
  109.6 1.5 all-to-all-done
  111.1 0.1 convert_reduce_fusion
  111.2 0.2 collective-permute-done.12
  111.5 0.0 copy-start.1
  111.5 0.2 fusion.3
  111.7 0.1 broadcast_in_dim.17
  111.7 11.5 %all_to_all.15 = f32[16,8,128]{2,1,0:T(8,128)S(1)} all-to-all(f32[16,8,128]{2,1,0:T(8,128)S(1)} %broadcast_in_dim.18), channel_id=1, replica_groups=mesh['x'=4,'k'=2,'z'=8,'y'=4] {'x','y'}, dimensions={0} | all-to-all | bytes 131072 | tf_op jit(solution)/shard_map/all_to_all | solution.py:239
  123.2 19.0 %all_to_all.16 = f32[16,8,128]{2,1,0:T(8,128)S(1)} all-to-all(f32[16,8,128]{2,1,0:T(8,128)S(1)} %broadcast_in_dim.19), channel_id=1, replica_groups=mesh['x'=4,'k'=2,'z'=8,'y'=4] {'k','z'}, dimensions={0} | all-to-all | bytes 131072 | tf_op jit(solution)/shard_map/all_to_all | solution.py:239
  142.2 0.7 div.23.gram_ref
  142.9 0.0 copy-done.1
  142.9 4.6 %finish.1 = (f32[32,512]{1,0:T(8,128)}, f32[32,32]{1,0:T(8,128)}) custom-call(f32[32,32]{1,0:T(8,128)} %div.23.gram_ref, f32[32,512]{1,0:T(8,128)} %copy-done.1), custom_call_target="tpu_custom_call" | custom-call | tf_op jit(solution)/shard_map/finish/pallas_call | solution.py:242
  (14 shorter events, 0.2 us)
Async XLA Ops:
  7.2 2.1 %copy-start.2 = (bf16[256,512]{1,0:T(8,128)(2,1)S(1)}, bf16[256,512]{1,0:T(8,128)(2,1)}, u32[]{:S(2)}) copy-start(bf16[256,512]{1,0:T(8,128)(2,1)} %param.4) | copy-start | bytes 786436
  7.2 25.4 %copy-start.3 = (s32[24,2]{0,1:T(2,128)S(1)}, s32[24,2]{0,1:T(2,128)}, u32[]{:S(2)}) copy-start(s32[24,2]{0,1:T(2,128)} %param.6) | copy-start | bytes 580
  7.2 68.1 %all-gather.3.cloned.1.call-start = ((), (), s32[]{:S(2)}) async-start(), calls=%async_computation.3 | async-start | bytes 9732096 | tf_op jit(solution)/shard_map/all_gather | solution.py:174
  10.1 13.2 %collective-permute-start.6 = (bf16[288,512]{1,0:T(8,128)(2,1)S(1)}, bf16[288,512]{1,0:T(8,128)(2,1)S(1)}, u32[]{:S(2)}, u32[]{:S(2)}) collective-permute-start(bf16[288,512]{1,0:T(8,128)(2,1)S(1)} %get-tuple-element.12.refs_0_), channel_id=1, source_target_pairs={{0,4},{4,8},{8,12},{12,16},{16,20},{20,24},{24,28},{28,0},{1,5},{5... | collective-permute-start | bytes 884744 | tf_op jit(solution)/shard_map/ppermute | solution.py:163
  12.6 10.7 %collective-permute-start.3 = (bf16[288,512]{1,0:T(8,128)(2,1)S(1)}, bf16[288,512]{1,0:T(8,128)(2,1)S(1)}, u32[]{:S(2)}, u32[]{:S(2)}) collective-permute-start(bf16[288,512]{1,0:T(8,128)(2,1)S(1)} %get-tuple-element.12.refs_0_), channel_id=1, source_target_pairs={{0,28},{4,0},{8,4},{12,8},{16,12},{20,16},{24,20},{28,24},{1,29},{... | collective-permute-start | bytes 884744 | tf_op jit(solution)/shard_map/ppermute | solution.py:163
  23.3 8.6 %collective-permute-start.7 = (bf16[288,512]{1,0:T(8,128)(2,1)S(1)}, bf16[288,512]{1,0:T(8,128)(2,1)S(1)}, u32[]{:S(2)}, u32[]{:S(2)}) collective-permute-start(bf16[288,512]{1,0:T(8,128)(2,1)S(1)} %collective-permute-done.6.refs_7_), channel_id=1, source_target_pairs={{0,4},{4,8},{8,12},{12,16},{16,20},{20,24},{24,28},{28,0},{1,5},{5... | collective-permute-start | bytes 884744 | tf_op jit(solution)/shard_map/ppermute | solution.py:163
  23.3 15.1 %collective-permute-start.4 = (bf16[288,512]{1,0:T(8,128)(2,1)S(1)}, bf16[288,512]{1,0:T(8,128)(2,1)S(1)}, u32[]{:S(2)}, u32[]{:S(2)}) collective-permute-start(bf16[288,512]{1,0:T(8,128)(2,1)S(1)} %collective-permute-done.3.refs_1_), channel_id=1, source_target_pairs={{0,28},{4,0},{8,4},{12,8},{16,12},{20,16},{24,20},{28,24},{1,29},{... | collective-permute-start | bytes 884744 | tf_op jit(solution)/shard_map/ppermute | solution.py:163
  31.9 9.2 %collective-permute-start.8 = (bf16[288,512]{1,0:T(8,128)(2,1)S(1)}, bf16[288,512]{1,0:T(8,128)(2,1)S(1)}, u32[]{:S(2)}, u32[]{:S(2)}) collective-permute-start(bf16[288,512]{1,0:T(8,128)(2,1)S(1)} %collective-permute-done.7.refs_6_), channel_id=1, source_target_pairs={{0,4},{4,8},{8,12},{12,16},{16,20},{20,24},{24,28},{28,0},{1,5},{5... | collective-permute-start | bytes 884744 | tf_op jit(solution)/shard_map/ppermute | solution.py:163
  32.8 9.0 %collective-permute-start.1 = (s32[128]{0:T(128)S(1)}, s32[128]{0:T(128)S(1)}, u32[]{:S(2)}, u32[]{:S(2)}) collective-permute-start(s32[128]{0:T(128)S(1)} %pad_add_fusion.2), channel_id=1, source_target_pairs={{0,2},{1,3},{2,0},{3,1},{4,6},{5,7},{6,4},{7,5},{8,10},{9,11},{10,... | collective-permute-start | bytes 1544 | tf_op jit(solution)/shard_map/ppermute | solution.py:163
  35.7 6.1 %collective-permute-start = (s32[128]{0:T(128)S(1)}, s32[128]{0:T(128)S(1)}, u32[]{:S(2)}, u32[]{:S(2)}) collective-permute-start(s32[128]{0:T(128)S(1)} %pad_add_fusion.2), channel_id=1, source_target_pairs={{0,1},{1,2},{2,3},{3,0},{4,5},{5,6},{6,7},{7,4},{8,9},{9,10},{10,1... | collective-permute-start | bytes 1544 | tf_op jit(solution)/shard_map/ppermute | solution.py:163
  36.1 5.7 %collective-permute-start.2 = (s32[128]{0:T(128)S(1)}, s32[128]{0:T(128)S(1)}, u32[]{:S(2)}, u32[]{:S(2)}) collective-permute-start(s32[128]{0:T(128)S(1)} %pad_add_fusion.2), channel_id=1, source_target_pairs={{0,3},{1,0},{2,1},{3,2},{4,7},{5,4},{6,5},{7,6},{8,11},{9,8},{10,9... | collective-permute-start | bytes 1544 | tf_op jit(solution)/shard_map/ppermute | solution.py:163
  38.4 6.6 %collective-permute-start.5 = (bf16[288,512]{1,0:T(8,128)(2,1)S(1)}, bf16[288,512]{1,0:T(8,128)(2,1)S(1)}, u32[]{:S(2)}, u32[]{:S(2)}) collective-permute-start(bf16[288,512]{1,0:T(8,128)(2,1)S(1)} %collective-permute-done.4.refs_2_), channel_id=1, source_target_pairs={{0,28},{4,0},{8,4},{12,8},{16,12},{20,16},{24,20},{28,24},{1,29},{... | collective-permute-start | bytes 884744 | tf_op jit(solution)/shard_map/ppermute | solution.py:163
  41.1 6.8 %collective-permute-start.9 = (bf16[288,512]{1,0:T(8,128)(2,1)S(1)}, bf16[288,512]{1,0:T(8,128)(2,1)S(1)}, u32[]{:S(2)}, u32[]{:S(2)}) collective-permute-start(bf16[288,512]{1,0:T(8,128)(2,1)S(1)} %collective-permute-done.8.refs_5_), channel_id=1, source_target_pairs={{0,4},{4,8},{8,12},{12,16},{16,20},{20,24},{24,28},{28,0},{1,5},{5... | collective-permute-start | bytes 884744 | tf_op jit(solution)/shard_map/ppermute | solution.py:163
  75.3 0.7 copy-start
  87.4 2.4 %collective-permute-start.13 = (bf16[16,48,512]{2,1,0:T(8,128)(2,1)S(1)}, bf16[16,48,512]{2,1,0:T(8,128)(2,1)S(1)}, u32[]{:S(2)}, u32[]{:S(2)}) collective-permute-start(bf16[16,48,512]{2,1,0:T(8,128)(2,1)S(1)} %get-tuple-element.9), channel_id=1, source_target_pairs={{0,32},{32,0},{1,33},{33,1},{2,34},{34,2},{3,35},{35,3},{4,36},{36... | collective-permute-start | bytes 2359304 | tf_op jit(solution)/shard_map/ppermute | solution.py:167
  87.8 10.6 %collective-permute-start.10 = (bf16[4,48,512]{2,1,0:T(8,128)(2,1)S(1)}, bf16[4,48,512]{2,1,0:T(8,128)(2,1)S(1)}, u32[]{:S(2)}, u32[]{:S(2)}) collective-permute-start(bf16[4,48,512]{2,1,0:T(8,128)(2,1)S(1)} %get-tuple-element.7), channel_id=1, source_target_pairs={{0,4},{4,0},{8,12},{12,8},{16,20},{20,16},{24,28},{28,24},{1,5},{5... | collective-permute-start | bytes 589832 | tf_op jit(solution)/shard_map/ppermute | solution.py:167
  91.0 20.1 %all-to-all-start = ((bf16[16,48,512]{2,1,0:T(8,128)(2,1)}), bf16[16,48,512]{2,1,0:T(8,128)(2,1)S(1)}, u32[]{:S(2)}, u32[]{:S(2)}) async-start(bf16[16,48,512]{2,1,0:T(8,128)(2,1)} %add_convert_fusion), calls=%async_computation | async-start | bytes 1572864 | tf_op jit(solution)/shard_map/all_to_all | solution.py:226
  98.5 4.5 %collective-permute-start.11 = (bf16[2,48,512]{2,1,0:T(8,128)(2,1)S(1)}, bf16[2,48,512]{2,1,0:T(8,128)(2,1)S(1)}, u32[]{:S(2)}, u32[]{:S(2)}) collective-permute-start(bf16[2,48,512]{2,1,0:T(8,128)(2,1)S(1)} %slice.51), channel_id=1, source_target_pairs={{0,8},{4,12},{8,0},{12,4},{16,24},{20,28},{24,16},{28,20},{1,9},{5... | collective-permute-start | bytes 294920 | tf_op jit(solution)/shard_map/ppermute | solution.py:167
  103.0 8.4 %collective-permute-start.12 = (bf16[1,48,512]{2,1,0:T(8,128)(2,1)S(1)}, bf16[1,48,512]{2,1,0:T(8,128)(2,1)S(1)}, u32[]{:S(2)}, u32[]{:S(2)}) collective-permute-start(bf16[1,48,512]{2,1,0:T(8,128)(2,1)S(1)} %slice.52), channel_id=1, source_target_pairs={{0,16},{4,20},{8,24},{12,28},{16,0},{20,4},{24,8},{28,12},{1,17},{... | collective-permute-start | bytes 147464 | tf_op jit(solution)/shard_map/ppermute | solution.py:167
  111.5 31.4 %copy-start.1 = (f32[32,512]{1,0:T(8,128)}, f32[32,512]{1,0:T(8,128)S(1)}, u32[]{:S(2)}) copy-start(f32[32,512]{1,0:T(8,128)S(1)} %slice_divide_fusion.walked_ref) | copy-start | bytes 196612
Sparse Core Ops, SparseCore 0:
  10.6 64.6 all-gather.2

commit v8 on v7

--- a/solution.py
+++ b/solution.py
@@ -10,8 +10,9 @@
 from jax.sharding import PartitionSpec as P
 
 X, K, Z, Y = 4, 2, 8, 4
-FAR = ("x", "k", "y")
-EVERY = ("x", "k", "z", "y")
+AXIS_Y = ("h", "l")
+FAR = ("x", "k", "l")
+EVERY = ("x", "k", "z", "h", "l")
 FARS = X * K * Y
 BS = 512
 EMB = 256
@@ -37,7 +38,8 @@
             apart = row_z ^ own_z
             back = (apart & 1) * 4 + (apart & 2) + (apart >> 2)
             col_row = col_block >> 5
-            far = col_row * Y + (col_block & 3)
+            col_y = col_block & 3
+            far = col_row * Y + (col_y & 1) * 2 + ((col_y >> 1) ^ (own_y >> 1))
             home = ((col_row & 1) ^ own_k) * (X * Y) + (col_row >> 1) * Y + (col_block & 3)
             same = (row_block == col_block).astype(jnp.int32)
             picked_ref[found + 1] = (((same * 8 + back) * 8 + near) * FARS + home) * FARS + far
@@ -171,7 +173,8 @@
     score_scale = 0.5 / math.sqrt(EMB)
     vector_bf16 = vectors.astype(jnp.bfloat16)
     far_send = lax.optimization_barrier(jnp.concatenate([embeddings, vector_bf16], axis=0))
-    far_all = lax.all_gather(far_send, FAR)
+    far_two = jnp.stack([far_send, swap(far_send, "h", 2, 1)])
+    far_all = lax.all_gather(far_two, FAR).reshape((FARS,) + far_send.shape)
     turned = embeddings.T
     near_send = jnp.concatenate(
         [
@@ -190,8 +193,8 @@
     own_list = jnp.concatenate(
         [block_pairs.reshape(-1), counts, jnp.zeros((128 - 2 * MAXP - 1,), jnp.int32)]
     )
-    lists = jnp.stack([own_list] + [shift(own_list, "y", Y, by) for by in (1, 2, 3)])
-    place = jnp.stack([lax.axis_index(name) for name in ("y", "k", "z")]).astype(jnp.int32)
+    lists = jnp.stack([own_list] + [shift(own_list, AXIS_Y, Y, by) for by in (1, 2, 3)])
+    place = jnp.stack([lax.axis_index(name) for name in (AXIS_Y, "k", "z")]).astype(jnp.int32)
     smem = pl.BlockSpec(memory_space=pltpu.SMEM)
     vmem = pl.BlockSpec(memory_space=pltpu.VMEM)
     picked = pl.pallas_call(
@@ -223,7 +226,7 @@
     )(picked, far_all, *near_blocks)
     far_taken = swap(far_give, "k", K, 1)
     far_pair = (far_total + far_taken.astype(jnp.float32)).astype(jnp.bfloat16)
-    far_back = lax.all_to_all(far_pair, ("x", "y"), 0, 0)
+    far_back = lax.all_to_all(far_pair, ("x",) + AXIS_Y, 0, 0)
     for bit in (1, 2, 4):
         left = near_total.shape[0] if bit == 1 else near_total.shape[0] // 2
         give = near_give if bit == 1 else near_total[left:].astype(jnp.bfloat16)
@@ -235,7 +238,7 @@
         walked, walked.T, precision=lax.Precision.HIGHEST, preferred_element_type=jnp.float32
     )
     partial_gram = local_gram.reshape(1, 8, 128)
-    for group in (("x", "y"), ("k", "z")):
+    for group in (("x",) + AXIS_Y, ("k", "z")):
         shares = lax.all_to_all(jnp.broadcast_to(partial_gram, (16, 8, 128)), group, 0, 0)
         partial_gram = jnp.sum(shares, axis=0, keepdims=True)
     gram_matrix = partial_gram.reshape(VEC, VEC) / points
@@ -254,7 +257,7 @@
 
 
 def solution(mesh):
-    fine = Mesh(mesh.devices.reshape(X, K, Z, Y), EVERY)
+    fine = Mesh(mesh.devices.reshape(X, K, Z, 2, 2), EVERY)
     in_specs = (P(None, EVERY), P(None, EVERY), P(EVERY, None), P(EVERY))
     out_specs = (P(None, EVERY), P())
     return jax.shard_map(

time: 155 us -> 169 us (1.090)
  waiting for transfers between devices: 48.7 us -> 59 us
  starting transfers between devices: 34.2 us -> 38.4 us
    ppermute x4 -> x5, waiting for transfers between devices: 4.36 us -> 14.7 us  [swap(): return lax.ppermute(values, axis, [(i, i ^ bit) for i in range(size)])]
    all_gather x1, waiting for transfers between devices: 27.4 us -> 31.3 us  [on_device(): far_all = lax.all_gather(far_two, FAR).reshape((FARS,) + far_send.shape)]
    ppermute x10, waiting for transfers between devices: 15.4 us -> 12.9 us  [shift(): lax.ppermute(values, axis, [(i, (i + by) % size) for i in range(size)])]
    ppermute x4 -> x5, starting transfers between devices: 9.32 us -> 11.6 us  [swap(): return lax.ppermute(values, axis, [(i, i ^ bit) for i in range(size)])]
    all_to_all x1, starting transfers between devices: 7.33 us -> 9.23 us  [on_device(): far_back = lax.all_to_all(far_pair, ('x',) + AXIS_Y, 0, 0)]
  transfers between devices with their start and end apart: 16 -> 17, of which waited for: 8 -> 8; matrix products, arithmetic and copies ran while one was open for 2% -> 2% of each run, Pallas kernels for 2% -> 2%
where the time goes in v8:
time: 169 us
  waiting for transfers between devices  59 us (35%)
  starting transfers between devices  38.4 us (23%)
  blocking collectives  30 us (18%)
  Pallas kernels  19.1 us (11%)
  between operations  14.9 us (9%)
  other arithmetic  4.73 us (3%)
  local copies, waits for them, and re-layouts  2.74 us (2%)
    all_gather x1, waiting for transfers between devices, on_device(): far_all = lax.all_gather(far_two, FAR).reshape((FARS,) + far_send.shape)  31.3 us
    all_to_all x2, blocking collectives, on_device(): lax.all_to_all(jnp.broadcast_to(partial_gram, (16, 8, 128)), group, 0, 0)  30 us
    ppermute x10, starting transfers between devices, shift(): lax.ppermute(values, axis, [(i, (i + by) % size) for i in range(size)])  17.5 us
    ppermute x5, waiting for transfers between devices, swap(): return lax.ppermute(values, axis, [(i, i ^ bit) for i in range(size)])  14.7 us
    ppermute x10, waiting for transfers between devices, shift(): lax.ppermute(values, axis, [(i, (i + by) % size) for i in range(size)])  12.9 us
    ppermute x5, starting transfers between devices, swap(): return lax.ppermute(values, axis, [(i, i ^ bit) for i in range(size)])  11.6 us
    pallas_call x1, Pallas kernels, on_device(): pl.pallas_call(tile_kernel, out_shape=[jax.ShapeDtypeStruct((Z // 2, AUG,...  11.5 us
    all_to_all x1, starting transfers between devices, on_device(): far_back = lax.all_to_all(far_pair, ('x',) + AXIS_Y, 0, 0)  9.23 us
  transfers between devices with their start and end apart: 17, of which 8 were waited for; matrix products, arithmetic and copies ran while one was open for 2% of the time, Pallas kernels for 2%

profile of v8, /device:TPU:1, one launch (start us, length us, event | category | flops | bytes accessed | tf_op | source)
XLA Modules:
  0.0 169.0 jit_solution(2503899471738111165)
XLA Ops:
  7.2 0.0 copy-start.2
  7.2 0.0 all-gather.3.cloned.1.call-start
  7.2 0.9 convert_element_type.23
  8.1 1.1 copy.13
  9.3 0.0 copy-done.2
  9.3 0.0 copy-start.3
  9.3 3.8 %collective-permute-start.3 = (bf16[288,512]{1,0:T(8,128)(2,1)S(1)}, bf16[288,512]{1,0:T(8,128)(2,1)S(1)}, u32[]{:S(2)}, u32[]{:S(2)}) collective-permute-start(bf16[288,512]{1,0:T(8,128)(2,1)S(1)} %get-tuple-element.13), channel_id=1, source_target_pairs={{0,2},{2,0},{1,3},{3,1},{4,6},{6,4},{5,7},{7,5},{8,10},{10,8},{9,1... | collective-permute-start | bytes 884744 | tf_op jit(solution)/shard_map/ppermute | solution.py:169
  13.2 5.7 %collective-permute-done.3 = bf16[288,512]{1,0:T(8,128)(2,1)S(1)} collective-permute-done((bf16[288,512]{1,0:T(8,128)(2,1)S(1)}, bf16[288,512]{1,0:T(8,128)(2,1)S(1)}, u32[]{:S(2)}, u32[]{:S(2)}) %collective-permute-start.3) | collective-permute-done | bytes 294944 | tf_op jit(solution)/shard_map/ppermute | solution.py:169
  18.8 0.9 pad_maximum_fusion
  19.7 0.0 all-gather.3.cloned.1.call-update
  19.7 2.5 %collective-permute-start.7 = (bf16[288,512]{1,0:T(8,128)(2,1)S(1)}, bf16[288,512]{1,0:T(8,128)(2,1)S(1)}, u32[]{:S(2)}, u32[]{:S(2)}) collective-permute-start(bf16[288,512]{1,0:T(8,128)(2,1)S(1)} %get-tuple-element.12.refs_0_), channel_id=1, source_target_pairs={{0,4},{4,8},{8,12},{12,16},{16,20},{20,24},{24,28},{28,0},{1,5},{5... | collective-permute-start | bytes 884744 | tf_op jit(solution)/shard_map/ppermute | solution.py:165
  22.3 4.0 %collective-permute-start.4 = (bf16[288,512]{1,0:T(8,128)(2,1)S(1)}, bf16[288,512]{1,0:T(8,128)(2,1)S(1)}, u32[]{:S(2)}, u32[]{:S(2)}) collective-permute-start(bf16[288,512]{1,0:T(8,128)(2,1)S(1)} %get-tuple-element.12.refs_0_), channel_id=1, source_target_pairs={{0,28},{4,0},{8,4},{12,8},{16,12},{20,16},{24,20},{28,24},{1,29},{... | collective-permute-start | bytes 884744 | tf_op jit(solution)/shard_map/ppermute | solution.py:165
  26.3 5.7 %collective-permute-done.7.refs_7_ = bf16[288,512]{1,0:T(8,128)(2,1)S(1)} collective-permute-done((bf16[288,512]{1,0:T(8,128)(2,1)S(1)}, bf16[288,512]{1,0:T(8,128)(2,1)S(1)}, u32[]{:S(2)}, u32[]{:S(2)}) %collective-permute-start.7) | collective-permute-done | bytes 294944 | tf_op jit(solution)/shard_map/ppermute | solution.py:165
  32.0 0.0 collective-permute-start.8
  32.0 0.0 collective-permute-done.4.refs_1_
  32.0 2.7 %collective-permute-start.5 = (bf16[288,512]{1,0:T(8,128)(2,1)S(1)}, bf16[288,512]{1,0:T(8,128)(2,1)S(1)}, u32[]{:S(2)}, u32[]{:S(2)}) collective-permute-start(bf16[288,512]{1,0:T(8,128)(2,1)S(1)} %collective-permute-done.4.refs_1_), channel_id=1, source_target_pairs={{0,28},{4,0},{8,4},{12,8},{16,12},{20,16},{24,20},{28,24},{1,29},{... | collective-permute-start | bytes 884744 | tf_op jit(solution)/shard_map/ppermute | solution.py:165
  34.6 4.8 %collective-permute-done.8.refs_6_ = bf16[288,512]{1,0:T(8,128)(2,1)S(1)} collective-permute-done((bf16[288,512]{1,0:T(8,128)(2,1)S(1)}, bf16[288,512]{1,0:T(8,128)(2,1)S(1)}, u32[]{:S(2)}, u32[]{:S(2)}) %collective-permute-start.8) | collective-permute-done | bytes 294944 | tf_op jit(solution)/shard_map/ppermute | solution.py:165
  39.5 0.0 collective-permute-start.9
  40.1 0.0 copy-done.3
  40.2 0.1 copy.12
  40.2 0.1 reshape.15
  40.4 0.1 pad_add_fusion.2
  40.4 2.9 %collective-permute-start.1 = (s32[128]{0:T(128)S(1)}, s32[128]{0:T(128)S(1)}, u32[]{:S(2)}, u32[]{:S(2)}) collective-permute-start(s32[128]{0:T(128)S(1)} %pad_add_fusion.2), channel_id=1, source_target_pairs={{0,2},{1,3},{2,0},{3,1},{4,6},{5,7},{6,4},{7,5},{8,10},{9,11},{10,... | collective-permute-start | bytes 1544 | tf_op jit(solution)/shard_map/ppermute | solution.py:165
  43.4 0.4 collective-permute-start
  43.8 2.3 %collective-permute-start.2 = (s32[128]{0:T(128)S(1)}, s32[128]{0:T(128)S(1)}, u32[]{:S(2)}, u32[]{:S(2)}) collective-permute-start(s32[128]{0:T(128)S(1)} %pad_add_fusion.2), channel_id=1, source_target_pairs={{0,3},{1,0},{2,1},{3,2},{4,7},{5,4},{6,5},{7,6},{8,11},{9,8},{10,9... | collective-permute-start | bytes 1544 | tf_op jit(solution)/shard_map/ppermute | solution.py:165
  46.0 0.0 collective-permute-done.5.refs_2_
  46.1 2.7 %collective-permute-start.6 = (bf16[288,512]{1,0:T(8,128)(2,1)S(1)}, bf16[288,512]{1,0:T(8,128)(2,1)S(1)}, u32[]{:S(2)}, u32[]{:S(2)}) collective-permute-start(bf16[288,512]{1,0:T(8,128)(2,1)S(1)} %collective-permute-done.5.refs_2_), channel_id=1, source_target_pairs={{0,28},{4,0},{8,4},{12,8},{16,12},{20,16},{24,20},{28,24},{1,29},{... | collective-permute-start | bytes 884744 | tf_op jit(solution)/shard_map/ppermute | solution.py:165
  48.7 0.0 collective-permute-done.9.refs_5_
  48.7 0.0 collective-permute-start.10
  48.7 0.1 fusion.6
  48.8 0.7 pad_add_fusion.1.place_ref
  49.5 0.0 collective-permute-done.1
  49.5 0.0 collective-permute-done
  49.5 0.0 collective-permute-done.2
  49.5 0.6 pad_add_fusion.lists_ref
  50.1 3.0 %select_pairs.1.picked_ref = s32[128]{0:T(128)} custom-call(s32[3]{0:T(128)} %pad_add_fusion.1.place_ref, s32[4,128]{1,0:T(4,128)} %pad_add_fusion.lists_ref), custom_call_target="tpu_custom_call" | custom-call | tf_op jit(solution)/shard_map/select_pairs/pallas_call | solution.py:200
  53.1 0.0 collective-permute-done.6.refs_3_
  53.1 2.4 %collective-permute-done.10.refs_4_ = bf16[288,512]{1,0:T(8,128)(2,1)S(1)} collective-permute-done((bf16[288,512]{1,0:T(8,128)(2,1)S(1)}, bf16[288,512]{1,0:T(8,128)(2,1)S(1)}, u32[]{:S(2)}, u32[]{:S(2)}) %collective-permute-start.10) | collective-permute-done | bytes 294944 | tf_op jit(solution)/shard_map/ppermute | solution.py:165
  55.5 31.3 %all-gather.3.cloned.1.call-done.far_hbm = bf16[32,288,512]{2,1,0:T(8,128)(2,1)} async-done(((bf16[2,288,512]{2,1,0:T(8,128)(2,1)}), bf16[32,288,512]{2,1,0:T(8,128)(2,1)}) %all-gather.3.cloned.1.call-update) | async-done | bytes 9437200 | tf_op jit(solution)/shard_map/all_gather | solution.py:177
  86.8 0.0 copy-start
  86.8 0.7 copy-done
  87.5 11.5 %tiles.1 = (f32[4,48,512]{2,1,0:T(8,128)S(1)}, bf16[4,48,512]{2,1,0:T(8,128)(2,1)S(1)}, f32[16,48,512]{2,1,0:T(8,128)S(1)}, bf16[16,48,512]{2,1,0:T(8,128)(2,1)S(1)}) custom-call(s32[128]{0:T(128)S(1)} %copy-done, bf16[32,288,512]{2,1,0:T(8,128)(2,1)} %all-gather.3.cloned.1.call-done.far_hbm, bf16[288,512]{1,0:T(8,128)(2,1)S(1)} %get-tuple-element.12.refs_0_, ...), custom_call_target="tpu_custom_call" | custom-call | tf_op jit(solution)/shard_map/tiles/pallas_call | solution.py:207
  98.9 0.1 collective-permute-start.14
  99.0 0.1 collective-permute-start.11
  99.1 2.2 %collective-permute-done.14 = bf16[16,48,512]{2,1,0:T(8,128)(2,1)S(1)} collective-permute-done((bf16[16,48,512]{2,1,0:T(8,128)(2,1)S(1)}, bf16[16,48,512]{2,1,0:T(8,128)(2,1)S(1)}, u32[]{:S(2)}, u32[]{:S(2)}) %collective-permute-start.14) | collective-permute-done | bytes 786464 | tf_op jit(solution)/shard_map/ppermute | solution.py:169
  101.3 1.2 add_convert_fusion
  102.5 9.2 %all-to-all-start = ((bf16[16,48,512]{2,1,0:T(8,128)(2,1)}), bf16[16,48,512]{2,1,0:T(8,128)(2,1)S(1)}, u32[]{:S(2)}, u32[]{:S(2)}) async-start(bf16[16,48,512]{2,1,0:T(8,128)(2,1)} %add_convert_fusion), calls=%async_computation | async-start | bytes 1572864 | tf_op jit(solution)/shard_map/all_to_all | solution.py:229
  111.8 0.0 collective-permute-done.11
  111.8 0.1 convert_add_fusion
  111.8 2.0 %collective-permute-start.12 = (bf16[2,48,512]{2,1,0:T(8,128)(2,1)S(1)}, bf16[2,48,512]{2,1,0:T(8,128)(2,1)S(1)}, u32[]{:S(2)}, u32[]{:S(2)}) collective-permute-start(bf16[2,48,512]{2,1,0:T(8,128)(2,1)S(1)} %slice.51), channel_id=1, source_target_pairs={{0,8},{4,12},{8,0},{12,4},{16,24},{20,28},{24,16},{28,20},{1,9},{5... | collective-permute-start | bytes 294920 | tf_op jit(solution)/shard_map/ppermute | solution.py:169
  113.8 5.2 %collective-permute-done.12 = bf16[2,48,512]{2,1,0:T(8,128)(2,1)S(1)} collective-permute-done((bf16[2,48,512]{2,1,0:T(8,128)(2,1)S(1)}, bf16[2,48,512]{2,1,0:T(8,128)(2,1)S(1)}, u32[]{:S(2)}, u32[]{:S(2)}) %collective-permute-start.12) | collective-permute-done | bytes 98336 | tf_op jit(solution)/shard_map/ppermute | solution.py:169
  119.1 5.6 %collective-permute-start.13 = (bf16[1,48,512]{2,1,0:T(8,128)(2,1)S(1)}, bf16[1,48,512]{2,1,0:T(8,128)(2,1)S(1)}, u32[]{:S(2)}, u32[]{:S(2)}) collective-permute-start(bf16[1,48,512]{2,1,0:T(8,128)(2,1)S(1)} %slice.52), channel_id=1, source_target_pairs={{0,16},{4,20},{8,24},{12,28},{16,0},{20,4},{24,8},{28,12},{1,17},{... | collective-permute-start | bytes 147464 | tf_op jit(solution)/shard_map/ppermute | solution.py:169
  124.7 0.0 all-to-all-done
  124.7 0.1 convert_reduce_fusion
  124.9 1.7 collective-permute-done.13
  126.6 0.0 copy-start.1
  126.6 0.2 fusion.3
  126.8 0.1 broadcast_in_dim.17
  126.9 12.3 %all_to_all.15 = f32[16,8,128]{2,1,0:T(8,128)S(1)} all-to-all(f32[16,8,128]{2,1,0:T(8,128)S(1)} %broadcast_in_dim.18), channel_id=1, replica_groups=mesh['x'=4,'k'=2,'z'=8,'h'=2,'l'=2] {'x','h','l'}, dimensions={0} | all-to-all | bytes 131072 | tf_op jit(solution)/shard_map/all_to_all | solution.py:242
  139.2 17.6 %all_to_all.16 = f32[16,8,128]{2,1,0:T(8,128)S(1)} all-to-all(f32[16,8,128]{2,1,0:T(8,128)S(1)} %broadcast_in_dim.19), channel_id=1, replica_groups=mesh['x'=4,'k'=2,'z'=8,'h'=2,'l'=2] {'k','z'}, dimensions={0} | all-to-all | bytes 131072 | tf_op jit(solution)/shard_map/all_to_all | solution.py:242
  156.9 0.7 div.23.gram_ref
  157.5 0.0 copy-done.1
  157.6 4.6 %finish.1 = (f32[32,512]{1,0:T(8,128)}, f32[32,32]{1,0:T(8,128)}) custom-call(f32[32,32]{1,0:T(8,128)} %div.23.gram_ref, f32[32,512]{1,0:T(8,128)} %copy-done.1), custom_call_target="tpu_custom_call" | custom-call | tf_op jit(solution)/shard_map/finish/pallas_call | solution.py:245
  (15 shorter events, 0.3 us)
Async XLA Ops:
  7.2 2.1 %copy-start.2 = (bf16[256,512]{1,0:T(8,128)(2,1)S(1)}, bf16[256,512]{1,0:T(8,128)(2,1)}, u32[]{:S(2)}) copy-start(bf16[256,512]{1,0:T(8,128)(2,1)} %param.4) | copy-start | bytes 786436
  7.2 79.6 %all-gather.3.cloned.1.call-start = ((), (), s32[]{:S(2)}) async-start(), calls=%async_computation.3 | async-start | bytes 10027008 | tf_op jit(solution)/shard_map/all_gather | solution.py:177
  9.3 30.9 %copy-start.3 = (s32[24,2]{0,1:T(2,128)S(1)}, s32[24,2]{0,1:T(2,128)}, u32[]{:S(2)}) copy-start(s32[24,2]{0,1:T(2,128)} %param.6) | copy-start | bytes 580
  9.3 9.5 %collective-permute-start.3 = (bf16[288,512]{1,0:T(8,128)(2,1)S(1)}, bf16[288,512]{1,0:T(8,128)(2,1)S(1)}, u32[]{:S(2)}, u32[]{:S(2)}) collective-permute-start(bf16[288,512]{1,0:T(8,128)(2,1)S(1)} %get-tuple-element.13), channel_id=1, source_target_pairs={{0,2},{2,0},{1,3},{3,1},{4,6},{6,4},{5,7},{7,5},{8,10},{10,8},{9,1... | collective-permute-start | bytes 884744 | tf_op jit(solution)/shard_map/ppermute | solution.py:169
  19.7 12.2 %collective-permute-start.7 = (bf16[288,512]{1,0:T(8,128)(2,1)S(1)}, bf16[288,512]{1,0:T(8,128)(2,1)S(1)}, u32[]{:S(2)}, u32[]{:S(2)}) collective-permute-start(bf16[288,512]{1,0:T(8,128)(2,1)S(1)} %get-tuple-element.12.refs_0_), channel_id=1, source_target_pairs={{0,4},{4,8},{8,12},{12,16},{16,20},{20,24},{24,28},{28,0},{1,5},{5... | collective-permute-start | bytes 884744 | tf_op jit(solution)/shard_map/ppermute | solution.py:165
  22.3 9.7 %collective-permute-start.4 = (bf16[288,512]{1,0:T(8,128)(2,1)S(1)}, bf16[288,512]{1,0:T(8,128)(2,1)S(1)}, u32[]{:S(2)}, u32[]{:S(2)}) collective-permute-start(bf16[288,512]{1,0:T(8,128)(2,1)S(1)} %get-tuple-element.12.refs_0_), channel_id=1, source_target_pairs={{0,28},{4,0},{8,4},{12,8},{16,12},{20,16},{24,20},{28,24},{1,29},{... | collective-permute-start | bytes 884744 | tf_op jit(solution)/shard_map/ppermute | solution.py:165
  32.0 7.5 %collective-permute-start.8 = (bf16[288,512]{1,0:T(8,128)(2,1)S(1)}, bf16[288,512]{1,0:T(8,128)(2,1)S(1)}, u32[]{:S(2)}, u32[]{:S(2)}) collective-permute-start(bf16[288,512]{1,0:T(8,128)(2,1)S(1)} %collective-permute-done.7.refs_7_), channel_id=1, source_target_pairs={{0,4},{4,8},{8,12},{12,16},{16,20},{20,24},{24,28},{28,0},{1,5},{5... | collective-permute-start | bytes 884744 | tf_op jit(solution)/shard_map/ppermute | solution.py:165
  32.0 14.1 %collective-permute-start.5 = (bf16[288,512]{1,0:T(8,128)(2,1)S(1)}, bf16[288,512]{1,0:T(8,128)(2,1)S(1)}, u32[]{:S(2)}, u32[]{:S(2)}) collective-permute-start(bf16[288,512]{1,0:T(8,128)(2,1)S(1)} %collective-permute-done.4.refs_1_), channel_id=1, source_target_pairs={{0,28},{4,0},{8,4},{12,8},{16,12},{20,16},{24,20},{28,24},{1,29},{... | collective-permute-start | bytes 884744 | tf_op jit(solution)/shard_map/ppermute | solution.py:165
  39.5 9.2 %collective-permute-start.9 = (bf16[288,512]{1,0:T(8,128)(2,1)S(1)}, bf16[288,512]{1,0:T(8,128)(2,1)S(1)}, u32[]{:S(2)}, u32[]{:S(2)}) collective-permute-start(bf16[288,512]{1,0:T(8,128)(2,1)S(1)} %collective-permute-done.8.refs_6_), channel_id=1, source_target_pairs={{0,4},{4,8},{8,12},{12,16},{16,20},{20,24},{24,28},{28,0},{1,5},{5... | collective-permute-start | bytes 884744 | tf_op jit(solution)/shard_map/ppermute | solution.py:165
  40.4 9.1 %collective-permute-start.1 = (s32[128]{0:T(128)S(1)}, s32[128]{0:T(128)S(1)}, u32[]{:S(2)}, u32[]{:S(2)}) collective-permute-start(s32[128]{0:T(128)S(1)} %pad_add_fusion.2), channel_id=1, source_target_pairs={{0,2},{1,3},{2,0},{3,1},{4,6},{5,7},{6,4},{7,5},{8,10},{9,11},{10,... | collective-permute-start | bytes 1544 | tf_op jit(solution)/shard_map/ppermute | solution.py:165
  43.4 6.1 %collective-permute-start = (s32[128]{0:T(128)S(1)}, s32[128]{0:T(128)S(1)}, u32[]{:S(2)}, u32[]{:S(2)}) collective-permute-start(s32[128]{0:T(128)S(1)} %pad_add_fusion.2), channel_id=1, source_target_pairs={{0,1},{1,2},{2,3},{3,0},{4,5},{5,6},{6,7},{7,4},{8,9},{9,10},{10,1... | collective-permute-start | bytes 1544 | tf_op jit(solution)/shard_map/ppermute | solution.py:165
  43.8 5.7 %collective-permute-start.2 = (s32[128]{0:T(128)S(1)}, s32[128]{0:T(128)S(1)}, u32[]{:S(2)}, u32[]{:S(2)}) collective-permute-start(s32[128]{0:T(128)S(1)} %pad_add_fusion.2), channel_id=1, source_target_pairs={{0,3},{1,0},{2,1},{3,2},{4,7},{5,4},{6,5},{7,6},{8,11},{9,8},{10,9... | collective-permute-start | bytes 1544 | tf_op jit(solution)/shard_map/ppermute | solution.py:165
  46.1 7.1 %collective-permute-start.6 = (bf16[288,512]{1,0:T(8,128)(2,1)S(1)}, bf16[288,512]{1,0:T(8,128)(2,1)S(1)}, u32[]{:S(2)}, u32[]{:S(2)}) collective-permute-start(bf16[288,512]{1,0:T(8,128)(2,1)S(1)} %collective-permute-done.5.refs_2_), channel_id=1, source_target_pairs={{0,28},{4,0},{8,4},{12,8},{16,12},{20,16},{24,20},{28,24},{1,29},{... | collective-permute-start | bytes 884744 | tf_op jit(solution)/shard_map/ppermute | solution.py:165
  48.7 6.8 %collective-permute-start.10 = (bf16[288,512]{1,0:T(8,128)(2,1)S(1)}, bf16[288,512]{1,0:T(8,128)(2,1)S(1)}, u32[]{:S(2)}, u32[]{:S(2)}) collective-permute-start(bf16[288,512]{1,0:T(8,128)(2,1)S(1)} %collective-permute-done.9.refs_5_), channel_id=1, source_target_pairs={{0,4},{4,8},{8,12},{12,16},{16,20},{20,24},{24,28},{28,0},{1,5},{5... | collective-permute-start | bytes 884744 | tf_op jit(solution)/shard_map/ppermute | solution.py:165
  86.8 0.7 copy-start
  98.9 2.4 %collective-permute-start.14 = (bf16[16,48,512]{2,1,0:T(8,128)(2,1)S(1)}, bf16[16,48,512]{2,1,0:T(8,128)(2,1)S(1)}, u32[]{:S(2)}, u32[]{:S(2)}) collective-permute-start(bf16[16,48,512]{2,1,0:T(8,128)(2,1)S(1)} %get-tuple-element.9), channel_id=1, source_target_pairs={{0,32},{32,0},{1,33},{33,1},{2,34},{34,2},{3,35},{35,3},{4,36},{36... | collective-permute-start | bytes 2359304 | tf_op jit(solution)/shard_map/ppermute | solution.py:169
  99.0 12.7 %collective-permute-start.11 = (bf16[4,48,512]{2,1,0:T(8,128)(2,1)S(1)}, bf16[4,48,512]{2,1,0:T(8,128)(2,1)S(1)}, u32[]{:S(2)}, u32[]{:S(2)}) collective-permute-start(bf16[4,48,512]{2,1,0:T(8,128)(2,1)S(1)} %get-tuple-element.7), channel_id=1, source_target_pairs={{0,4},{4,0},{8,12},{12,8},{16,20},{20,16},{24,28},{28,24},{1,5},{5... | collective-permute-start | bytes 589832 | tf_op jit(solution)/shard_map/ppermute | solution.py:169
  102.5 22.2 %all-to-all-start = ((bf16[16,48,512]{2,1,0:T(8,128)(2,1)}), bf16[16,48,512]{2,1,0:T(8,128)(2,1)S(1)}, u32[]{:S(2)}, u32[]{:S(2)}) async-start(bf16[16,48,512]{2,1,0:T(8,128)(2,1)} %add_convert_fusion), calls=%async_computation | async-start | bytes 1572864 | tf_op jit(solution)/shard_map/all_to_all | solution.py:229
  111.8 7.2 %collective-permute-start.12 = (bf16[2,48,512]{2,1,0:T(8,128)(2,1)S(1)}, bf16[2,48,512]{2,1,0:T(8,128)(2,1)S(1)}, u32[]{:S(2)}, u32[]{:S(2)}) collective-permute-start(bf16[2,48,512]{2,1,0:T(8,128)(2,1)S(1)} %slice.51), channel_id=1, source_target_pairs={{0,8},{4,12},{8,0},{12,4},{16,24},{20,28},{24,16},{28,20},{1,9},{5... | collective-permute-start | bytes 294920 | tf_op jit(solution)/shard_map/ppermute | solution.py:169
  119.1 7.4 %collective-permute-start.13 = (bf16[1,48,512]{2,1,0:T(8,128)(2,1)S(1)}, bf16[1,48,512]{2,1,0:T(8,128)(2,1)S(1)}, u32[]{:S(2)}, u32[]{:S(2)}) collective-permute-start(bf16[1,48,512]{2,1,0:T(8,128)(2,1)S(1)} %slice.52), channel_id=1, source_target_pairs={{0,16},{4,20},{8,24},{12,28},{16,0},{20,4},{24,8},{28,12},{1,17},{... | collective-permute-start | bytes 147464 | tf_op jit(solution)/shard_map/ppermute | solution.py:169
  126.6 31.0 %copy-start.1 = (f32[32,512]{1,0:T(8,128)}, f32[32,512]{1,0:T(8,128)S(1)}, u32[]{:S(2)}) copy-start(f32[32,512]{1,0:T(8,128)S(1)} %slice_divide_fusion.walked_ref) | copy-start | bytes 196612
Sparse Core Ops, SparseCore 0:
  19.9 66.8 all-gather.2

commit v9 on v7

--- a/solution.py
+++ b/solution.py
@@ -17,10 +17,11 @@
 EMB = 256
 VEC = 32
 AUG = 48
+SENT = 40
 MAXP = 24
 SLOTS = 128
-PAIR = 2
-AHEAD = 2
+PAIR = 4
+AHEAD = 1
 
 
 def select_kernel(place_ref, lists_ref, picked_ref):
@@ -170,7 +171,8 @@
 def on_device(embeddings, vectors, block_pairs, counts):
     score_scale = 0.5 / math.sqrt(EMB)
     vector_bf16 = vectors.astype(jnp.bfloat16)
-    far_send = lax.optimization_barrier(jnp.concatenate([embeddings, vector_bf16], axis=0))
+    far_send = jnp.concatenate([embeddings, vector_bf16], axis=0)
+    far_send, embeddings = lax.optimization_barrier((far_send, embeddings))
     far_all = lax.all_gather(far_send, FAR)
     turned = embeddings.T
     near_send = jnp.concatenate(
@@ -222,12 +224,12 @@
         name="tiles",
     )(picked, far_all, *near_blocks)
     far_taken = swap(far_give, "k", K, 1)
-    far_pair = (far_total + far_taken.astype(jnp.float32)).astype(jnp.bfloat16)
+    far_pair = (far_total + far_taken.astype(jnp.float32))[:, :SENT].astype(jnp.bfloat16)
     far_back = lax.all_to_all(far_pair, ("x", "y"), 0, 0)
     for bit in (1, 2, 4):
         left = near_total.shape[0] if bit == 1 else near_total.shape[0] // 2
         give = near_give if bit == 1 else near_total[left:].astype(jnp.bfloat16)
-        near_total = near_total[:left] + swap(give, "z", Z, bit).astype(jnp.float32)
+        near_total = (near_total[:left] + swap(give, "z", Z, bit).astype(jnp.float32))[:, :SENT]
     total = near_total[0] + jnp.sum(far_back.astype(jnp.float32), axis=0)
     walked = total[:VEC] / total[VEC : VEC + 1]
     points = BS * X * K * Z * Y

time: 155 us -> 154 us (level)
  Pallas kernels: 18.6 us -> 17 us
    ppermute x4, waiting for transfers between devices: 4.36 us -> 7.01 us  [swap(): return lax.ppermute(values, axis, [(i, i ^ bit) for i in range(size)])]
    ppermute x4, starting transfers between devices: 9.32 us -> 11.6 us  [swap(): return lax.ppermute(values, axis, [(i, i ^ bit) for i in range(size)])]
    concatenate x0 -> x1, other arithmetic: none -> 1.69 us  [on_device(): far_send = jnp.concatenate([embeddings, vector_bf16], axis=0)]
    pallas_call x1, Pallas kernels: 11.5 us -> 9.87 us  [on_device(): pl.pallas_call(tile_kernel, out_shape=[jax.ShapeDtypeStruct((Z // 2, AUG,...]
  transfers between devices with their start and end apart: 16 -> 16, of which waited for: 8 -> 7; matrix products, arithmetic and copies ran while one was open for 2% -> 3% of each run, Pallas kernels for 2% -> 2%
where the time goes in v9:
time: 154 us
  waiting for transfers between devices  49.1 us (32%)
  starting transfers between devices  35.2 us (23%)
  blocking collectives  29.5 us (19%)
  Pallas kernels  17 us (11%)
  between operations  14.9 us (10%)
  other arithmetic  5.27 us (3%)
  local copies, waits for them, and re-layouts  2.74 us (2%)
    all_to_all x2, blocking collectives, on_device(): lax.all_to_all(jnp.broadcast_to(partial_gram, (16, 8, 128)), group, 0, 0)  29.5 us
    all_gather x1, waiting for transfers between devices, on_device(): far_all = lax.all_gather(far_send, FAR)  26.5 us
    ppermute x10, starting transfers between devices, shift(): lax.ppermute(values, axis, [(i, (i + by) % size) for i in range(size)])  17.5 us
    ppermute x10, waiting for transfers between devices, shift(): lax.ppermute(values, axis, [(i, (i + by) % size) for i in range(size)])  15.5 us
    ppermute x4, starting transfers between devices, swap(): return lax.ppermute(values, axis, [(i, i ^ bit) for i in range(size)])  11.6 us
    pallas_call x1, Pallas kernels, on_device(): pl.pallas_call(tile_kernel, out_shape=[jax.ShapeDtypeStruct((Z // 2, AUG,...  9.87 us
    ppermute x4, waiting for transfers between devices, swap(): return lax.ppermute(values, axis, [(i, i ^ bit) for i in range(size)])  7.01 us
    all_to_all x1, starting transfers between devices, on_device(): far_back = lax.all_to_all(far_pair, ('x', 'y'), 0, 0)  6.07 us
  transfers between devices with their start and end apart: 16, of which 7 were waited for; matrix products, arithmetic and copies ran while one was open for 3% of the time, Pallas kernels for 2%

profile of v9, /device:TPU:1, one launch (start us, length us, event | category | flops | bytes accessed | tf_op | source)
XLA Modules:
  0.0 153.9 jit_solution(8855754716952155538)
XLA Ops:
  7.2 0.0 all-gather.3.cloned.1.call-start
  7.2 0.8 convert_element_type.21
  8.1 1.7 %pad_maximum_fusion.1 = bf16[288,512]{1,0:T(8,128)(2,1)} fusion(bf16[32,512]{1,0:T(8,128)(2,1)S(1)} %convert_element_type.21, bf16[256,512]{1,0:T(8,128)(2,1)} %param.4), kind=kLoop, calls=%fused_computation.5 | loop fusion | flops 589824 | bytes 589824 | tf_op jit(solution)/shard_map/concatenate | solution.py:174
  9.7 0.0 copy-start.2
  9.7 0.0 all-gather.3.cloned.1.call-update
  9.8 1.1 copy.11
  11.0 2.5 %collective-permute-start.6 = (bf16[288,512]{1,0:T(8,128)(2,1)S(1)}, bf16[288,512]{1,0:T(8,128)(2,1)S(1)}, u32[]{:S(2)}, u32[]{:S(2)}) collective-permute-start(bf16[288,512]{1,0:T(8,128)(2,1)S(1)} %pad_maximum_fusion.refs_0_), channel_id=1, source_target_pairs={{0,4},{4,8},{8,12},{12,16},{16,20},{20,24},{24,28},{28,0},{1,5},{5... | collective-permute-start | bytes 884744 | tf_op jit(solution)/shard_map/ppermute | solution.py:164
  13.5 4.0 %collective-permute-start.3 = (bf16[288,512]{1,0:T(8,128)(2,1)S(1)}, bf16[288,512]{1,0:T(8,128)(2,1)S(1)}, u32[]{:S(2)}, u32[]{:S(2)}) collective-permute-start(bf16[288,512]{1,0:T(8,128)(2,1)S(1)} %pad_maximum_fusion.refs_0_), channel_id=1, source_target_pairs={{0,28},{4,0},{8,4},{12,8},{16,12},{20,16},{24,20},{28,24},{1,29},{... | collective-permute-start | bytes 884744 | tf_op jit(solution)/shard_map/ppermute | solution.py:164
  17.5 6.6 %collective-permute-done.6.refs_7_ = bf16[288,512]{1,0:T(8,128)(2,1)S(1)} collective-permute-done((bf16[288,512]{1,0:T(8,128)(2,1)S(1)}, bf16[288,512]{1,0:T(8,128)(2,1)S(1)}, u32[]{:S(2)}, u32[]{:S(2)}) %collective-permute-start.6) | collective-permute-done | bytes 294944 | tf_op jit(solution)/shard_map/ppermute | solution.py:164
  24.2 0.0 collective-permute-start.7
  24.2 0.0 collective-permute-done.3.refs_1_
  24.2 2.7 %collective-permute-start.4 = (bf16[288,512]{1,0:T(8,128)(2,1)S(1)}, bf16[288,512]{1,0:T(8,128)(2,1)S(1)}, u32[]{:S(2)}, u32[]{:S(2)}) collective-permute-start(bf16[288,512]{1,0:T(8,128)(2,1)S(1)} %collective-permute-done.3.refs_1_), channel_id=1, source_target_pairs={{0,28},{4,0},{8,4},{12,8},{16,12},{20,16},{24,20},{28,24},{1,29},{... | collective-permute-start | bytes 884744 | tf_op jit(solution)/shard_map/ppermute | solution.py:164
  26.9 5.9 %collective-permute-done.7.refs_6_ = bf16[288,512]{1,0:T(8,128)(2,1)S(1)} collective-permute-done((bf16[288,512]{1,0:T(8,128)(2,1)S(1)}, bf16[288,512]{1,0:T(8,128)(2,1)S(1)}, u32[]{:S(2)}, u32[]{:S(2)}) %collective-permute-start.7) | collective-permute-done | bytes 294944 | tf_op jit(solution)/shard_map/ppermute | solution.py:164
  32.8 0.0 collective-permute-start.8
  33.4 0.0 copy-done.2
  33.4 0.1 copy.10
  33.5 0.1 reshape.12
  33.6 0.1 pad_add_fusion.2
  33.7 2.9 %collective-permute-start.1 = (s32[128]{0:T(128)S(1)}, s32[128]{0:T(128)S(1)}, u32[]{:S(2)}, u32[]{:S(2)}) collective-permute-start(s32[128]{0:T(128)S(1)} %pad_add_fusion.2), channel_id=1, source_target_pairs={{0,2},{1,3},{2,0},{3,1},{4,6},{5,7},{6,4},{7,5},{8,10},{9,11},{10,... | collective-permute-start | bytes 1544 | tf_op jit(solution)/shard_map/ppermute | solution.py:164
  36.6 0.3 collective-permute-start
  37.0 2.4 %collective-permute-start.2 = (s32[128]{0:T(128)S(1)}, s32[128]{0:T(128)S(1)}, u32[]{:S(2)}, u32[]{:S(2)}) collective-permute-start(s32[128]{0:T(128)S(1)} %pad_add_fusion.2), channel_id=1, source_target_pairs={{0,3},{1,0},{2,1},{3,2},{4,7},{5,4},{6,5},{7,6},{8,11},{9,8},{10,9... | collective-permute-start | bytes 1544 | tf_op jit(solution)/shard_map/ppermute | solution.py:164
  39.3 0.0 collective-permute-done.4.refs_2_
  39.3 2.7 %collective-permute-start.5 = (bf16[288,512]{1,0:T(8,128)(2,1)S(1)}, bf16[288,512]{1,0:T(8,128)(2,1)S(1)}, u32[]{:S(2)}, u32[]{:S(2)}) collective-permute-start(bf16[288,512]{1,0:T(8,128)(2,1)S(1)} %collective-permute-done.4.refs_2_), channel_id=1, source_target_pairs={{0,28},{4,0},{8,4},{12,8},{16,12},{20,16},{24,20},{28,24},{1,29},{... | collective-permute-start | bytes 884744 | tf_op jit(solution)/shard_map/ppermute | solution.py:164
  42.0 0.0 collective-permute-done.8.refs_5_
  42.0 0.0 collective-permute-start.9
  42.0 0.1 fusion.7
  42.1 0.6 pad_add_fusion.1.place_ref
  42.7 0.0 collective-permute-done.1
  42.7 0.0 collective-permute-done
  42.7 0.0 collective-permute-done.2
  42.7 0.6 pad_add_fusion.lists_ref
  43.3 2.5 %select_pairs.1.picked_ref = s32[128]{0:T(128)} custom-call(s32[3]{0:T(128)} %pad_add_fusion.1.place_ref, s32[4,128]{1,0:T(4,128)} %pad_add_fusion.lists_ref), custom_call_target="tpu_custom_call" | custom-call | tf_op jit(solution)/shard_map/select_pairs/pallas_call | solution.py:199
  45.8 0.0 collective-permute-done.5.refs_3_
  45.8 3.0 %collective-permute-done.9.refs_4_ = bf16[288,512]{1,0:T(8,128)(2,1)S(1)} collective-permute-done((bf16[288,512]{1,0:T(8,128)(2,1)S(1)}, bf16[288,512]{1,0:T(8,128)(2,1)S(1)}, u32[]{:S(2)}, u32[]{:S(2)}) %collective-permute-start.9) | collective-permute-done | bytes 294944 | tf_op jit(solution)/shard_map/ppermute | solution.py:164
  48.8 26.5 %all-gather.3.cloned.1.call-done = bf16[9216,512]{1,0:T(8,128)(2,1)} async-done(((bf16[288,512]{1,0:T(8,128)(2,1)}), bf16[9216,512]{1,0:T(8,128)(2,1)}) %all-gather.3.cloned.1.call-update) | async-done | bytes 9437200 | tf_op jit(solution)/shard_map/all_gather | solution.py:176
  75.3 0.0 copy-start
  75.3 0.7 copy-done
  75.9 9.9 %tiles.1 = (f32[4,48,512]{2,1,0:T(8,128)S(1)}, bf16[4,48,512]{2,1,0:T(8,128)(2,1)S(1)}, f32[16,48,512]{2,1,0:T(8,128)S(1)}, bf16[16,48,512]{2,1,0:T(8,128)(2,1)S(1)}) custom-call(s32[128]{0:T(128)S(1)} %copy-done, bf16[32,288,512]{2,1,0:T(8,128)(2,1)} %bitcast.17, bf16[288,512]{1,0:T(8,128)(2,1)S(1)} %pad_maximum_fusion.refs_0_, ...), custom_call_target="tpu_custom_call" | custom-call | tf_op jit(solution)/shard_map/tiles/pallas_call | solution.py:206
  85.8 2.2 %collective-permute-start.13 = (bf16[16,48,512]{2,1,0:T(8,128)(2,1)S(1)}, bf16[16,48,512]{2,1,0:T(8,128)(2,1)S(1)}, u32[]{:S(2)}, u32[]{:S(2)}) collective-permute-start(bf16[16,48,512]{2,1,0:T(8,128)(2,1)S(1)} %get-tuple-element.13), channel_id=1, source_target_pairs={{0,32},{32,0},{1,33},{33,1},{2,34},{34,2},{3,35},{35,3},{4,36},{36... | collective-permute-start | bytes 2359304 | tf_op jit(solution)/shard_map/ppermute | solution.py:168
  88.1 1.3 collective-permute-start.10
  89.3 0.6 collective-permute-done.13
  90.0 1.1 fusion
  91.1 6.1 %all-to-all-start = ((bf16[16,40,512]{2,1,0:T(8,128)(2,1)}), bf16[16,40,512]{2,1,0:T(8,128)(2,1)S(1)}, u32[]{:S(2)}, u32[]{:S(2)}) async-start(bf16[16,40,512]{2,1,0:T(8,128)(2,1)} %fusion), calls=%async_computation | async-start | bytes 1310720 | tf_op jit(solution)/shard_map/all_to_all | solution.py:228
  97.2 0.0 collective-permute-done.10
  97.2 0.1 convert_add_fusion
  97.2 3.4 %collective-permute-start.11 = (bf16[2,40,512]{2,1,0:T(8,128)(2,1)S(1)}, bf16[2,40,512]{2,1,0:T(8,128)(2,1)S(1)}, u32[]{:S(2)}, u32[]{:S(2)}) collective-permute-start(bf16[2,40,512]{2,1,0:T(8,128)(2,1)S(1)} %slice.65), channel_id=1, source_target_pairs={{0,8},{4,12},{8,0},{12,4},{16,24},{20,28},{24,16},{28,20},{1,9},{5... | collective-permute-start | bytes 245768 | tf_op jit(solution)/shard_map/ppermute | solution.py:168
  100.7 4.2 %collective-permute-done.11 = bf16[2,40,512]{2,1,0:T(8,128)(2,1)S(1)} collective-permute-done((bf16[2,40,512]{2,1,0:T(8,128)(2,1)S(1)}, bf16[2,40,512]{2,1,0:T(8,128)(2,1)S(1)}, u32[]{:S(2)}, u32[]{:S(2)}) %collective-permute-start.11) | collective-permute-done | bytes 81952 | tf_op jit(solution)/shard_map/ppermute | solution.py:168
  105.0 4.7 %collective-permute-start.12 = (bf16[1,40,512]{2,1,0:T(8,128)(2,1)S(1)}, bf16[1,40,512]{2,1,0:T(8,128)(2,1)S(1)}, u32[]{:S(2)}, u32[]{:S(2)}) collective-permute-start(bf16[1,40,512]{2,1,0:T(8,128)(2,1)S(1)} %slice.66), channel_id=1, source_target_pairs={{0,16},{4,20},{8,24},{12,28},{16,0},{20,4},{24,8},{28,12},{1,17},{... | collective-permute-start | bytes 122888 | tf_op jit(solution)/shard_map/ppermute | solution.py:168
  109.6 0.0 all-to-all-done
  109.6 0.1 convert_reduce_fusion
  109.7 2.1 %collective-permute-done.12 = bf16[1,40,512]{2,1,0:T(8,128)(2,1)S(1)} collective-permute-done((bf16[1,40,512]{2,1,0:T(8,128)(2,1)S(1)}, bf16[1,40,512]{2,1,0:T(8,128)(2,1)S(1)}, u32[]{:S(2)}, u32[]{:S(2)}) %collective-permute-start.12) | collective-permute-done | bytes 40992 | tf_op jit(solution)/shard_map/ppermute | solution.py:168
  111.9 0.0 copy-start.1
  111.9 0.2 fusion.4
  112.1 0.1 broadcast_in_dim.17
  112.2 12.9 %all_to_all.15 = f32[16,8,128]{2,1,0:T(8,128)S(1)} all-to-all(f32[16,8,128]{2,1,0:T(8,128)S(1)} %broadcast_in_dim.18), channel_id=1, replica_groups=mesh['x'=4,'k'=2,'z'=8,'y'=4] {'x','y'}, dimensions={0} | all-to-all | bytes 131072 | tf_op jit(solution)/shard_map/all_to_all | solution.py:241
  125.1 16.6 %all_to_all.16 = f32[16,8,128]{2,1,0:T(8,128)S(1)} all-to-all(f32[16,8,128]{2,1,0:T(8,128)S(1)} %broadcast_in_dim.19), channel_id=1, replica_groups=mesh['x'=4,'k'=2,'z'=8,'y'=4] {'k','z'}, dimensions={0} | all-to-all | bytes 131072 | tf_op jit(solution)/shard_map/all_to_all | solution.py:241
  141.8 0.7 div.23.gram_ref
  142.4 0.0 copy-done.1
  142.4 4.6 %finish.1 = (f32[32,512]{1,0:T(8,128)}, f32[32,32]{1,0:T(8,128)}) custom-call(f32[32,32]{1,0:T(8,128)} %div.23.gram_ref, f32[32,512]{1,0:T(8,128)} %copy-done.1), custom_call_target="tpu_custom_call" | custom-call | tf_op jit(solution)/shard_map/finish/pallas_call | solution.py:244
  (15 shorter events, 0.2 us)
Async XLA Ops:
  7.2 68.1 %all-gather.3.cloned.1.call-start = ((), (), s32[]{:S(2)}) async-start(), calls=%async_computation.3 | async-start | bytes 9732096 | tf_op jit(solution)/shard_map/all_gather | solution.py:176
  9.7 23.7 %copy-start.2 = (s32[24,2]{0,1:T(2,128)S(1)}, s32[24,2]{0,1:T(2,128)}, u32[]{:S(2)}) copy-start(s32[24,2]{0,1:T(2,128)} %param.6) | copy-start | bytes 580
  11.0 13.2 %collective-permute-start.6 = (bf16[288,512]{1,0:T(8,128)(2,1)S(1)}, bf16[288,512]{1,0:T(8,128)(2,1)S(1)}, u32[]{:S(2)}, u32[]{:S(2)}) collective-permute-start(bf16[288,512]{1,0:T(8,128)(2,1)S(1)} %pad_maximum_fusion.refs_0_), channel_id=1, source_target_pairs={{0,4},{4,8},{8,12},{12,16},{16,20},{20,24},{24,28},{28,0},{1,5},{5... | collective-permute-start | bytes 884744 | tf_op jit(solution)/shard_map/ppermute | solution.py:164
  13.5 10.7 %collective-permute-start.3 = (bf16[288,512]{1,0:T(8,128)(2,1)S(1)}, bf16[288,512]{1,0:T(8,128)(2,1)S(1)}, u32[]{:S(2)}, u32[]{:S(2)}) collective-permute-start(bf16[288,512]{1,0:T(8,128)(2,1)S(1)} %pad_maximum_fusion.refs_0_), channel_id=1, source_target_pairs={{0,28},{4,0},{8,4},{12,8},{16,12},{20,16},{24,20},{28,24},{1,29},{... | collective-permute-start | bytes 884744 | tf_op jit(solution)/shard_map/ppermute | solution.py:164
  24.2 8.6 %collective-permute-start.7 = (bf16[288,512]{1,0:T(8,128)(2,1)S(1)}, bf16[288,512]{1,0:T(8,128)(2,1)S(1)}, u32[]{:S(2)}, u32[]{:S(2)}) collective-permute-start(bf16[288,512]{1,0:T(8,128)(2,1)S(1)} %collective-permute-done.6.refs_7_), channel_id=1, source_target_pairs={{0,4},{4,8},{8,12},{12,16},{16,20},{20,24},{24,28},{28,0},{1,5},{5... | collective-permute-start | bytes 884744 | tf_op jit(solution)/shard_map/ppermute | solution.py:164
  24.2 15.1 %collective-permute-start.4 = (bf16[288,512]{1,0:T(8,128)(2,1)S(1)}, bf16[288,512]{1,0:T(8,128)(2,1)S(1)}, u32[]{:S(2)}, u32[]{:S(2)}) collective-permute-start(bf16[288,512]{1,0:T(8,128)(2,1)S(1)} %collective-permute-done.3.refs_1_), channel_id=1, source_target_pairs={{0,28},{4,0},{8,4},{12,8},{16,12},{20,16},{24,20},{28,24},{1,29},{... | collective-permute-start | bytes 884744 | tf_op jit(solution)/shard_map/ppermute | solution.py:164
  32.8 9.2 %collective-permute-start.8 = (bf16[288,512]{1,0:T(8,128)(2,1)S(1)}, bf16[288,512]{1,0:T(8,128)(2,1)S(1)}, u32[]{:S(2)}, u32[]{:S(2)}) collective-permute-start(bf16[288,512]{1,0:T(8,128)(2,1)S(1)} %collective-permute-done.7.refs_6_), channel_id=1, source_target_pairs={{0,4},{4,8},{8,12},{12,16},{16,20},{20,24},{24,28},{28,0},{1,5},{5... | collective-permute-start | bytes 884744 | tf_op jit(solution)/shard_map/ppermute | solution.py:164
  33.7 8.9 %collective-permute-start.1 = (s32[128]{0:T(128)S(1)}, s32[128]{0:T(128)S(1)}, u32[]{:S(2)}, u32[]{:S(2)}) collective-permute-start(s32[128]{0:T(128)S(1)} %pad_add_fusion.2), channel_id=1, source_target_pairs={{0,2},{1,3},{2,0},{3,1},{4,6},{5,7},{6,4},{7,5},{8,10},{9,11},{10,... | collective-permute-start | bytes 1544 | tf_op jit(solution)/shard_map/ppermute | solution.py:164
  36.6 6.0 %collective-permute-start = (s32[128]{0:T(128)S(1)}, s32[128]{0:T(128)S(1)}, u32[]{:S(2)}, u32[]{:S(2)}) collective-permute-start(s32[128]{0:T(128)S(1)} %pad_add_fusion.2), channel_id=1, source_target_pairs={{0,1},{1,2},{2,3},{3,0},{4,5},{5,6},{6,7},{7,4},{8,9},{9,10},{10,1... | collective-permute-start | bytes 1544 | tf_op jit(solution)/shard_map/ppermute | solution.py:164
  37.0 5.7 %collective-permute-start.2 = (s32[128]{0:T(128)S(1)}, s32[128]{0:T(128)S(1)}, u32[]{:S(2)}, u32[]{:S(2)}) collective-permute-start(s32[128]{0:T(128)S(1)} %pad_add_fusion.2), channel_id=1, source_target_pairs={{0,3},{1,0},{2,1},{3,2},{4,7},{5,4},{6,5},{7,6},{8,11},{9,8},{10,9... | collective-permute-start | bytes 1544 | tf_op jit(solution)/shard_map/ppermute | solution.py:164
  39.3 6.5 %collective-permute-start.5 = (bf16[288,512]{1,0:T(8,128)(2,1)S(1)}, bf16[288,512]{1,0:T(8,128)(2,1)S(1)}, u32[]{:S(2)}, u32[]{:S(2)}) collective-permute-start(bf16[288,512]{1,0:T(8,128)(2,1)S(1)} %collective-permute-done.4.refs_2_), channel_id=1, source_target_pairs={{0,28},{4,0},{8,4},{12,8},{16,12},{20,16},{24,20},{28,24},{1,29},{... | collective-permute-start | bytes 884744 | tf_op jit(solution)/shard_map/ppermute | solution.py:164
  42.0 6.8 %collective-permute-start.9 = (bf16[288,512]{1,0:T(8,128)(2,1)S(1)}, bf16[288,512]{1,0:T(8,128)(2,1)S(1)}, u32[]{:S(2)}, u32[]{:S(2)}) collective-permute-start(bf16[288,512]{1,0:T(8,128)(2,1)S(1)} %collective-permute-done.8.refs_5_), channel_id=1, source_target_pairs={{0,4},{4,8},{8,12},{12,16},{16,20},{20,24},{24,28},{28,0},{1,5},{5... | collective-permute-start | bytes 884744 | tf_op jit(solution)/shard_map/ppermute | solution.py:164
  75.3 0.7 copy-start
  85.8 4.2 %collective-permute-start.13 = (bf16[16,48,512]{2,1,0:T(8,128)(2,1)S(1)}, bf16[16,48,512]{2,1,0:T(8,128)(2,1)S(1)}, u32[]{:S(2)}, u32[]{:S(2)}) collective-permute-start(bf16[16,48,512]{2,1,0:T(8,128)(2,1)S(1)} %get-tuple-element.13), channel_id=1, source_target_pairs={{0,32},{32,0},{1,33},{33,1},{2,34},{34,2},{3,35},{35,3},{4,36},{36... | collective-permute-start | bytes 2359304 | tf_op jit(solution)/shard_map/ppermute | solution.py:168
  88.1 9.1 %collective-permute-start.10 = (bf16[4,48,512]{2,1,0:T(8,128)(2,1)S(1)}, bf16[4,48,512]{2,1,0:T(8,128)(2,1)S(1)}, u32[]{:S(2)}, u32[]{:S(2)}) collective-permute-start(bf16[4,48,512]{2,1,0:T(8,128)(2,1)S(1)} %get-tuple-element.11), channel_id=1, source_target_pairs={{0,4},{4,0},{8,12},{12,8},{16,20},{20,16},{24,28},{28,24},{1,5},{5... | collective-permute-start | bytes 589832 | tf_op jit(solution)/shard_map/ppermute | solution.py:168
  91.1 18.5 %all-to-all-start = ((bf16[16,40,512]{2,1,0:T(8,128)(2,1)}), bf16[16,40,512]{2,1,0:T(8,128)(2,1)S(1)}, u32[]{:S(2)}, u32[]{:S(2)}) async-start(bf16[16,40,512]{2,1,0:T(8,128)(2,1)} %fusion), calls=%async_computation | async-start | bytes 1310720 | tf_op jit(solution)/shard_map/all_to_all | solution.py:228
  97.2 7.7 %collective-permute-start.11 = (bf16[2,40,512]{2,1,0:T(8,128)(2,1)S(1)}, bf16[2,40,512]{2,1,0:T(8,128)(2,1)S(1)}, u32[]{:S(2)}, u32[]{:S(2)}) collective-permute-start(bf16[2,40,512]{2,1,0:T(8,128)(2,1)S(1)} %slice.65), channel_id=1, source_target_pairs={{0,8},{4,12},{8,0},{12,4},{16,24},{20,28},{24,16},{28,20},{1,9},{5... | collective-permute-start | bytes 245768 | tf_op jit(solution)/shard_map/ppermute | solution.py:168
  105.0 6.9 %collective-permute-start.12 = (bf16[1,40,512]{2,1,0:T(8,128)(2,1)S(1)}, bf16[1,40,512]{2,1,0:T(8,128)(2,1)S(1)}, u32[]{:S(2)}, u32[]{:S(2)}) collective-permute-start(bf16[1,40,512]{2,1,0:T(8,128)(2,1)S(1)} %slice.66), channel_id=1, source_target_pairs={{0,16},{4,20},{8,24},{12,28},{16,0},{20,4},{24,8},{28,12},{1,17},{... | collective-permute-start | bytes 122888 | tf_op jit(solution)/shard_map/ppermute | solution.py:168
  111.9 30.5 %copy-start.1 = (f32[32,512]{1,0:T(8,128)}, f32[32,512]{1,0:T(8,128)S(1)}, u32[]{:S(2)}) copy-start(f32[32,512]{1,0:T(8,128)S(1)} %slice_divide_fusion.walked_ref) | copy-start | bytes 196612
Sparse Core Ops, SparseCore 0:
  10.6 64.6 all-gather.2

commit v10 on v9

--- a/solution.py
+++ b/solution.py
@@ -237,8 +237,8 @@
         walked, walked.T, precision=lax.Precision.HIGHEST, preferred_element_type=jnp.float32
     )
     partial_gram = local_gram.reshape(1, 8, 128)
-    for group in (("x", "y"), ("k", "z")):
-        shares = lax.all_to_all(jnp.broadcast_to(partial_gram, (16, 8, 128)), group, 0, 0)
+    for group, ways in ((("x", "k"), X * K), (("z", "y"), Z * Y)):
+        shares = lax.all_to_all(jnp.broadcast_to(partial_gram, (ways, 8, 128)), group, 0, 0)
         partial_gram = jnp.sum(shares, axis=0, keepdims=True)
     gram_matrix = partial_gram.reshape(VEC, VEC) / points
     embedding_basis, gram_factor = pl.pallas_call(

time: 154 us -> 154 us (level)
  blocking collectives: 29.5 us -> 26.1 us
  starting transfers between devices: 35.2 us -> 38.4 us
  waiting for transfers between devices: 49.1 us -> 51.4 us
  Pallas kernels: 17 us -> 14.9 us
    ppermute x4, starting transfers between devices: 11.6 us -> 15.9 us  [swap(): return lax.ppermute(values, axis, [(i, i ^ bit) for i in range(size)])]
    all_to_all x2, blocking collectives: 29.5 us -> 26.1 us  [on_device(): lax.all_to_all(jnp.broadcast_to(partial_gram, (ways, 8, 128)), group, 0, 0)]
    ppermute x4, waiting for transfers between devices: 7.01 us -> 9.13 us  [swap(): return lax.ppermute(values, axis, [(i, i ^ bit) for i in range(size)])]
    pallas_call x1, Pallas kernels: 9.87 us -> 8.06 us  [on_device(): pl.pallas_call(tile_kernel, out_shape=[jax.ShapeDtypeStruct((Z // 2, AUG,...]
where the time goes in v10:
time: 154 us
  waiting for transfers between devices  51.4 us (33%)
  starting transfers between devices  38.4 us (25%)
  blocking collectives  26.1 us (17%)
  Pallas kernels  14.9 us (10%)
  between operations  14.8 us (10%)
  other arithmetic  5.28 us (3%)
  local copies, waits for them, and re-layouts  2.74 us (2%)
    all_gather x1, waiting for transfers between devices, on_device(): far_all = lax.all_gather(far_send, FAR)  26.5 us
    all_to_all x2, blocking collectives, on_device(): lax.all_to_all(jnp.broadcast_to(partial_gram, (ways, 8, 128)), group, 0, 0)  26.1 us
    ppermute x10, starting transfers between devices, shift(): lax.ppermute(values, axis, [(i, (i + by) % size) for i in range(size)])  17.5 us
    ppermute x4, starting transfers between devices, swap(): return lax.ppermute(values, axis, [(i, i ^ bit) for i in range(size)])  15.9 us
    ppermute x10, waiting for transfers between devices, shift(): lax.ppermute(values, axis, [(i, (i + by) % size) for i in range(size)])  15.8 us
    ppermute x4, waiting for transfers between devices, swap(): return lax.ppermute(values, axis, [(i, i ^ bit) for i in range(size)])  9.13 us
    pallas_call x1, Pallas kernels, on_device(): pl.pallas_call(tile_kernel, out_shape=[jax.ShapeDtypeStruct((Z // 2, AUG,...  8.06 us
    all_to_all x1, starting transfers between devices, on_device(): far_back = lax.all_to_all(far_pair, ('x', 'y'), 0, 0)  5.01 us
  transfers between devices with their start and end apart: 16, of which 7 were waited for; matrix products, arithmetic and copies ran while one was open for 3% of the time, Pallas kernels for 2%

profile of v10, /device:TPU:1, one launch (start us, length us, event | category | flops | bytes accessed | tf_op | source)
XLA Modules:
  0.0 154.0 jit_solution(147329233856273834)
XLA Ops:
  7.2 0.0 all-gather.3.cloned.1.call-start
  7.2 0.8 convert_element_type.21
  8.1 1.7 %pad_maximum_fusion.1 = bf16[288,512]{1,0:T(8,128)(2,1)} fusion(bf16[32,512]{1,0:T(8,128)(2,1)S(1)} %convert_element_type.21, bf16[256,512]{1,0:T(8,128)(2,1)} %param.4), kind=kLoop, calls=%fused_computation.5 | loop fusion | flops 589824 | bytes 589824 | tf_op jit(solution)/shard_map/concatenate | solution.py:174
  9.7 0.0 copy-start.2
  9.7 0.0 all-gather.3.cloned.1.call-update
  9.8 1.1 copy.11
  11.0 2.5 %collective-permute-start.6 = (bf16[288,512]{1,0:T(8,128)(2,1)S(1)}, bf16[288,512]{1,0:T(8,128)(2,1)S(1)}, u32[]{:S(2)}, u32[]{:S(2)}) collective-permute-start(bf16[288,512]{1,0:T(8,128)(2,1)S(1)} %pad_maximum_fusion.refs_0_), channel_id=1, source_target_pairs={{0,4},{4,8},{8,12},{12,16},{16,20},{20,24},{24,28},{28,0},{1,5},{5... | collective-permute-start | bytes 884744 | tf_op jit(solution)/shard_map/ppermute | solution.py:164
  13.5 4.0 %collective-permute-start.3 = (bf16[288,512]{1,0:T(8,128)(2,1)S(1)}, bf16[288,512]{1,0:T(8,128)(2,1)S(1)}, u32[]{:S(2)}, u32[]{:S(2)}) collective-permute-start(bf16[288,512]{1,0:T(8,128)(2,1)S(1)} %pad_maximum_fusion.refs_0_), channel_id=1, source_target_pairs={{0,28},{4,0},{8,4},{12,8},{16,12},{20,16},{24,20},{28,24},{1,29},{... | collective-permute-start | bytes 884744 | tf_op jit(solution)/shard_map/ppermute | solution.py:164
  17.5 6.6 %collective-permute-done.6.refs_7_ = bf16[288,512]{1,0:T(8,128)(2,1)S(1)} collective-permute-done((bf16[288,512]{1,0:T(8,128)(2,1)S(1)}, bf16[288,512]{1,0:T(8,128)(2,1)S(1)}, u32[]{:S(2)}, u32[]{:S(2)}) %collective-permute-start.6) | collective-permute-done | bytes 294944 | tf_op jit(solution)/shard_map/ppermute | solution.py:164
  24.2 0.0 collective-permute-start.7
  24.2 0.0 collective-permute-done.3.refs_1_
  24.2 2.7 %collective-permute-start.4 = (bf16[288,512]{1,0:T(8,128)(2,1)S(1)}, bf16[288,512]{1,0:T(8,128)(2,1)S(1)}, u32[]{:S(2)}, u32[]{:S(2)}) collective-permute-start(bf16[288,512]{1,0:T(8,128)(2,1)S(1)} %collective-permute-done.3.refs_1_), channel_id=1, source_target_pairs={{0,28},{4,0},{8,4},{12,8},{16,12},{20,16},{24,20},{28,24},{1,29},{... | collective-permute-start | bytes 884744 | tf_op jit(solution)/shard_map/ppermute | solution.py:164
  26.9 5.9 %collective-permute-done.7.refs_6_ = bf16[288,512]{1,0:T(8,128)(2,1)S(1)} collective-permute-done((bf16[288,512]{1,0:T(8,128)(2,1)S(1)}, bf16[288,512]{1,0:T(8,128)(2,1)S(1)}, u32[]{:S(2)}, u32[]{:S(2)}) %collective-permute-start.7) | collective-permute-done | bytes 294944 | tf_op jit(solution)/shard_map/ppermute | solution.py:164
  32.8 0.0 collective-permute-start.8
  33.4 0.0 copy-done.2
  33.4 0.1 copy.10
  33.5 0.1 reshape.12
  33.6 0.1 pad_add_fusion.2
  33.7 2.9 %collective-permute-start.1 = (s32[128]{0:T(128)S(1)}, s32[128]{0:T(128)S(1)}, u32[]{:S(2)}, u32[]{:S(2)}) collective-permute-start(s32[128]{0:T(128)S(1)} %pad_add_fusion.2), channel_id=1, source_target_pairs={{0,2},{1,3},{2,0},{3,1},{4,6},{5,7},{6,4},{7,5},{8,10},{9,11},{10,... | collective-permute-start | bytes 1544 | tf_op jit(solution)/shard_map/ppermute | solution.py:164
  36.6 0.3 collective-permute-start
  37.0 2.4 %collective-permute-start.2 = (s32[128]{0:T(128)S(1)}, s32[128]{0:T(128)S(1)}, u32[]{:S(2)}, u32[]{:S(2)}) collective-permute-start(s32[128]{0:T(128)S(1)} %pad_add_fusion.2), channel_id=1, source_target_pairs={{0,3},{1,0},{2,1},{3,2},{4,7},{5,4},{6,5},{7,6},{8,11},{9,8},{10,9... | collective-permute-start | bytes 1544 | tf_op jit(solution)/shard_map/ppermute | solution.py:164
  39.3 0.0 collective-permute-done.4.refs_2_
  39.3 2.7 %collective-permute-start.5 = (bf16[288,512]{1,0:T(8,128)(2,1)S(1)}, bf16[288,512]{1,0:T(8,128)(2,1)S(1)}, u32[]{:S(2)}, u32[]{:S(2)}) collective-permute-start(bf16[288,512]{1,0:T(8,128)(2,1)S(1)} %collective-permute-done.4.refs_2_), channel_id=1, source_target_pairs={{0,28},{4,0},{8,4},{12,8},{16,12},{20,16},{24,20},{28,24},{1,29},{... | collective-permute-start | bytes 884744 | tf_op jit(solution)/shard_map/ppermute | solution.py:164
  42.0 0.0 collective-permute-done.8.refs_5_
  42.0 0.0 collective-permute-start.9
  42.0 0.1 fusion.7
  42.1 0.6 pad_add_fusion.1.place_ref
  42.7 0.0 collective-permute-done.1
  42.7 0.0 collective-permute-done
  42.7 0.0 collective-permute-done.2
  42.7 0.6 pad_add_fusion.lists_ref
  43.3 2.3 %select_pairs.1.picked_ref = s32[128]{0:T(128)} custom-call(s32[3]{0:T(128)} %pad_add_fusion.1.place_ref, s32[4,128]{1,0:T(4,128)} %pad_add_fusion.lists_ref), custom_call_target="tpu_custom_call" | custom-call | tf_op jit(solution)/shard_map/select_pairs/pallas_call | solution.py:199
  45.6 0.1 collective-permute-done.5.refs_3_
  45.7 3.1 %collective-permute-done.9.refs_4_ = bf16[288,512]{1,0:T(8,128)(2,1)S(1)} collective-permute-done((bf16[288,512]{1,0:T(8,128)(2,1)S(1)}, bf16[288,512]{1,0:T(8,128)(2,1)S(1)}, u32[]{:S(2)}, u32[]{:S(2)}) %collective-permute-start.9) | collective-permute-done | bytes 294944 | tf_op jit(solution)/shard_map/ppermute | solution.py:164
  48.8 26.5 %all-gather.3.cloned.1.call-done = bf16[9216,512]{1,0:T(8,128)(2,1)} async-done(((bf16[288,512]{1,0:T(8,128)(2,1)}), bf16[9216,512]{1,0:T(8,128)(2,1)}) %all-gather.3.cloned.1.call-update) | async-done | bytes 9437200 | tf_op jit(solution)/shard_map/all_gather | solution.py:176
  75.3 0.0 copy-start
  75.3 0.7 copy-done
  75.9 8.1 %tiles.1 = (f32[4,48,512]{2,1,0:T(8,128)S(1)}, bf16[4,48,512]{2,1,0:T(8,128)(2,1)S(1)}, f32[16,48,512]{2,1,0:T(8,128)S(1)}, bf16[16,48,512]{2,1,0:T(8,128)(2,1)S(1)}) custom-call(s32[128]{0:T(128)S(1)} %copy-done, bf16[32,288,512]{2,1,0:T(8,128)(2,1)} %bitcast.17, bf16[288,512]{1,0:T(8,128)(2,1)S(1)} %pad_maximum_fusion.refs_0_, ...), custom_call_target="tpu_custom_call" | custom-call | tf_op jit(solution)/shard_map/tiles/pallas_call | solution.py:206
  84.0 2.3 %collective-permute-start.13 = (bf16[16,48,512]{2,1,0:T(8,128)(2,1)S(1)}, bf16[16,48,512]{2,1,0:T(8,128)(2,1)S(1)}, u32[]{:S(2)}, u32[]{:S(2)}) collective-permute-start(bf16[16,48,512]{2,1,0:T(8,128)(2,1)S(1)} %get-tuple-element.13), channel_id=1, source_target_pairs={{0,32},{32,0},{1,33},{33,1},{2,34},{34,2},{3,35},{35,3},{4,36},{36... | collective-permute-start | bytes 2359304 | tf_op jit(solution)/shard_map/ppermute | solution.py:168
  86.3 4.9 %collective-permute-start.10 = (bf16[4,48,512]{2,1,0:T(8,128)(2,1)S(1)}, bf16[4,48,512]{2,1,0:T(8,128)(2,1)S(1)}, u32[]{:S(2)}, u32[]{:S(2)}) collective-permute-start(bf16[4,48,512]{2,1,0:T(8,128)(2,1)S(1)} %get-tuple-element.11), channel_id=1, source_target_pairs={{0,4},{4,0},{8,12},{12,8},{16,20},{20,16},{24,28},{28,24},{1,5},{5... | collective-permute-start | bytes 589832 | tf_op jit(solution)/shard_map/ppermute | solution.py:168
  91.2 0.0 collective-permute-done.13
  91.2 1.1 fusion
  92.3 5.0 %all-to-all-start = ((bf16[16,40,512]{2,1,0:T(8,128)(2,1)}), bf16[16,40,512]{2,1,0:T(8,128)(2,1)S(1)}, u32[]{:S(2)}, u32[]{:S(2)}) async-start(bf16[16,40,512]{2,1,0:T(8,128)(2,1)} %fusion), calls=%async_computation | async-start | bytes 1310720 | tf_op jit(solution)/shard_map/all_to_all | solution.py:228
  97.3 0.0 collective-permute-done.10
  97.3 0.1 convert_add_fusion
  97.4 6.6 %collective-permute-start.11 = (bf16[2,40,512]{2,1,0:T(8,128)(2,1)S(1)}, bf16[2,40,512]{2,1,0:T(8,128)(2,1)S(1)}, u32[]{:S(2)}, u32[]{:S(2)}) collective-permute-start(bf16[2,40,512]{2,1,0:T(8,128)(2,1)S(1)} %slice.65), channel_id=1, source_target_pairs={{0,8},{4,12},{8,0},{12,4},{16,24},{20,28},{24,16},{28,20},{1,9},{5... | collective-permute-start | bytes 245768 | tf_op jit(solution)/shard_map/ppermute | solution.py:168
  104.0 4.0 %collective-permute-done.11 = bf16[2,40,512]{2,1,0:T(8,128)(2,1)S(1)} collective-permute-done((bf16[2,40,512]{2,1,0:T(8,128)(2,1)S(1)}, bf16[2,40,512]{2,1,0:T(8,128)(2,1)S(1)}, u32[]{:S(2)}, u32[]{:S(2)}) %collective-permute-start.11) | collective-permute-done | bytes 81952 | tf_op jit(solution)/shard_map/ppermute | solution.py:168
  108.0 2.1 %collective-permute-start.12 = (bf16[1,40,512]{2,1,0:T(8,128)(2,1)S(1)}, bf16[1,40,512]{2,1,0:T(8,128)(2,1)S(1)}, u32[]{:S(2)}, u32[]{:S(2)}) collective-permute-start(bf16[1,40,512]{2,1,0:T(8,128)(2,1)S(1)} %slice.66), channel_id=1, source_target_pairs={{0,16},{4,20},{8,24},{12,28},{16,0},{20,4},{24,8},{28,12},{1,17},{... | collective-permute-start | bytes 122888 | tf_op jit(solution)/shard_map/ppermute | solution.py:168
  110.1 0.0 all-to-all-done
  110.1 0.1 convert_reduce_fusion
  110.2 5.2 %collective-permute-done.12 = bf16[1,40,512]{2,1,0:T(8,128)(2,1)S(1)} collective-permute-done((bf16[1,40,512]{2,1,0:T(8,128)(2,1)S(1)}, bf16[1,40,512]{2,1,0:T(8,128)(2,1)S(1)}, u32[]{:S(2)}, u32[]{:S(2)}) %collective-permute-start.12) | collective-permute-done | bytes 40992 | tf_op jit(solution)/shard_map/ppermute | solution.py:168
  115.4 0.0 copy-start.1
  115.4 0.2 fusion.4
  115.6 0.1 broadcast_in_dim.17
  115.7 10.2 %all_to_all.15 = f32[8,8,128]{2,1,0:T(8,128)S(1)} all-to-all(f32[8,8,128]{2,1,0:T(8,128)S(1)} %broadcast_in_dim.18), channel_id=1, replica_groups=mesh['x'=4,'k'=2,'z'=8,'y'=4] {'x','k'}, dimensions={0} | all-to-all | bytes 65536 | tf_op jit(solution)/shard_map/all_to_all | solution.py:241
  126.0 15.9 %all_to_all.16 = f32[32,8,128]{2,1,0:T(8,128)S(1)} all-to-all(f32[32,8,128]{2,1,0:T(8,128)S(1)} %broadcast_in_dim.19), channel_id=1, replica_groups=mesh['x'=4,'k'=2,'z'=8,'y'=4] {'z','y'}, dimensions={0} | all-to-all | bytes 262144 | tf_op jit(solution)/shard_map/all_to_all | solution.py:241
  141.9 0.7 div.23.gram_ref
  142.6 0.0 copy-done.1
  142.6 4.6 %finish.1 = (f32[32,512]{1,0:T(8,128)}, f32[32,32]{1,0:T(8,128)}) custom-call(f32[32,32]{1,0:T(8,128)} %div.23.gram_ref, f32[32,512]{1,0:T(8,128)} %copy-done.1), custom_call_target="tpu_custom_call" | custom-call | tf_op jit(solution)/shard_map/finish/pallas_call | solution.py:244
  (15 shorter events, 0.2 us)
Async XLA Ops:
  7.2 68.1 %all-gather.3.cloned.1.call-start = ((), (), s32[]{:S(2)}) async-start(), calls=%async_computation.3 | async-start | bytes 9732096 | tf_op jit(solution)/shard_map/all_gather | solution.py:176
  9.7 23.7 %copy-start.2 = (s32[24,2]{0,1:T(2,128)S(1)}, s32[24,2]{0,1:T(2,128)}, u32[]{:S(2)}) copy-start(s32[24,2]{0,1:T(2,128)} %param.6) | copy-start | bytes 580
  11.0 13.2 %collective-permute-start.6 = (bf16[288,512]{1,0:T(8,128)(2,1)S(1)}, bf16[288,512]{1,0:T(8,128)(2,1)S(1)}, u32[]{:S(2)}, u32[]{:S(2)}) collective-permute-start(bf16[288,512]{1,0:T(8,128)(2,1)S(1)} %pad_maximum_fusion.refs_0_), channel_id=1, source_target_pairs={{0,4},{4,8},{8,12},{12,16},{16,20},{20,24},{24,28},{28,0},{1,5},{5... | collective-permute-start | bytes 884744 | tf_op jit(solution)/shard_map/ppermute | solution.py:164
  13.5 10.7 %collective-permute-start.3 = (bf16[288,512]{1,0:T(8,128)(2,1)S(1)}, bf16[288,512]{1,0:T(8,128)(2,1)S(1)}, u32[]{:S(2)}, u32[]{:S(2)}) collective-permute-start(bf16[288,512]{1,0:T(8,128)(2,1)S(1)} %pad_maximum_fusion.refs_0_), channel_id=1, source_target_pairs={{0,28},{4,0},{8,4},{12,8},{16,12},{20,16},{24,20},{28,24},{1,29},{... | collective-permute-start | bytes 884744 | tf_op jit(solution)/shard_map/ppermute | solution.py:164
  24.2 8.6 %collective-permute-start.7 = (bf16[288,512]{1,0:T(8,128)(2,1)S(1)}, bf16[288,512]{1,0:T(8,128)(2,1)S(1)}, u32[]{:S(2)}, u32[]{:S(2)}) collective-permute-start(bf16[288,512]{1,0:T(8,128)(2,1)S(1)} %collective-permute-done.6.refs_7_), channel_id=1, source_target_pairs={{0,4},{4,8},{8,12},{12,16},{16,20},{20,24},{24,28},{28,0},{1,5},{5... | collective-permute-start | bytes 884744 | tf_op jit(solution)/shard_map/ppermute | solution.py:164
  24.2 15.1 %collective-permute-start.4 = (bf16[288,512]{1,0:T(8,128)(2,1)S(1)}, bf16[288,512]{1,0:T(8,128)(2,1)S(1)}, u32[]{:S(2)}, u32[]{:S(2)}) collective-permute-start(bf16[288,512]{1,0:T(8,128)(2,1)S(1)} %collective-permute-done.3.refs_1_), channel_id=1, source_target_pairs={{0,28},{4,0},{8,4},{12,8},{16,12},{20,16},{24,20},{28,24},{1,29},{... | collective-permute-start | bytes 884744 | tf_op jit(solution)/shard_map/ppermute | solution.py:164
  32.8 9.2 %collective-permute-start.8 = (bf16[288,512]{1,0:T(8,128)(2,1)S(1)}, bf16[288,512]{1,0:T(8,128)(2,1)S(1)}, u32[]{:S(2)}, u32[]{:S(2)}) collective-permute-start(bf16[288,512]{1,0:T(8,128)(2,1)S(1)} %collective-permute-done.7.refs_6_), channel_id=1, source_target_pairs={{0,4},{4,8},{8,12},{12,16},{16,20},{20,24},{24,28},{28,0},{1,5},{5... | collective-permute-start | bytes 884744 | tf_op jit(solution)/shard_map/ppermute | solution.py:164
  33.7 8.9 %collective-permute-start.1 = (s32[128]{0:T(128)S(1)}, s32[128]{0:T(128)S(1)}, u32[]{:S(2)}, u32[]{:S(2)}) collective-permute-start(s32[128]{0:T(128)S(1)} %pad_add_fusion.2), channel_id=1, source_target_pairs={{0,2},{1,3},{2,0},{3,1},{4,6},{5,7},{6,4},{7,5},{8,10},{9,11},{10,... | collective-permute-start | bytes 1544 | tf_op jit(solution)/shard_map/ppermute | solution.py:164
  36.6 6.0 %collective-permute-start = (s32[128]{0:T(128)S(1)}, s32[128]{0:T(128)S(1)}, u32[]{:S(2)}, u32[]{:S(2)}) collective-permute-start(s32[128]{0:T(128)S(1)} %pad_add_fusion.2), channel_id=1, source_target_pairs={{0,1},{1,2},{2,3},{3,0},{4,5},{5,6},{6,7},{7,4},{8,9},{9,10},{10,1... | collective-permute-start | bytes 1544 | tf_op jit(solution)/shard_map/ppermute | solution.py:164
  37.0 5.7 %collective-permute-start.2 = (s32[128]{0:T(128)S(1)}, s32[128]{0:T(128)S(1)}, u32[]{:S(2)}, u32[]{:S(2)}) collective-permute-start(s32[128]{0:T(128)S(1)} %pad_add_fusion.2), channel_id=1, source_target_pairs={{0,3},{1,0},{2,1},{3,2},{4,7},{5,4},{6,5},{7,6},{8,11},{9,8},{10,9... | collective-permute-start | bytes 1544 | tf_op jit(solution)/shard_map/ppermute | solution.py:164
  39.3 6.3 %collective-permute-start.5 = (bf16[288,512]{1,0:T(8,128)(2,1)S(1)}, bf16[288,512]{1,0:T(8,128)(2,1)S(1)}, u32[]{:S(2)}, u32[]{:S(2)}) collective-permute-start(bf16[288,512]{1,0:T(8,128)(2,1)S(1)} %collective-permute-done.4.refs_2_), channel_id=1, source_target_pairs={{0,28},{4,0},{8,4},{12,8},{16,12},{20,16},{24,20},{28,24},{1,29},{... | collective-permute-start | bytes 884744 | tf_op jit(solution)/shard_map/ppermute | solution.py:164
  42.0 6.8 %collective-permute-start.9 = (bf16[288,512]{1,0:T(8,128)(2,1)S(1)}, bf16[288,512]{1,0:T(8,128)(2,1)S(1)}, u32[]{:S(2)}, u32[]{:S(2)}) collective-permute-start(bf16[288,512]{1,0:T(8,128)(2,1)S(1)} %collective-permute-done.8.refs_5_), channel_id=1, source_target_pairs={{0,4},{4,8},{8,12},{12,16},{16,20},{20,24},{24,28},{28,0},{1,5},{5... | collective-permute-start | bytes 884744 | tf_op jit(solution)/shard_map/ppermute | solution.py:164
  75.3 0.7 copy-start
  84.0 7.2 %collective-permute-start.13 = (bf16[16,48,512]{2,1,0:T(8,128)(2,1)S(1)}, bf16[16,48,512]{2,1,0:T(8,128)(2,1)S(1)}, u32[]{:S(2)}, u32[]{:S(2)}) collective-permute-start(bf16[16,48,512]{2,1,0:T(8,128)(2,1)S(1)} %get-tuple-element.13), channel_id=1, source_target_pairs={{0,32},{32,0},{1,33},{33,1},{2,34},{34,2},{3,35},{35,3},{4,36},{36... | collective-permute-start | bytes 2359304 | tf_op jit(solution)/shard_map/ppermute | solution.py:168
  86.3 11.0 %collective-permute-start.10 = (bf16[4,48,512]{2,1,0:T(8,128)(2,1)S(1)}, bf16[4,48,512]{2,1,0:T(8,128)(2,1)S(1)}, u32[]{:S(2)}, u32[]{:S(2)}) collective-permute-start(bf16[4,48,512]{2,1,0:T(8,128)(2,1)S(1)} %get-tuple-element.11), channel_id=1, source_target_pairs={{0,4},{4,0},{8,12},{12,8},{16,20},{20,16},{24,28},{28,24},{1,5},{5... | collective-permute-start | bytes 589832 | tf_op jit(solution)/shard_map/ppermute | solution.py:168
  92.3 17.8 %all-to-all-start = ((bf16[16,40,512]{2,1,0:T(8,128)(2,1)}), bf16[16,40,512]{2,1,0:T(8,128)(2,1)S(1)}, u32[]{:S(2)}, u32[]{:S(2)}) async-start(bf16[16,40,512]{2,1,0:T(8,128)(2,1)} %fusion), calls=%async_computation | async-start | bytes 1310720 | tf_op jit(solution)/shard_map/all_to_all | solution.py:228
  97.4 10.6 %collective-permute-start.11 = (bf16[2,40,512]{2,1,0:T(8,128)(2,1)S(1)}, bf16[2,40,512]{2,1,0:T(8,128)(2,1)S(1)}, u32[]{:S(2)}, u32[]{:S(2)}) collective-permute-start(bf16[2,40,512]{2,1,0:T(8,128)(2,1)S(1)} %slice.65), channel_id=1, source_target_pairs={{0,8},{4,12},{8,0},{12,4},{16,24},{20,28},{24,16},{28,20},{1,9},{5... | collective-permute-start | bytes 245768 | tf_op jit(solution)/shard_map/ppermute | solution.py:168
  108.0 7.3 %collective-permute-start.12 = (bf16[1,40,512]{2,1,0:T(8,128)(2,1)S(1)}, bf16[1,40,512]{2,1,0:T(8,128)(2,1)S(1)}, u32[]{:S(2)}, u32[]{:S(2)}) collective-permute-start(bf16[1,40,512]{2,1,0:T(8,128)(2,1)S(1)} %slice.66), channel_id=1, source_target_pairs={{0,16},{4,20},{8,24},{12,28},{16,0},{20,4},{24,8},{28,12},{1,17},{... | collective-permute-start | bytes 122888 | tf_op jit(solution)/shard_map/ppermute | solution.py:168
  115.4 27.2 %copy-start.1 = (f32[32,512]{1,0:T(8,128)}, f32[32,512]{1,0:T(8,128)S(1)}, u32[]{:S(2)}) copy-start(f32[32,512]{1,0:T(8,128)S(1)} %slice_divide_fusion.walked_ref) | copy-start | bytes 196612
Sparse Core Ops, SparseCore 0:
  10.6 64.6 all-gather.2
